TPU v7x, 128 devices: a whole 4x4x4 slice. The times are simulated.
128 devices in a mesh: hist: 8 (over x, z_lo), tok: 16 (over z_hi, y, core).
Axes of the slice: x: 4, y: 4, z: 4 (z_hi: 2, z_lo: 2; z = z_hi * 2 + z_lo), core: 2. Of those that a mesh axis runs over, the one named last changes fastest.
Arguments:
- history: bfloat16 [24, 16384, 2048], P('hist', 'tok'), may hold values from -6 to 6
- layer_ids: int32 [24], replicated, may hold values from 0 to 23, each once
- mix_weights: float32 [4, 24, 16384], P(None, None, 'tok'), may hold values from -1.5 to 1.5
- doc_ids: int32 [16384], P('tok'), may hold values from 0 to 63, never falling along the last dimension, each value on 1 to 512 neighbouring positions
- gains: float32 [5, 2048], replicated, may hold values from 0.5 to 1.5
- w_qkv: bfloat16 [2048, 3, 2048], P('tok', None, 'hist'), may hold values from -0.125 to 0.125
- w_out: bfloat16 [2048, 2048], P('tok', 'hist'), may hold values from -1 to 1
- w_up: bfloat16 [2048, 8192], P('tok', 'hist'), may hold values from -0.125 to 0.125
- w_down: bfloat16 [2048, 8192], P('tok', 'hist'), may hold values from -0.1875 to 0.1875
- da_in: bfloat16 [2048, 100], replicated, may hold values from -0.125 to 0.125
- da_out: bfloat16 [100, 100], replicated, may hold values from -0.625 to 0.625
- da_bias: float32 [100], replicated, may hold values from -3 to 3
- out_grad: bfloat16 [16384, 2048], P(('tok', 'hist')), may hold values from -6 to 6
- mix_grad_in: float32 [16384, 100], P(('tok', 'hist')), may hold values from -6 to 6
Outputs:
- block_out: bfloat16 [16384, 2048], P(('tok', 'hist'))
- mix_next: float32 [16384, 100], P(('tok', 'hist'))
- history_grad: bfloat16 [24, 16384, 2048], P('hist', 'tok')
- mix_grad: float32 [4, 24, 16384], P(None, 'hist', 'tok')
- gains_grad: float32 [5, 2048], replicated
- w_qkv_grad: float32 [2048, 3, 2048], P('tok', None, 'hist')
- w_out_grad: float32 [2048, 2048], P('tok', 'hist')
- w_up_grad: float32 [2048, 8192], P('tok', 'hist')
- w_down_grad: float32 [2048, 8192], P('tok', 'hist')
- da_in_grad: float32 [2048, 100], replicated
- da_out_grad: float32 [100, 100], replicated
- da_bias_grad: float32 [100], replicated
Inputs may be any that keep to these rules, and one draw needn't show every extreme that they name: A permutation: slot j of history holds history entry layer_ids[j]. `doc_ids`: never decrease along the tokens; no document has more than 512 tokens; a sequence may begin or end inside a document.
All inputs are finite; a program needn't handle non-finite values.
Results may differ from a plain program's by a relative error of at most 0.04.
Values may be sent and summed in bfloat16 or wider, within the bound.
A program may use at most 192 MiB of HBM per device.

v0:
```python
import jax
import jax.numpy as jnp
from jax import lax
from jax.sharding import PartitionSpec as P

HD = 128
ROT = 32


EPSILON = 1e-05
NEGATIVE = -1e30
HIGHEST = lax.Precision.HIGHEST


def norm_rows(values):
    row_mean = jnp.mean(values, axis=-1, keepdims=True)
    centered = values - row_mean
    inv_std = lax.rsqrt(jnp.mean(centered * centered, axis=-1, keepdims=True) + EPSILON)
    return (centered * inv_std, inv_std)


def norm_back(grad_unit, norm_unit, inv_std):
    return inv_std * (
        grad_unit
        - jnp.mean(grad_unit, axis=-1, keepdims=True)
        - norm_unit * jnp.mean(grad_unit * norm_unit, axis=-1, keepdims=True)
    )


def gelu_slope(values):
    return (
        0.5 * (1.0 + lax.erf(values * 0.7071067811865476))
        + values * jnp.exp(-0.5 * values * values) * 0.3989422804014327
    )


def rotary_tables(length, rotated):
    half_rot = rotated // 2
    frequency = 10000.0 ** (-2.0 * jnp.arange(half_rot, dtype=jnp.float32) / rotated)
    angles = jnp.arange(length, dtype=jnp.float32)[:, None] * frequency[None, :]
    return (jnp.cos(angles), jnp.sin(angles))


def rotate(values, cosine, sine_table, direction):
    half_rot = cosine.shape[1]
    first_half = values[..., :half_rot]
    second_half = values[..., half_rot : 2 * half_rot]
    cos_part = cosine[:, None, :]
    sin_part = direction * sine_table[:, None, :]
    return jnp.concatenate(
        [
            first_half * cos_part - second_half * sin_part,
            second_half * cos_part + first_half * sin_part,
            values[..., 2 * half_rot :],
        ],
        axis=-1,
    )


def contract(left_side, right_side, left_dim, right_dim):
    return lax.dot_general(
        left_side,
        right_side,
        (((left_dim,), (right_dim,)), ((), ())),
        preferred_element_type=jnp.float32,
    )


def masked_scores(query_rows, keys, doc_ids, begin_row):
    row_count = query_rows.shape[0]
    query_pos = begin_row + jnp.arange(row_count, dtype=jnp.int32)
    key_pos = jnp.arange(doc_ids.shape[0], dtype=jnp.int32)
    query_docs = lax.dynamic_slice_in_dim(doc_ids, begin_row, row_count, 0)
    allowed = (key_pos[None, :] <= query_pos[:, None]) & (doc_ids[None, :] == query_docs[:, None])
    scores = jnp.einsum(
        "qhd,khd->hqk", query_rows, keys, preferred_element_type=jnp.float32
    ) * keys.shape[2] ** (-0.5)
    return jnp.where(allowed[None], scores, NEGATIVE)


def attend(queries, keys, values, doc_ids):
    length = queries.shape[0]
    row_block = min(512, length)

    def one_block(block_idx):
        begin_row = block_idx * row_block
        query_rows = lax.dynamic_slice_in_dim(queries, begin_row, row_block, 0)
        scores = masked_scores(query_rows, keys, doc_ids, begin_row)
        row_max = jnp.max(scores, axis=-1, keepdims=True)
        shifted = jnp.exp(scores - row_max)
        row_total = jnp.sum(shifted, axis=-1, keepdims=True)
        attn_probs = (shifted / row_total).astype(jnp.bfloat16)
        result = jnp.einsum("hqk,khd->qhd", attn_probs, values, preferred_element_type=jnp.float32)
        return (result, (row_max + jnp.log(row_total))[..., 0])

    results, log_totals = lax.map(one_block, jnp.arange(length // row_block, dtype=jnp.int32))
    return (results.reshape(queries.shape), log_totals)


def attend_back(queries, keys, values, doc_ids, log_totals, out_cot):
    length = queries.shape[0]
    row_block = min(512, length)
    scale = queries.shape[2] ** (-0.5)

    def one_block(carry, inputs):
        key_grad, value_grad = carry
        block_idx, block_lse = inputs
        begin_row = block_idx * row_block
        query_rows = lax.dynamic_slice_in_dim(queries, begin_row, row_block, 0)
        cot_rows = lax.dynamic_slice_in_dim(out_cot, begin_row, row_block, 0)
        scores = masked_scores(query_rows, keys, doc_ids, begin_row)
        attn_probs = jnp.exp(scores - block_lse[..., None])
        prob_grad = jnp.einsum("qhd,khd->hqk", cot_rows, values, preferred_element_type=jnp.float32)
        row_dot = jnp.sum(attn_probs * prob_grad, axis=-1, keepdims=True)
        score_cot = (attn_probs * (prob_grad - row_dot)).astype(jnp.bfloat16)
        query_grad = (
            jnp.einsum("hqk,khd->qhd", score_cot, keys, preferred_element_type=jnp.float32) * scale
        )
        key_grad = (
            key_grad
            + jnp.einsum("hqk,qhd->khd", score_cot, query_rows, preferred_element_type=jnp.float32)
            * scale
        )
        value_grad = value_grad + jnp.einsum(
            "hqk,qhd->khd",
            attn_probs.astype(jnp.bfloat16),
            cot_rows,
            preferred_element_type=jnp.float32,
        )
        return ((key_grad, value_grad), query_grad)

    zero_grad = jnp.zeros(queries.shape, jnp.float32)
    (key_grad, value_grad), query_grads = lax.scan(
        one_block,
        (zero_grad, zero_grad),
        (jnp.arange(length // row_block, dtype=jnp.int32), log_totals),
    )
    return (query_grads.reshape(queries.shape), key_grad, value_grad)


def body(
    history,
    layer_ids,
    mix_weights,
    doc_ids,
    gains,
    w_qkv,
    w_out,
    w_up,
    w_down,
    da_in,
    da_out,
    da_bias,
    out_grad,
    mix_grad_in,
):
    place = lax.axis_index("hist")
    slots = history.shape[0]
    seq_len = history.shape[1]
    width = history.shape[2]
    stream_count = mix_weights.shape[0]
    layers = mix_weights.shape[1]
    full_qkv, full_out, full_up, full_down = (
        lax.all_gather(w_qkv, "tok", axis=0, tiled=True),
        lax.all_gather(w_out, "tok", axis=0, tiled=True),
        lax.all_gather(w_up, "tok", axis=0, tiled=True),
        lax.all_gather(w_down, "tok", axis=0, tiled=True),
    )
    layer_range = jnp.arange(layers, dtype=jnp.int32)
    local_ids = lax.dynamic_slice_in_dim(layer_ids, place * slots, slots, 0)
    local_pick = (local_ids[:, None] == layer_range[None, :]).astype(jnp.float32)
    slot_weights = jnp.einsum("jl,slt->sjt", local_pick, mix_weights, precision=HIGHEST)
    partial_sum = jnp.zeros((stream_count, seq_len, width), jnp.float32)
    for slot_idx in range(slots):
        partial_sum = partial_sum + slot_weights[:, slot_idx, :, None] * history[slot_idx][
            None
        ].astype(jnp.float32)
    owned = lax.psum_scatter(
        partial_sum.astype(jnp.bfloat16), "hist", scatter_dimension=1, tiled=True
    ).astype(jnp.float32)
    norm_unit, inv_std = norm_rows(owned[:3])
    normed = (norm_unit * gains[:3, None, :]).astype(jnp.bfloat16)
    gathered = lax.all_gather(normed, "hist", axis=1, tiled=True)
    heads_here = full_qkv.shape[2] // HD
    cosine, sine_table = rotary_tables(seq_len, ROT)

    def project(which):
        return jnp.dot(
            gathered[which], full_qkv[:, which, :], preferred_element_type=jnp.float32
        ).reshape(seq_len, heads_here, HD)

    queries = rotate(project(0), cosine, sine_table, 1.0).astype(jnp.bfloat16)
    keys = rotate(project(1), cosine, sine_table, 1.0).astype(jnp.bfloat16)
    values = project(2).astype(jnp.bfloat16)
    attended, log_totals = attend(queries, keys, values, doc_ids)
    heads_flat = attended.reshape(seq_len, -1).astype(jnp.bfloat16)
    attn_owned = lax.psum_scatter(
        contract(heads_flat, full_out, 1, 1).astype(jnp.bfloat16),
        "hist",
        scatter_dimension=0,
        tiled=True,
    ).astype(jnp.float32)
    residual = owned[3] + attn_owned
    mid_unit, mid_std = norm_rows(residual)
    mid_norm = (mid_unit * gains[3]).astype(jnp.bfloat16)
    mid_all = lax.all_gather(mid_norm, "hist", axis=0, tiled=True)
    up_proj = jnp.dot(mid_all, full_up, preferred_element_type=jnp.float32)
    activated = jax.nn.gelu(up_proj, approximate=False).astype(jnp.bfloat16)
    mlp_owned = lax.psum_scatter(
        contract(activated, full_down, 1, 1).astype(jnp.bfloat16),
        "hist",
        scatter_dimension=0,
        tiled=True,
    ).astype(jnp.float32)
    layer_out = residual + mlp_owned
    rms_inv = lax.rsqrt(jnp.mean(layer_out * layer_out, axis=-1, keepdims=True) + EPSILON)
    rms_unit = layer_out * rms_inv
    da_norm = (rms_unit * gains[4]).astype(jnp.bfloat16)
    inner_pre = jnp.dot(da_norm, da_in, preferred_element_type=jnp.float32)
    inner_act = jax.nn.gelu(inner_pre, approximate=False).astype(jnp.bfloat16)
    mix_next = jnp.dot(inner_act, da_out, preferred_element_type=jnp.float32) + da_bias
    bias_grad = jnp.sum(mix_grad_in, axis=0)
    mix_cot = mix_grad_in.astype(jnp.bfloat16)
    da_out_grad = contract(inner_act, mix_cot, 0, 0)
    inner_cot = (contract(mix_cot, da_out, 1, 1) * gelu_slope(inner_pre)).astype(jnp.bfloat16)
    da_in_grad = contract(da_norm, inner_cot, 0, 0)
    rms_grad = contract(inner_cot, da_in, 1, 1)
    rms_gain_grad = jnp.sum(rms_grad * rms_unit, axis=0)
    rms_scaled = rms_grad * gains[4]
    out_total = out_grad.astype(jnp.float32) + rms_inv * (
        rms_scaled - rms_unit * jnp.mean(rms_scaled * rms_unit, axis=-1, keepdims=True)
    )
    mlp_cot = lax.all_gather(out_total.astype(jnp.bfloat16), "hist", axis=0, tiled=True)
    down_grad = contract(mlp_cot, activated, 0, 0)
    up_cot = (
        jnp.dot(mlp_cot, full_down, preferred_element_type=jnp.float32) * gelu_slope(up_proj)
    ).astype(jnp.bfloat16)
    up_grad = contract(mid_all, up_cot, 0, 0)
    mid_back = lax.psum_scatter(
        contract(up_cot, full_up, 1, 1).astype(jnp.bfloat16),
        "hist",
        scatter_dimension=0,
        tiled=True,
    ).astype(jnp.float32)
    mid_gain_grad = jnp.sum(mid_back * mid_unit, axis=0)
    residual_grad = out_total + norm_back(mid_back * gains[3], mid_unit, mid_std)
    attn_cot = lax.all_gather(residual_grad.astype(jnp.bfloat16), "hist", axis=0, tiled=True)
    out_proj_grad = contract(attn_cot, heads_flat, 0, 0)
    heads_cot = (
        jnp.dot(attn_cot, full_out, preferred_element_type=jnp.float32)
        .astype(jnp.bfloat16)
        .reshape(seq_len, heads_here, HD)
    )
    query_grad, key_grad, value_grad = attend_back(
        queries, keys, values, doc_ids, log_totals, heads_cot
    )
    proj_cots = (
        rotate(query_grad, cosine, sine_table, -1.0).reshape(seq_len, -1).astype(jnp.bfloat16),
        rotate(key_grad, cosine, sine_table, -1.0).reshape(seq_len, -1).astype(jnp.bfloat16),
        value_grad.reshape(seq_len, -1).astype(jnp.bfloat16),
    )
    qkv_grad = jnp.stack(
        [contract(gathered[which], proj_cots[which], 0, 0) for which in range(3)], axis=1
    )
    back_parts = jnp.stack(
        [contract(proj_cots[which], full_qkv[:, which, :], 1, 1) for which in range(3)], axis=0
    )
    in_back = lax.psum_scatter(
        back_parts.astype(jnp.bfloat16), "hist", scatter_dimension=1, tiled=True
    ).astype(jnp.float32)
    in_gain_grad = jnp.sum(in_back * norm_unit, axis=1)
    stream_part = norm_back(in_back * gains[:3, None, :], norm_unit, inv_std)
    stream_cot = jnp.concatenate([stream_part, residual_grad[None]], axis=0).astype(jnp.bfloat16)
    stream_all = lax.all_gather(stream_cot, "hist", axis=1, tiled=True)
    stream_wide = stream_all.astype(jnp.float32)
    slot_grads = []
    for slot_idx in range(slots):
        slot_grads.append(jnp.sum(slot_weights[:, slot_idx, :, None] * stream_wide, axis=0))
    history_grad = jnp.stack(slot_grads, axis=0).astype(jnp.bfloat16)
    mix_grad = jnp.einsum("jtd,std->sjt", history, stream_all, preferred_element_type=jnp.float32)
    qkv_sum, out_sum, up_sum, down_sum = (
        lax.psum_scatter(
            qkv_grad.astype(jnp.bfloat16), "tok", scatter_dimension=0, tiled=True
        ).astype(jnp.float32),
        lax.psum_scatter(
            out_proj_grad.astype(jnp.bfloat16), "tok", scatter_dimension=0, tiled=True
        ).astype(jnp.float32),
        lax.psum_scatter(
            up_grad.astype(jnp.bfloat16), "tok", scatter_dimension=0, tiled=True
        ).astype(jnp.float32),
        lax.psum_scatter(
            down_grad.astype(jnp.bfloat16), "tok", scatter_dimension=0, tiled=True
        ).astype(jnp.float32),
    )
    gains_local = jnp.concatenate([in_gain_grad, mid_gain_grad[None], rms_gain_grad[None]], axis=0)
    gains_sum, da_in_sum, da_out_sum, bias_sum = lax.psum(
        (gains_local, da_in_grad, da_out_grad, bias_grad), ("hist", "tok")
    )
    return (
        layer_out.astype(jnp.bfloat16),
        mix_next,
        history_grad,
        mix_grad,
        gains_sum,
        qkv_sum,
        out_sum,
        up_sum,
        down_sum,
        da_in_sum,
        da_out_sum,
        bias_sum,
    )


def solution(mesh):
    return jax.shard_map(
        body,
        mesh=mesh,
        in_specs=(
            P("hist", "tok", None),
            P(),
            P(None, None, "tok"),
            P("tok"),
            P(),
            P("tok", None, "hist"),
            P("tok", "hist"),
            P("tok", "hist"),
            P("tok", "hist"),
            P(),
            P(),
            P(),
            P(("tok", "hist"), None),
            P(("tok", "hist"), None),
        ),
        out_specs=(
            P(("tok", "hist"), None),
            P(("tok", "hist"), None),
            P("hist", "tok", None),
            P(None, "hist", "tok"),
            P(),
            P("tok", None, "hist"),
            P("tok", "hist"),
            P("tok", "hist"),
            P("tok", "hist"),
            P(),
            P(),
            P(),
        ),
        check_vma=False,
    )
```

profile of v0, /device:TPU:1, one launch (start us, length us, event | category | flops | bytes accessed | tf_op | source)
XLA Modules:
  0.0 2388.6 jit_solution(17264164614803084950)
XLA Ops:
  18.9 13.5 add_convert_fusion
  33.3 339.6 %reduce-scatter.10.cloned.1.call-done = bf16[4,128,2048]{2,1,0:T(8,128)(2,1)} async-done(((bf16[4,1024,2048]{2,1,0:T(8,128)(2,1)}), bf16[4,128,2048]{2,1,0:T(8,128)(2,1)}) %reduce-scatter.10.cloned.1.call-update) | async-done | bytes 2097168 | tf_op jit(solution)/shard_map/reduce_scatter | solution.py:178
  388.1 238.7 %all-gather.10.cloned.1.call-done = bf16[3,1024,2048]{2,1,0:T(8,128)(2,1)} async-done(((bf16[3,128,2048]{2,1,0:T(8,128)(2,1)}), bf16[3,1024,2048]{2,1,0:T(8,128)(2,1)}) %all-gather.10.cloned.1.call-update) | async-done | bytes 12582928 | tf_op jit(solution)/shard_map/all_gather | solution.py:183
  639.3 13.9 while.27
  655.6 20.2 all-gather.14.cloned.1.call-done
  681.2 87.6 %reduce-scatter.12.cloned.1.call-done = bf16[128,2048]{1,0:T(8,128)(2,1)} async-done(((bf16[1024,2048]{1,0:T(8,128)(2,1)}), bf16[128,2048]{1,0:T(8,128)(2,1)}) %reduce-scatter.12.cloned.1.call-update) | async-done | bytes 524304 | tf_op jit(solution)/shard_map/reduce_scatter | solution.py:197
  772.8 56.1 %all-gather.18.cloned.1.call-done = bf16[2048,1024]{1,0:T(8,128)(2,1)} async-done(((bf16[128,1024]{1,0:T(8,128)(2,1)}), bf16[2048,1024]{1,0:T(8,128)(2,1)}) %all-gather.18.cloned.1.call-update) | async-done | bytes 4194320 | tf_op jit(solution)/shard_map/all_gather | solution.py:166
  828.9 90.1 %all-gather.16.cloned.1.call-done = bf16[1024,2048]{1,0:T(8,128)(2,1)} async-done(((bf16[128,2048]{1,0:T(8,128)(2,1)}), bf16[1024,2048]{1,0:T(8,128)(2,1)}) %all-gather.16.cloned.1.call-update) | async-done | bytes 4194320 | tf_op jit(solution)/shard_map/all_gather | solution.py:206
  918.9 17.5 fusion.48
  936.4 42.5 %all-gather.20.cloned.1.call-done = bf16[2048,1024]{1,0:T(8,128)(2,1)} async-done(((bf16[128,1024]{1,0:T(8,128)(2,1)}), bf16[2048,1024]{1,0:T(8,128)(2,1)}) %all-gather.20.cloned.1.call-update) | async-done | bytes 4194320 | tf_op jit(solution)/shard_map/all_gather | solution.py:167
  988.3 88.6 %reduce-scatter.14.cloned.1.call-done = bf16[128,2048]{1,0:T(8,128)(2,1)} async-done(((bf16[1024,2048]{1,0:T(8,128)(2,1)}), bf16[128,2048]{1,0:T(8,128)(2,1)}) %reduce-scatter.14.cloned.1.call-update) | async-done | bytes 524304 | tf_op jit(solution)/shard_map/reduce_scatter | solution.py:209
  1081.6 90.8 %all-gather.22.cloned.1.call-done = bf16[1024,2048]{1,0:T(8,128)(2,1)} async-done(((bf16[128,2048]{1,0:T(8,128)(2,1)}), bf16[1024,2048]{1,0:T(8,128)(2,1)}) %all-gather.22.cloned.1.call-update) | async-done | bytes 4194320 | tf_op jit(solution)/shard_map/all_gather | solution.py:233
  1189.2 93.0 %reduce-scatter.16.cloned.1.call-done = bf16[128,2048]{1,0:T(8,128)(2,1)} async-done(((bf16[1024,2048]{1,0:T(8,128)(2,1)}), bf16[128,2048]{1,0:T(8,128)(2,1)}) %reduce-scatter.16.cloned.1.call-update) | async-done | bytes 524304 | tf_op jit(solution)/shard_map/reduce_scatter | solution.py:239
  1287.5 90.8 %all-gather.24.cloned.1.call-done = bf16[1024,2048]{1,0:T(8,128)(2,1)} async-done(((bf16[128,2048]{1,0:T(8,128)(2,1)}), bf16[1024,2048]{1,0:T(8,128)(2,1)}) %all-gather.24.cloned.1.call-update) | async-done | bytes 4194320 | tf_op jit(solution)/shard_map/all_gather | solution.py:247
  1382.1 57.9 %while.28 = (s32[]{:T(128)}, f32[1024,2,128]{0,2,1:T(8,128)}, f32[1024,2,128]{0,2,1:T(8,128)}, f32[2,512,2,128]{1,0,3,2:T(2,128)}, s32[2]{0:T(128)S(1)}, /*index...) while((s32[]{:T(128)}, f32[1024,2,128]{0,2,1:T(8,128)}, ...), condition=%wide.region_18.19_spmd.clone, body=%wide.region_16.18_spmd.clone.sunk | while | flops 1360920064 | bytes 89172440 | solution.py:133
  1394.3 10.4 dynamic_update_slice.19
  1493.0 212.1 %reduce-scatter.18.cloned.1.call-done = bf16[3,128,2048]{2,1,0:T(8,128)(2,1)} async-done(((bf16[3,1024,2048]{2,1,0:T(8,128)(2,1)}), bf16[3,128,2048]{2,1,0:T(8,128)(2,1)}) %reduce-scatter.18.cloned.1.call-update) | async-done | bytes 1572880 | tf_op jit(solution)/shard_map/reduce_scatter | solution.py:268
  1716.7 165.4 %reduce-scatter.26.cloned.1.call-done = bf16[128,1024]{1,0:T(8,128)(2,1)} async-done(((bf16[2048,1024]{1,0:T(8,128)(2,1)}), bf16[128,1024]{1,0:T(8,128)(2,1)}) %reduce-scatter.26.cloned.1.call-update) | async-done | bytes 262160 | tf_op jit(solution)/shard_map/reduce_scatter | solution.py:291
  1883.9 186.2 %reduce-scatter.24.cloned.1.call-done = bf16[128,1024]{1,0:T(8,128)(2,1)} async-done(((bf16[2048,1024]{1,0:T(8,128)(2,1)}), bf16[128,1024]{1,0:T(8,128)(2,1)}) %reduce-scatter.24.cloned.1.call-update) | async-done | bytes 262160 | tf_op jit(solution)/shard_map/reduce_scatter | solution.py:288
  2071.9 66.8 %reduce-scatter.22.cloned.1.call-done = bf16[128,256]{1,0:T(8,128)(2,1)} async-done(((bf16[2048,256]{1,0:T(8,128)(2,1)}), bf16[128,256]{1,0:T(8,128)(2,1)}) %reduce-scatter.22.cloned.1.call-update) | async-done | bytes 65552 | tf_op jit(solution)/shard_map/reduce_scatter | solution.py:285
  2140.3 77.5 %reduce-scatter.20.cloned.1.call-done = bf16[128,3,256]{2,0,1:T(8,128)(2,1)} async-done(((bf16[2048,3,256]{2,0,1:T(8,128)(2,1)}), bf16[128,3,256]{2,0,1:T(8,128)(2,1)}) %reduce-scatter.20.cloned.1.call-update) | async-done | bytes 196624 | tf_op jit(solution)/shard_map/reduce_scatter | solution.py:282
  2220.2 17.2 fusion.40
  2237.5 74.9 %fusion.107 = f32[4,3,1024]{0,1,2:T(4,128)} fusion(bf16[3,1024,2048]{2,1,0:T(8,128)(2,1)} %param.18, bf16[4,1024,2048]{2,1,0:T(8,128)(2,1)} %all-gather.26.cloned.1.call-done), kind=kOutput, calls=%fused_computation.143 | convolution fusion | flops 50331648 | bytes 29409280 | tf_op jit(solution)/shard_map/jtd,std->sjt/dot_general | solution.py:280
  2320.1 54.7 %all-reduce.6.cloned.1.call-done = (f32[5,2048]{1,0:T(8,128)}, f32[100,100]{1,0:T(8,128)}, f32[100]{0:T(128)}) async-done(((f32[5,2048]{1,0:T(8,128)}, f32[100,100]{1,0:T(8,128)}, f32[100]{0:T(128)}), (f32[5,2048]{1,0:T(8,128)}, f32[100,100]{1,0:T(8,128)}, f32[100]{0:T(128)})) %all-reduce.6.cloned.1.call-update) | async-done | bytes 81376 | tf_op jit(solution)/shard_map/psum | solution.py:296
  (291 shorter events, 234.6 us)
Async XLA Ops:
  8.0 1070.2 %copy-start = (bf16[2048,100]{0,1:T(8,128)(2,1)S(1)}, bf16[2048,100]{0,1:T(8,128)(2,1)}, u32[]{:S(2)}) copy-start(bf16[2048,100]{0,1:T(8,128)(2,1)} %param.27) | copy-start | bytes 1228804
  8.0 364.9 %reduce-scatter.10.cloned.1.call-start = ((), (), s32[]{:S(2)}) async-start(), calls=%async_computation.9 | async-start | bytes 18874368 | tf_op jit(solution)/shard_map/reduce_scatter | solution.py:178
  32.4 348.2 %all-gather.12.cloned.1.call-start = ((), (), s32[]{:S(2)}) async-start(), calls=%async_computation.11 | async-start | bytes 3342336 | tf_op jit(solution)/shard_map/all_gather | solution.py:164
  33.0 593.8 %all-gather.10.cloned.1.call-start = ((), (), s32[]{:S(2)}) async-start(), calls=%async_computation.10 | async-start | bytes 14155776 | tf_op jit(solution)/shard_map/all_gather | solution.py:183
  378.8 297.0 %all-gather.14.cloned.1.call-start = ((), (), s32[]{:S(2)}) async-start(), calls=%async_computation.12 | async-start | bytes 1114112 | tf_op jit(solution)/shard_map/all_gather | solution.py:165
  379.4 389.4 %reduce-scatter.12.cloned.1.call-start = ((), (), s32[]{:S(2)}) async-start(), calls=%async_computation.13 | async-start | bytes 4718592 | tf_op jit(solution)/shard_map/reduce_scatter | solution.py:197
  680.4 148.5 %all-gather.18.cloned.1.call-start = ((), (), s32[]{:S(2)}) async-start(), calls=%async_computation.15 | async-start | bytes 4456448 | tf_op jit(solution)/shard_map/all_gather | solution.py:166
  681.1 237.8 %all-gather.16.cloned.1.call-start = ((), (), s32[]{:S(2)}) async-start(), calls=%async_computation.14 | async-start | bytes 4718592 | tf_op jit(solution)/shard_map/all_gather | solution.py:206
  771.7 207.2 %all-gather.20.cloned.1.call-start = ((), (), s32[]{:S(2)}) async-start(), calls=%async_computation.16 | async-start | bytes 4456448 | tf_op jit(solution)/shard_map/all_gather | solution.py:167
  772.3 304.7 %reduce-scatter.14.cloned.1.call-start = ((), (), s32[]{:S(2)}) async-start(), calls=%async_computation.17 | async-start | bytes 4718592 | tf_op jit(solution)/shard_map/reduce_scatter | solution.py:209
  988.3 184.1 %all-gather.22.cloned.1.call-start = ((), (), s32[]{:S(2)}) async-start(), calls=%async_computation.18 | async-start | bytes 4718592 | tf_op jit(solution)/shard_map/all_gather | solution.py:233
  1081.6 200.6 %reduce-scatter.16.cloned.1.call-start = ((), (), s32[]{:S(2)}) async-start(), calls=%async_computation.19 | async-start | bytes 4718592 | tf_op jit(solution)/shard_map/reduce_scatter | solution.py:239
  1189.2 189.2 %all-gather.24.cloned.1.call-start = ((), (), s32[]{:S(2)}) async-start(), calls=%async_computation.20 | async-start | bytes 4718592 | tf_op jit(solution)/shard_map/all_gather | solution.py:247
  1287.5 417.6 %reduce-scatter.18.cloned.1.call-start = ((), (), s32[]{:S(2)}) async-start(), calls=%async_computation.21 | async-start | bytes 14155776 | tf_op jit(solution)/shard_map/reduce_scatter | solution.py:268
  1454.4 427.7 %reduce-scatter.26.cloned.1.call-start = ((), (), s32[]{:S(2)}) async-start(), calls=%async_computation.26 | async-start | bytes 4456448 | tf_op jit(solution)/shard_map/reduce_scatter | solution.py:291
  1463.9 606.2 %reduce-scatter.24.cloned.1.call-start = ((), (), s32[]{:S(2)}) async-start(), calls=%async_computation.25 | async-start | bytes 4456448 | tf_op jit(solution)/shard_map/reduce_scatter | solution.py:288
  1474.3 664.5 %reduce-scatter.22.cloned.1.call-start = ((), (), s32[]{:S(2)}) async-start(), calls=%async_computation.24 | async-start | bytes 1114112 | tf_op jit(solution)/shard_map/reduce_scatter | solution.py:285
  1479.8 737.9 %reduce-scatter.20.cloned.1.call-start = ((), (), s32[]{:S(2)}) async-start(), calls=%async_computation.23 | async-start | bytes 3342336 | tf_op jit(solution)/shard_map/reduce_scatter | solution.py:282
  1492.9 727.3 %all-gather.26.cloned.1.call-start = ((), (), s32[]{:S(2)}) async-start(), calls=%async_computation.22 | async-start | bytes 18874368 | tf_op jit(solution)/shard_map/all_gather | solution.py:274
  1713.0 507.2 %copy-start.33 = (f32[4,1,1024]{2,0,1:T(4,128)S(1)}, f32[4,1,1024]{2,0,1:T(4,128)}, u32[]{:S(2)}) copy-start(f32[4,1,1024]{2,0,1:T(4,128)} %copy-done.32) | copy-start | bytes 49156
  1713.0 507.2 %copy-start.35 = (f32[4,1024]{1,0:T(4,128)S(1)}, f32[4,1024]{1,0:T(4,128)}, u32[]{:S(2)}) copy-start(f32[4,1024]{1,0:T(4,128)} %copy-done.34) | copy-start | bytes 49156
  1713.0 507.2 %copy-start.37 = (f32[4,1024]{1,0:T(4,128)S(1)}, f32[4,1024]{1,0:T(4,128)}, u32[]{:S(2)}) copy-start(f32[4,1024]{1,0:T(4,128)} %copy-done.36) | copy-start | bytes 49156
  1713.1 607.1 %all-reduce.4.cloned.1.call-start = ((), (), s32[]{:S(2)}) async-start(), calls=%async_computation.27 | async-start | bytes 1703936 | tf_op jit(solution)/shard_map/psum | solution.py:296
  1715.8 659.0 %all-reduce.6.cloned.1.call-start = ((), (), s32[]{:S(2)}) async-start(), calls=%async_computation.28 | async-start | bytes 238592 | tf_op jit(solution)/shard_map/psum | solution.py:296
  (51 other events, 1941.3 us)
Sparse Core Ops, SparseCore 0:
  32.6 340.2 reduce-scatter.9
  988.4 88.5 reduce-scatter.13
  1081.7 90.6 all-gather.21
  1189.3 92.8 reduce-scatter.15
  1287.6 90.6 all-gather.23
  1713.2 354.8 all-gather.25
  2073.4 154.5 all-reduce.3
  2235.3 139.4 all-reduce.5
Sparse Core Ops, SparseCore 1:
  35.4 106.2 all-gather.11
  378.9 247.8 all-gather.9
  629.1 46.7 all-gather.13
  680.4 88.3 reduce-scatter.11
  771.3 57.5 all-gather.17
  831.1 87.8 all-gather.15
  921.2 57.6 all-gather.19
  1454.5 250.5 reduce-scatter.17
  1709.0 173.0 reduce-scatter.25
  1886.8 183.3 reduce-scatter.23
  2073.9 64.9 reduce-scatter.21
  2143.4 74.4 reduce-scatter.19
where the time goes:
time: 2400 us; the launch traced here: 2390 us
  waiting for transfers between devices  2000 us (83%)
  matrix products  215 us (9%)
  other arithmetic  92.3 us (4%)
  local copies, waits for them, and re-layouts  56.3 us (2%)
    reduce_scatter x1, waiting for transfers between devices, body(): lax.psum_scatter(partial_sum.astype(jnp.bfloat16), 'hist', scatter_dimens...  340 us
    all_gather x1, waiting for transfers between devices, body(): gathered = lax.all_gather(normed, 'hist', axis=1, tiled=True)  239 us
    reduce_scatter x1, waiting for transfers between devices, body(): lax.psum_scatter(back_parts.astype(jnp.bfloat16), 'hist', scatter_dimensi...  212 us
    reduce_scatter x1, waiting for transfers between devices, body(): lax.psum_scatter(up_grad.astype(jnp.bfloat16), 'tok', scatter_dimension=0...  186 us
    reduce_scatter x1, waiting for transfers between devices, body(): lax.psum_scatter(down_grad.astype(jnp.bfloat16), 'tok', scatter_dimension...  165 us
    reduce_scatter x1, waiting for transfers between devices, body(): lax.psum_scatter(contract(up_cot, full_up, 1, 1).astype(jnp.bfloat16), 'h...  93 us
    all_gather x1, waiting for transfers between devices, body(): lax.all_gather(out_total.astype(jnp.bfloat16), 'hist', axis=0, tiled=True)  90.8 us
    all_gather x1, waiting for transfers between devices, body(): lax.all_gather(residual_grad.astype(jnp.bfloat16), 'hist', axis=0, tiled=...  90.8 us
  transfers between devices with their start and end apart: 20, of which 17 were waited for; matrix products, arithmetic and copies ran while one was open for 9% of the time, Pallas kernels for 0%

commit v1 on v0

v1 whole, which is shorter than its diff:
```python
import jax
import jax.numpy as jnp
from jax import lax
from jax.experimental import pallas as pl
from jax.experimental.pallas import tpu as pltpu
from jax.sharding import PartitionSpec as P

HD = 128
ROT = 32


EPSILON = 1e-05
NEGATIVE = -1e30
HIGHEST = lax.Precision.HIGHEST


def norm_rows(values):
    row_mean = jnp.mean(values, axis=-1, keepdims=True)
    centered = values - row_mean
    inv_std = lax.rsqrt(jnp.mean(centered * centered, axis=-1, keepdims=True) + EPSILON)
    return (centered * inv_std, inv_std)


def norm_back(grad_unit, norm_unit, inv_std):
    return inv_std * (
        grad_unit
        - jnp.mean(grad_unit, axis=-1, keepdims=True)
        - norm_unit * jnp.mean(grad_unit * norm_unit, axis=-1, keepdims=True)
    )


def gelu_slope(values):
    return (
        0.5 * (1.0 + lax.erf(values * 0.7071067811865476))
        + values * jnp.exp(-0.5 * values * values) * 0.3989422804014327
    )


def rotary_tables(length, rotated):
    half_rot = rotated // 2
    frequency = 10000.0 ** (-2.0 * jnp.arange(half_rot, dtype=jnp.float32) / rotated)
    angles = jnp.arange(length, dtype=jnp.float32)[:, None] * frequency[None, :]
    return (jnp.cos(angles), jnp.sin(angles))


def rotate(values, cosine, sine_table, direction):
    half_rot = cosine.shape[1]
    first_half = values[..., :half_rot]
    second_half = values[..., half_rot : 2 * half_rot]
    cos_part = cosine[:, None, :]
    sin_part = direction * sine_table[:, None, :]
    return jnp.concatenate(
        [
            first_half * cos_part - second_half * sin_part,
            second_half * cos_part + first_half * sin_part,
            values[..., 2 * half_rot :],
        ],
        axis=-1,
    )


def contract(left_side, right_side, left_dim, right_dim):
    return lax.dot_general(
        left_side,
        right_side,
        (((left_dim,), (right_dim,)), ((), ())),
        preferred_element_type=jnp.float32,
    )


MESH = pl.DeviceIdType.MESH
ANY = pl.BlockSpec(memory_space=pl.ANY)
BF16 = jnp.bfloat16
BLOCK = 128


def coords():
    hist = lax.axis_index("hist")
    tok = lax.axis_index("tok")
    return hist // 2, hist % 2, tok // 8, (tok // 2) % 4, tok % 2


def device(x, zl, zh, y, c):
    return (x * 2 + zl, zh * 8 + y * 2 + c)


def greet(peers):
    barrier = pltpu.get_barrier_semaphore()
    for peer in peers:
        pl.semaphore_signal(barrier, inc=1, device_id=peer, device_id_type=MESH)
    pl.semaphore_wait(barrier, len(peers))


def remote(src, dst, send_sem, recv_sem, peer):
    return pltpu.make_async_remote_copy(
        src_ref=src,
        dst_ref=dst,
        send_sem=send_sem,
        recv_sem=recv_sem,
        device_id=peer,
        device_id_type=MESH,
    )


def comm_call(kernel, out_shapes, sems, collective_id, name, *args):
    return pl.pallas_call(
        kernel,
        out_shape=out_shapes,
        in_specs=[ANY] * len(args),
        out_specs=[ANY] * len(out_shapes),
        scratch_shapes=[
            pltpu.SemaphoreType.DMA((sems,)),
            pltpu.SemaphoreType.DMA((sems,)),
            pltpu.SemaphoreType.DMA((4,)),
        ],
        compiler_params=pltpu.CompilerParams(collective_id=collective_id, has_side_effects=True),
        name=name,
    )(*args)


def shape(dims, dtype=BF16):
    return jax.ShapeDtypeStruct(dims, dtype)


def x_peers(x, zl, zh, y, c):
    return [((x + k) % 4, device((x + k) % 4, zl, zh, y, c)) for k in (1, 3, 2)]


def gather_x(shard, collective_id, name):
    n, rows, width = shard.shape

    def kernel(src, dst, send, recv, local):
        x, zl, zh, y, c = coords()
        peers = x_peers(x, zl, zh, y, c)
        greet([peer for _, peer in peers])
        copies = []
        for j in range(n):
            for k, (_, peer) in enumerate(peers):
                i = j * 3 + k
                copies.append(remote(src.at[j], dst.at[j, x], send.at[i], recv.at[i], peer))
                copies[-1].start()
        own = pltpu.make_async_copy(src, dst.at[:, x], local.at[0])
        own.start()
        own.wait()
        for copy in copies:
            copy.wait()

    return comm_call(kernel, [shape((n, 4, rows, width))], 3 * n, collective_id, name, shard)[0]


def scatter_x(parts, collective_id, name):
    n, _, rows, width = parts.shape

    def kernel(src, dst, send, recv, local):
        x, zl, zh, y, c = coords()
        peers = x_peers(x, zl, zh, y, c)
        greet([peer for _, peer in peers])
        copies = []
        for j in range(n):
            for k, (px, peer) in enumerate(peers):
                i = j * 3 + k
                copies.append(remote(src.at[j, px], dst.at[j, x], send.at[i], recv.at[i], peer))
                copies[-1].start()
        own = pltpu.make_async_copy(src.at[:, x], dst.at[:, x], local.at[0])
        own.start()
        own.wait()
        for copy in copies:
            copy.wait()

    return comm_call(kernel, [shape(parts.shape)], 3 * n, collective_id, name, parts)[0]


def swap_z(mine, collective_id, name):
    def kernel(src, dst, send, recv, local):
        x, zl, zh, y, c = coords()
        peer = device(x, 1 - zl, zh, y, c)
        greet([peer])
        copy = remote(src, dst, send.at[0], recv.at[0], peer)
        copy.start()
        copy.wait()

    return comm_call(kernel, [shape(mine.shape)], 1, collective_id, name, mine)[0]


def hist_peers(x, zl):
    steps = ((0, 1), (1, 0), (3, 0), (1, 1), (3, 1), (2, 0), (2, 1))
    return [((x + dx) % 4, (zl + dz) % 2) for dx, dz in steps]


def collect(history, small, large):
    slots, _, width = history.shape

    def kernel(hist, wa, wb, own_hist, full_a, full_b, send, recv, local):
        x, zl, zh, y, c = coords()
        place = x * 2 + zl
        partner = device(x, 1 - zl, zh, y, c)
        across = device(x, 1 - zl, 1 - zh, y, c)
        sibling = device(x, zl, zh, y, 1 - c)
        rows_of = [device(x, zl, zh, (y + k) % 4, c) for k in (1, 3, 2)]
        others = hist_peers(x, zl)
        hist_devices = [device(px, pz, zh, y, c) for px, pz in others]
        greet(hist_devices + [across, sibling] + rows_of)

        def view(ref, b_zl, b_zh, b_y, b_c):
            wide = ref.shape[2] // 2
            row = (b_zh * 8 + b_y * 2 + b_c) * BLOCK
            return ref.at[
                :, pl.ds(pl.multiple_of(row, BLOCK), BLOCK), pl.ds(pl.multiple_of(b_zl * wide, wide), wide)
            ]

        fulls = (full_a, full_b)
        z_of = [(zl, zh), (1 - zl, zh), (1 - zl, 1 - zh), (zl, 1 - zh)]
        base = 7 * slots

        def arrived(zi, k, sib=0):
            steps = (0, 1, 3, 2)
            by = (y + 4 - steps[k]) % 4
            bc = 1 - c if sib else c
            out = []
            for a, full in enumerate(fulls):
                ref = view(full, *z_of[zi], by, bc)
                out.append((ref, base + ((zi * 4 + k) * 2 + sib) * 2 + a))
            return out

        def wait_block(zi, k, sib=0):
            for ref, i in arrived(zi, k, sib):
                remote(ref, ref, send.at[i], recv.at[i], sibling).wait_recv()

        started = []

        def push(src, dst, i, peer):
            copy = remote(src, dst, send.at[i], recv.at[i], peer)
            copy.start()
            started.append(copy)

        own_blocks = [view(full, zl, zh, y, c) for full in fulls]
        for a, src in enumerate((wa, wb)):
            push(src, own_blocks[a], base + (1 * 4 * 2) * 2 + a, partner)
        for a, src in enumerate((wa, wb)):
            push(src, own_blocks[a], base + (2 * 4 * 2) * 2 + a, across)
        for j in range(slots):
            for k, (px, pz) in enumerate(others):
                rows = pl.ds(pl.multiple_of((px * 2 + pz) * BLOCK, BLOCK), BLOCK)
                push(hist.at[j, rows], own_hist.at[place, j], k * slots + j, hist_devices[k])
        locals_ = [
            pltpu.make_async_copy(
                hist.at[:, pl.ds(pl.multiple_of(place * BLOCK, BLOCK), BLOCK)], own_hist.at[place], local.at[0]
            ),
            pltpu.make_async_copy(wa, own_blocks[0], local.at[1]),
            pltpu.make_async_copy(wb, own_blocks[1], local.at[2]),
        ]
        for copy in locals_:
            copy.start()

        def spread(zi, sources):
            for a, src in enumerate(sources):
                dst = view(fulls[a], *z_of[zi], y, c)
                for k, peer in enumerate(rows_of):
                    push(src, dst, base + ((zi * 4 + k + 1) * 2) * 2 + a, peer)
                push(src, dst, base + ((zi * 4) * 2 + 1) * 2 + a, sibling)

        spread(0, (wa, wb))
        wait_block(1, 0)
        for a, (ref, _) in enumerate(arrived(1, 0)):
            push(ref, ref, base + (3 * 4 * 2) * 2 + a, across)
        spread(1, [ref for ref, _ in arrived(1, 0)])
        wait_block(2, 0)
        spread(2, [ref for ref, _ in arrived(2, 0)])
        wait_block(3, 0)
        spread(3, [ref for ref, _ in arrived(3, 0)])
        for zi in range(4):
            for k in range(1, 4):
                wait_block(zi, k)
                for a, (ref, _) in enumerate(arrived(zi, k)):
                    push(ref, ref, base + ((zi * 4 + k) * 2 + 1) * 2 + a, sibling)
        for zi in range(4):
            for k in range(4):
                wait_block(zi, k, 1)
        for k, (px, pz) in enumerate(others):
            for j in range(slots):
                i = k * slots + j
                ref = own_hist.at[px * 2 + pz, j]
                remote(ref, ref, send.at[i], recv.at[i], sibling).wait_recv()
        for copy in started:
            copy.wait_send()
        for copy in locals_:
            copy.wait()

    n_a, rows_a, cols_a = small.shape
    n_b, rows_b, cols_b = large.shape
    return comm_call(
        kernel,
        [
            shape((8, slots, BLOCK, width)),
            shape((n_a, rows_a * 16, cols_a * 2)),
            shape((n_b, rows_b * 16, cols_b * 2)),
        ],
        7 * slots + 64,
        1,
        "collect",
        history,
        small,
        large,
    )


def swap_core(small, large, collective_id):
    def kernel(ga, gb, oa, ob, send, recv, local):
        x, zl, zh, y, c = coords()
        peer = device(x, zl, zh, y, 1 - c)
        greet([peer])
        copies = [
            remote(src.at[:, :, 1 - c], dst, send.at[i], recv.at[i], peer)
            for i, (src, dst) in enumerate(((ga, oa), (gb, ob)))
        ]
        for copy in copies:
            copy.start()
        for copy in copies:
            copy.wait()

    outs = [shape(g.shape[:2] + g.shape[3:]) for g in (small, large)]
    return comm_call(kernel, outs, 2, collective_id, "swap_core", small, large)


def hand_out(hist_grad, mix_grad, small, large, collective_id):
    groups, slots, rows, width = hist_grad.shape

    def kernel(hg, mg, ga, gb, ohg, omg, oa, ob, send, recv, local):
        x, zl, zh, y, c = coords()
        place = x * 2 + zl
        others = hist_peers(x, zl)
        hist_devices = [device(px, pz, zh, y, c) for px, pz in others]
        ys = [(y + k) % 4 for k in (1, 3, 2)]
        y_devices = [device(x, zl, zh, py, c) for py in ys]
        greet(hist_devices + y_devices)
        copies = []

        def push(src, dst, peer):
            i = len(copies)
            copies.append(remote(src, dst, send.at[i], recv.at[i], peer))
            copies[-1].start()

        own_rows = pl.ds(pl.multiple_of(place * BLOCK, BLOCK), BLOCK)
        for (px, pz), peer in zip(others, hist_devices):
            push(mg.at[px * 2 + pz], omg.at[place], peer)
        for py, peer in zip(ys, y_devices):
            push(gb.at[:, :, py], ob.at[y], peer)
            push(ga.at[:, :, py], oa.at[y], peer)
        for j in range(slots):
            for (px, pz), peer in zip(others, hist_devices):
                push(hg.at[px * 2 + pz, j], ohg.at[j, own_rows], peer)
        locals_ = [
            pltpu.make_async_copy(hg.at[place], ohg.at[:, own_rows], local.at[0]),
            pltpu.make_async_copy(mg.at[place], omg.at[place], local.at[1]),
            pltpu.make_async_copy(ga.at[:, :, y], oa.at[y], local.at[2]),
            pltpu.make_async_copy(gb.at[:, :, y], ob.at[y], local.at[3]),
        ]
        for copy in locals_:
            copy.start()
        for copy in copies + locals_:
            copy.wait()

    outs = [
        shape((slots, groups * rows, width)),
        shape(mix_grad.shape, jnp.float32),
    ] + [shape((4,) + g.shape[:2] + g.shape[3:]) for g in (small, large)]
    return comm_call(
        kernel, outs, 7 * (slots + 1) + 6, collective_id, "hand_out", hist_grad, mix_grad, small, large
    )


def scatter_z(small, large, collective_id):
    def kernel(ga, gb, oa, ob, send, recv, local):
        x, zl, zh, y, c = coords()
        places = [(1 - zl, zh), (1 - zl, 1 - zh), (zl, 1 - zh)]
        peers = [device(x, pl_, ph, y, c) for pl_, ph in places]
        greet(peers)
        mine = zh * 2 + zl

        def part(ref, p_zl, p_zh):
            wide = ref.shape[3] // 2
            return ref.at[:, p_zh, :, pl.ds(pl.multiple_of(p_zl * wide, wide), wide)]

        copies = []
        for place, peer in zip(places, peers):
            for src, dst in ((ga, oa), (gb, ob)):
                i = len(copies)
                copies.append(remote(part(src, *place), dst.at[mine], send.at[i], recv.at[i], peer))
                copies[-1].start()
        locals_ = [
            pltpu.make_async_copy(part(src, zl, zh), dst.at[mine], local.at[i])
            for i, (src, dst) in enumerate(((ga, oa), (gb, ob)))
        ]
        for copy in locals_:
            copy.start()
        for copy in copies + locals_:
            copy.wait()

    outs = [shape((4, g.shape[0], g.shape[2], g.shape[3] // 2)) for g in (small, large)]
    return comm_call(kernel, outs, 6, collective_id, "scatter_z", small, large)


def body(
    history,
    layer_ids,
    mix_weights,
    doc_ids,
    gains,
    w_qkv,
    w_out,
    w_up,
    w_down,
    da_in,
    da_out,
    da_bias,
    out_grad,
    mix_grad_in,
):
    place = lax.axis_index("hist")
    low_z = place % 2
    core = lax.axis_index("tok") % 2
    slots, seq_len, width = history.shape
    small = jnp.concatenate([jnp.transpose(w_qkv, (1, 0, 2)), w_out[None]], axis=0)
    large = jnp.stack([w_up, w_down], axis=0)
    own_hist, full_small, full_large = collect(history, small, large)
    w_q, w_k, w_v, full_out = (full_small[i] for i in range(4))
    full_up, full_down = full_large[0], full_large[1]
    own_hist = own_hist.reshape(8 * slots, BLOCK, width)

    own_mix = lax.dynamic_slice_in_dim(mix_weights, place * BLOCK, BLOCK, 2)
    pick = (layer_ids[:, None] == jnp.arange(own_mix.shape[1], dtype=jnp.int32)[None, :]).astype(jnp.float32)
    slot_weights = jnp.einsum("jl,slt->sjt", pick, own_mix, precision=HIGHEST)
    owned = jnp.zeros((4, BLOCK, width), jnp.float32)
    for j in range(8 * slots):
        owned = owned + slot_weights[:, j, :, None] * own_hist[j][None].astype(jnp.float32)

    norm_unit, inv_std = norm_rows(owned[:3])
    normed = (norm_unit * gains[:3, None, :]).astype(BF16)
    gathered = gather_x(normed, 2, "gather_normed").reshape(3, 4 * BLOCK, width)
    rows_here = 4 * BLOCK
    heads_here = full_out.shape[1] // HD
    cosine, sine_table = rotary_tables(seq_len, ROT)

    def here(table):
        return lax.dynamic_index_in_dim(table.reshape(4, 2, BLOCK, -1), low_z, 1, False).reshape(rows_here, -1)

    cos_here, sin_here = here(cosine), here(sine_table)

    def project(which, weight):
        return jnp.dot(gathered[which], weight, preferred_element_type=jnp.float32).reshape(
            rows_here, heads_here, HD
        )

    queries = rotate(project(0, w_q), cos_here, sin_here, 1.0).astype(BF16)
    keys_here = rotate(project(1, w_k), cos_here, sin_here, 1.0).astype(BF16)
    values_here = project(2, w_v).astype(BF16)
    mine = jnp.stack([keys_here, values_here]).reshape(2, 4, BLOCK, heads_here * HD)
    theirs = swap_z(mine, 3, "swap_keys")

    def interleave(own, other):
        first = jnp.where(low_z == 0, own, other)
        second = jnp.where(low_z == 0, other, own)
        return jnp.stack([first, second], axis=1)

    keys = interleave(mine[0], theirs[0]).reshape(seq_len, heads_here, HD)
    values = interleave(mine[1], theirs[1]).reshape(seq_len, heads_here, HD)
    key_pos = jnp.arange(seq_len, dtype=jnp.int32)
    query_pos = here(key_pos[:, None])[:, 0]
    query_docs = here(doc_ids[:, None])[:, 0]
    allowed = (key_pos[None, :] <= query_pos[:, None]) & (doc_ids[None, :] == query_docs[:, None])
    scale = HD ** (-0.5)
    scores = jnp.einsum("qhd,khd->hqk", queries, keys, preferred_element_type=jnp.float32) * scale
    scores = jnp.where(allowed[None], scores, NEGATIVE)
    row_max = jnp.max(scores, axis=-1, keepdims=True)
    shifted = jnp.exp(scores - row_max)
    row_total = jnp.sum(shifted, axis=-1, keepdims=True)
    probs = shifted / row_total
    attended = jnp.einsum("hqk,khd->qhd", probs.astype(BF16), values, preferred_element_type=jnp.float32)
    heads_flat = attended.reshape(rows_here, -1).astype(BF16)

    def reduce_rows(partial, collective_id, name):
        parts = scatter_x(partial.astype(BF16).reshape(-1, 4, BLOCK, width), collective_id, name)
        return jnp.sum(parts.astype(jnp.float32), axis=1)

    def all_rows(rows, collective_id, name):
        return gather_x(rows.astype(BF16)[None], collective_id, name).reshape(rows_here, width)

    attn_owned = reduce_rows(contract(heads_flat, full_out, 1, 1), 4, "scatter_attn")[0]
    residual = owned[3] + attn_owned
    mid_unit, mid_std = norm_rows(residual)
    mid_all = all_rows(mid_unit * gains[3], 5, "gather_mid")
    up_proj = jnp.dot(mid_all, full_up, preferred_element_type=jnp.float32)
    activated = jax.nn.gelu(up_proj, approximate=False).astype(BF16)
    mlp_owned = reduce_rows(contract(activated, full_down, 1, 1), 6, "scatter_mlp")[0]
    layer_out = residual + mlp_owned
    rms_inv = lax.rsqrt(jnp.mean(layer_out * layer_out, axis=-1, keepdims=True) + EPSILON)
    rms_unit = layer_out * rms_inv
    da_norm = (rms_unit * gains[4]).astype(BF16)
    inner_pre = jnp.dot(da_norm, da_in, preferred_element_type=jnp.float32)
    inner_act = jax.nn.gelu(inner_pre, approximate=False).astype(BF16)
    mix_next = jnp.dot(inner_act, da_out, preferred_element_type=jnp.float32) + da_bias
    bias_grad = jnp.sum(mix_grad_in, axis=0)
    mix_cot = mix_grad_in.astype(BF16)
    da_out_grad = contract(inner_act, mix_cot, 0, 0)
    inner_cot = (contract(mix_cot, da_out, 1, 1) * gelu_slope(inner_pre)).astype(BF16)
    da_in_grad = contract(da_norm, inner_cot, 0, 0)
    da_in_sum, da_out_sum, bias_sum = lax.psum((da_in_grad, da_out_grad, bias_grad), ("hist", "tok"))
    rms_grad = contract(inner_cot, da_in, 1, 1)
    rms_gain_grad = jnp.sum(rms_grad * rms_unit, axis=0)
    rms_scaled = rms_grad * gains[4]
    out_total = out_grad.astype(jnp.float32) + rms_inv * (
        rms_scaled - rms_unit * jnp.mean(rms_scaled * rms_unit, axis=-1, keepdims=True)
    )
    mlp_cot = all_rows(out_total, 7, "gather_mlp_cot")
    down_grad = contract(mlp_cot, activated, 0, 0)
    up_cot = (
        jnp.dot(mlp_cot, full_down, preferred_element_type=jnp.float32) * gelu_slope(up_proj)
    ).astype(BF16)
    up_grad = contract(mid_all, up_cot, 0, 0)
    mid_back = reduce_rows(contract(up_cot, full_up, 1, 1), 8, "scatter_mid")[0]
    mid_gain_grad = jnp.sum(mid_back * mid_unit, axis=0)
    residual_grad = out_total + norm_back(mid_back * gains[3], mid_unit, mid_std)
    attn_cot = all_rows(residual_grad, 9, "gather_attn_cot")
    out_proj_grad = contract(attn_cot, heads_flat, 0, 0)
    heads_cot = (
        jnp.dot(attn_cot, full_out, preferred_element_type=jnp.float32)
        .astype(BF16)
        .reshape(rows_here, heads_here, HD)
    )
    prob_grad = jnp.einsum("qhd,khd->hqk", heads_cot, values, preferred_element_type=jnp.float32)
    row_dot = jnp.sum(probs * prob_grad, axis=-1, keepdims=True)
    score_cot = (probs * (prob_grad - row_dot)).astype(BF16)
    query_grad = jnp.einsum("hqk,khd->qhd", score_cot, keys, preferred_element_type=jnp.float32) * scale
    key_grad = jnp.einsum("hqk,qhd->khd", score_cot, queries, preferred_element_type=jnp.float32) * scale
    value_grad = jnp.einsum("hqk,qhd->khd", probs.astype(BF16), heads_cot, preferred_element_type=jnp.float32)
    both = jnp.stack([key_grad, value_grad]).reshape(2, 4, 2, BLOCK, heads_here * HD)
    keep = lax.dynamic_index_in_dim(both, low_z, 2, False)
    give = lax.dynamic_index_in_dim(both, 1 - low_z, 2, False).astype(BF16)
    both = keep + swap_z(give, 10, "swap_key_grads").astype(jnp.float32)
    both = both.reshape(2, rows_here, heads_here, HD)
    proj_cots = (
        rotate(query_grad, cos_here, sin_here, -1.0).reshape(rows_here, -1).astype(BF16),
        rotate(both[0], cos_here, sin_here, -1.0).reshape(rows_here, -1).astype(BF16),
        both[1].reshape(rows_here, -1).astype(BF16),
    )
    small_grad = jnp.stack(
        [contract(gathered[which], proj_cots[which], 0, 0).astype(BF16) for which in range(3)]
        + [out_proj_grad.astype(BF16)]
    )
    large_grad = jnp.stack([up_grad.astype(BF16), down_grad.astype(BF16)])
    back_parts = jnp.stack(
        [contract(cot, weight, 1, 1).astype(BF16) for cot, weight in zip(proj_cots, (w_q, w_k, w_v))]
    )
    in_back = reduce_rows(back_parts, 11, "scatter_in")
    in_gain_grad = jnp.sum(in_back * norm_unit, axis=1)
    stream_part = norm_back(in_back * gains[:3, None, :], norm_unit, inv_std)
    stream_cot = jnp.concatenate([stream_part, residual_grad[None]], axis=0).astype(BF16)
    stream_wide = stream_cot.astype(jnp.float32)
    gains_local = jnp.concatenate([in_gain_grad, mid_gain_grad[None], rms_gain_grad[None]], axis=0)
    gains_sum = lax.psum(gains_local, ("hist", "tok"))

    hist_grads, mix_grads = [], []
    for j in range(8 * slots):
        hist_grads.append(jnp.sum(slot_weights[:, j, :, None] * stream_wide, axis=0).astype(BF16))
        mix_grads.append(jnp.sum(own_hist[j].astype(jnp.float32)[None] * stream_wide, axis=-1))
    hist_grads = jnp.stack(hist_grads).reshape(8, slots, BLOCK, width)
    mix_grads = jnp.stack(mix_grads).reshape(8, slots * 4, BLOCK)

    def by_core(grad):
        return grad.reshape(grad.shape[0], 8, 2, BLOCK, grad.shape[2])

    small_grad, large_grad = by_core(small_grad), by_core(large_grad)
    other_small, other_large = swap_core(small_grad, large_grad, 12)

    def add_core(grad, other):
        kept = lax.dynamic_index_in_dim(grad, core, 2, False)
        total = (kept.astype(jnp.float32) + other.astype(jnp.float32)).astype(BF16)
        return total.reshape(total.shape[0], 2, 4, BLOCK, total.shape[3])

    history_grad, mix_out, y_small, y_large = hand_out(
        hist_grads, mix_grads, add_core(small_grad, other_small), add_core(large_grad, other_large), 13
    )
    mix_grad = jnp.transpose(mix_out.reshape(8, slots, 4, BLOCK), (2, 1, 0, 3)).reshape(4, slots, seq_len)

    def add_four(parts):
        return jnp.sum(parts.astype(jnp.float32), axis=0)

    z_small, z_large = scatter_z(add_four(y_small).astype(BF16), add_four(y_large).astype(BF16), 14)
    small_sum, large_sum = add_four(z_small), add_four(z_large)
    return (
        layer_out.astype(BF16),
        mix_next,
        history_grad,
        mix_grad,
        gains_sum,
        jnp.transpose(small_sum[:3], (1, 0, 2)),
        small_sum[3],
        large_sum[0],
        large_sum[1],
        da_in_sum,
        da_out_sum,
        bias_sum,
    )


def solution(mesh):
    return jax.shard_map(
        body,
        mesh=mesh,
        in_specs=(
            P("hist", "tok", None),
            P(),
            P(None, None, "tok"),
            P("tok"),
            P(),
            P("tok", None, "hist"),
            P("tok", "hist"),
            P("tok", "hist"),
            P("tok", "hist"),
            P(),
            P(),
            P(),
            P(("tok", "hist"), None),
            P(("tok", "hist"), None),
        ),
        out_specs=(
            P(("tok", "hist"), None),
            P(("tok", "hist"), None),
            P("hist", "tok", None),
            P(None, "hist", "tok"),
            P(),
            P("tok", None, "hist"),
            P("tok", "hist"),
            P("tok", "hist"),
            P("tok", "hist"),
            P(),
            P(),
            P(),
        ),
        check_vma=False,
    )
```

time: 2400 us -> 1170 us (0.49)
  waiting for transfers between devices: 2000 us -> 57 us
  Pallas kernels: 0 us -> 701 us
  matrix products: 215 us -> 134 us
  other arithmetic: 92.3 us -> 151 us
  local copies, waits for them, and re-layouts: 56.3 us -> 102 us
    reduce_scatter x9 -> x0, waiting for transfers between devices: 1320 us -> none  [the longest x1 340 us: body(): lax.psum_scatter(partial_sum.astype(jnp.bfloat16), 'hist', scatter_dimens...]
    pallas_call x0 -> x14, Pallas kernels: none -> 701 us  [comm_call(): pl.pallas_call(kernel, out_shape=out_shapes, in_specs=[ANY] * len(args),...]
    all_gather x9 -> x0, waiting for transfers between devices: 629 us -> none  [the longest x1 239 us: body(): gathered = lax.all_gather(normed, 'hist', axis=1, tiled=True)]
    dot_general x20 -> x10, matrix products: 126 us -> 33.7 us  [the longest x3 10.5 us: project(): jnp.dot(gathered[which], weight, preferred_element_type=jnp.float32)]
    reduce_sum x3 -> x12, other arithmetic: 19.6 us -> 54.3 us  [the longest x2 20.1 us: body(): jnp.sum(slot_weights[:, j, :, None] * stream_wide, axis=0).astype(BF16)]
    unnamed x85 -> x405, local copies, waits for them, and re-layouts: 14.8 us -> 43.1 us
    dynamic_update_slice x4 -> x0, local copies, waits for them, and re-layouts: 24.6 us -> none  [attend(): lax.map(one_block, jnp.arange(length // row_block, dtype=jnp.int32))]
  transfers between devices with their start and end apart: 20 -> 2, of which waited for: 17 -> 1; matrix products, arithmetic and copies ran while one was open for 9% -> 11% of each run, Pallas kernels for 0% -> 20%
where the time goes in v1:
time: 1170 us; the launch traced here: 1160 us
  Pallas kernels  701 us (60%)
  other arithmetic  151 us (13%)
  matrix products  134 us (11%)
  local copies, waits for them, and re-layouts  102 us (9%)
  waiting for transfers between devices  57 us (5%)
  between operations  17 us (1%)
    pallas_call x14, Pallas kernels, comm_call(): pl.pallas_call(kernel, out_shape=out_shapes, in_specs=[ANY] * len(args),...  701 us
    dot_general x16, matrix products, contract(): lax.dot_general(left_side, right_side, (((left_dim,), (right_dim,)), ((),...  63.3 us
    psum x1, waiting for transfers between devices, body(): lax.psum((da_in_grad, da_out_grad, bias_grad), ('hist', 'tok'))  57 us
    unnamed x405, local copies, waits for them, and re-layouts  43.1 us
  transfers between devices with their start and end apart: 2, of which 1 were waited for; matrix products, arithmetic and copies ran while one was open for 11% of the time, Pallas kernels for 20%

profile of v1, /device:TPU:1, one launch (start us, length us, event | category | flops | bytes accessed | tf_op | source)
XLA Modules:
  0.0 1161.9 jit_solution(8482857647198816658)
XLA Ops:
  10.8 164.8 %collect.1 = (bf16[8,3,128,2048]{3,2,1,0:T(8,128)(2,1)}, bf16[4,2048,512]{2,1,0:T(8,128)(2,1)}, bf16[2,2048,2048]{2,1,0:T(8,128)(2,1)}) custom-call(bf16[3,1024,2048]{2,1,0:T(8,128)(2,1)} %hist.1, bf16[4,128,256]{2,1,0:T(8,128)(2,1)} %pad_maximum_fusion.13.wa, bf16[2,128,1024]{2,1,0:T(8,128)(2,1)} %pad_maximum_fusion.7.wb), custom_call_target="tpu_custom_call" | custom-call | tf_op jit(solution)/shard_map/collect/pallas_call | solution.py:106
  191.5 10.2 multiply_add_fusion
  206.4 74.8 %gather_normed.1 = bf16[3,4,128,2048]{3,2,1,0:T(8,128)(2,1)} custom-call(bf16[3,128,2048]{2,1,0:T(8,128)(2,1)} %multiply_convert_fusion.2.src), custom_call_target="tpu_custom_call" | custom-call | tf_op jit(solution)/shard_map/gather_normed/pallas_call | solution.py:106
  323.1 22.1 %swap_keys.1 = bf16[2,4,128,512]{3,2,1,0:T(8,128)(2,1)} custom-call(bf16[2,4,128,512]{3,2,1,0:T(8,128)(2,1)} %pad_maximum_fusion.4.src), custom_call_target="tpu_custom_call" | custom-call | tf_op jit(solution)/shard_map/swap_keys/pallas_call | solution.py:106
  369.2 23.7 %scatter_attn.1 = bf16[1,4,128,2048]{3,2,1,0:T(8,128)(2,1)} custom-call(bf16[1,4,128,2048]{3,2,1,0:T(8,128)(2,1)} %bitcast.505), custom_call_target="tpu_custom_call" | custom-call | tf_op jit(solution)/shard_map/scatter_attn/pallas_call | solution.py:106
  399.1 21.7 %gather_mid.1 = bf16[1,4,128,2048]{3,2,1,0:T(8,128)(2,1)} custom-call(bf16[1,128,2048]{2,1,0:T(8,128)(2,1)} %fusion.131.src), custom_call_target="tpu_custom_call" | custom-call | tf_op jit(solution)/shard_map/gather_mid/pallas_call | solution.py:106
  420.7 17.7 %fusion.20 = (bf16[512,2048]{1,0:T(8,128)(2,1)S(1)}, f32[512,2048]{1,0:T(8,128)}) fusion(bf16[512,2048]{1,0:T(8,128)(2,1)} %bitcast.495, bf16[2,2048,2048]{2,1,0:T(8,128)(2,1)} %get-tuple-element.25), kind=kOutput, calls=%fused_computation.88 | convolution fusion | flops 4363124736 | bytes 16777216 | tf_op jit(solution)/shard_map/dot_general | solution.py:492
  438.5 9.9 fusion.90
  448.4 21.0 %scatter_mlp.1 = bf16[1,4,128,2048]{3,2,1,0:T(8,128)(2,1)} custom-call(bf16[1,4,128,2048]{3,2,1,0:T(8,128)(2,1)} %bitcast.506), custom_call_target="tpu_custom_call" | custom-call | tf_op jit(solution)/shard_map/scatter_mlp/pallas_call | solution.py:106
  476.8 19.9 %gather_mlp_cot.1 = bf16[1,4,128,2048]{3,2,1,0:T(8,128)(2,1)} custom-call(bf16[1,128,2048]{2,1,0:T(8,128)(2,1)} %convert_bitcast_fusion.src), custom_call_target="tpu_custom_call" | custom-call | tf_op jit(solution)/shard_map/gather_mlp_cot/pallas_call | solution.py:106
  496.7 9.3 fusion.26
  506.0 9.8 fusion.87
  515.8 18.9 %scatter_mid.1 = bf16[1,4,128,2048]{3,2,1,0:T(8,128)(2,1)} custom-call(bf16[1,4,128,2048]{3,2,1,0:T(8,128)(2,1)} %bitcast.504), custom_call_target="tpu_custom_call" | custom-call | tf_op jit(solution)/shard_map/scatter_mid/pallas_call | solution.py:106
  539.6 19.5 %gather_attn_cot.1 = bf16[1,4,128,2048]{3,2,1,0:T(8,128)(2,1)} custom-call(bf16[1,128,2048]{2,1,0:T(8,128)(2,1)} %get-tuple-element.165.src), custom_call_target="tpu_custom_call" | custom-call | tf_op jit(solution)/shard_map/gather_attn_cot/pallas_call | solution.py:106
  601.6 16.1 %swap_key_grads.1 = bf16[2,4,128,512]{3,2,1,0:T(8,128)(2,1)} custom-call(bf16[2,4,128,512]{3,2,1,0:T(8,128)(2,1)} %fusion.127.src), custom_call_target="tpu_custom_call" | custom-call | tf_op jit(solution)/shard_map/swap_key_grads/pallas_call | solution.py:106
  649.0 61.6 %scatter_in.1 = bf16[3,4,128,2048]{3,2,1,0:T(8,128)(2,1)} custom-call(bf16[3,4,128,2048]{3,2,1,0:T(8,128)(2,1)} %pad_maximum_fusion.2.src), custom_call_target="tpu_custom_call" | custom-call | tf_op jit(solution)/shard_map/scatter_in/pallas_call | solution.py:106
  724.7 9.9 fusion.50
  734.8 10.3 fusion.44
  795.0 30.2 %swap_core.1 = (bf16[4,8,128,512]{3,2,1,0:T(8,128)(2,1)}, bf16[2,8,128,2048]{3,2,1,0:T(8,128)(2,1)}) custom-call(bf16[4,8,2,128,512]{4,3,2,1,0:T(8,128)(2,1)} %pad_maximum_fusion.1.ga, bf16[2,8,2,128,2048]{4,3,2,1,0:T(8,128)(2,1)} %pad_maximum_fusion.gb), custom_call_target="tpu_custom_call" | custom-call | tf_op jit(solution)/shard_map/swap_core/pallas_call | solution.py:106
  832.6 8.7 fusion.1
  860.5 169.1 %hand_out.1 = (bf16[3,1024,2048]{2,1,0:T(8,128)(2,1)}, f32[8,12,128]{2,1,0:T(8,128)}, bf16[4,4,2,128,512]{4,3,2,1,0:T(8,128)(2,1)}, bf16[4,2,2,128,2048]{4,3,2,1,0:T(8,128)(2,1)}) custom-call(bf16[8,3,128,2048]{3,2,1,0:T(8,128)(2,1)} %bitcast.130.hg, f32[8,12,128]{2,1,0:T(8,128)} %reshape.690.mg, bf16[4,2,4,128,512]{4,3,2,1,0:T(8,128)(2,1)} %bitcast.490, ...), custom_call_target="tpu_custom_call" | custom-call | tf_op jit(solution)/shard_map/hand_out/pallas_call | solution.py:106
  1041.0 37.2 %scatter_z.1 = (bf16[4,4,128,256]{3,2,1,0:T(8,128)(2,1)}, bf16[4,2,128,1024]{3,2,1,0:T(8,128)(2,1)}) custom-call(bf16[4,2,128,512]{3,2,1,0:T(8,128)(2,1)} %reduce_sum.724.ga, bf16[2,2,128,2048]{3,2,1,0:T(8,128)(2,1)} %reduce_sum.725.gb), custom_call_target="tpu_custom_call" | custom-call | tf_op jit(solution)/shard_map/scatter_z/pallas_call | solution.py:106
  1084.1 57.0 %all-reduce.4.cloned.1.call-done = f32[2048,100]{0,1:T(8,128)} async-done(((f32[2048,100]{0,1:T(8,128)}), f32[2048,100]{0,1:T(8,128)}) %all-reduce.4.cloned.1.call-update) | async-done | bytes 819216 | tf_op jit(solution)/shard_map/psum | solution.py:507
  1141.1 10.8 copy.156
  (546 shorter events, 290.7 us)
Async XLA Ops:
  7.2 464.6 %copy-start = (bf16[2048,100]{0,1:T(8,128)(2,1)S(1)}, bf16[2048,100]{0,1:T(8,128)(2,1)}, u32[]{:S(2)}) copy-start(bf16[2048,100]{0,1:T(8,128)(2,1)} %param.23) | copy-start | bytes 1228804
  7.2 1076.9 %all-reduce.6.cloned.1.call-start = ((), (), s32[]{:S(2)}) async-start(), calls=%async_computation.1 | async-start | bytes 238592 | tf_op jit(solution)/shard_map/psum | solution.py:560
  184.2 17.5 %copy-start.9 = (f32[128,2048]{1,0:T(8,128)}, f32[128,2048]{1,0:T(8,128)S(1)}, u32[]{:S(2)}) copy-start(f32[128,2048]{1,0:T(8,128)S(1)} %get-tuple-element.104) | copy-start | bytes 3145732
  184.2 17.5 %copy-start.11 = (f32[128,2048]{1,0:T(8,128)}, f32[128,2048]{1,0:T(8,128)S(1)}, u32[]{:S(2)}) copy-start(f32[128,2048]{1,0:T(8,128)S(1)} %get-tuple-element.105) | copy-start | bytes 3145732
  321.1 24.0 %copy-start.66 = (bf16[4,1,128,512]{3,2,0,1:T(8,128)(2,1)S(1)}, bf16[4,1,128,512]{3,2,0,1:T(8,128)(2,1)}, u32[]{:S(2)}) copy-start(bf16[4,1,128,512]{3,2,0,1:T(8,128)(2,1)} %squeeze.50) | copy-start | bytes 1572868
  396.5 42.0 %copy-start.151 = (f32[128]{0:T(128)}, f32[128]{0:T(128)S(1)}, u32[]{:S(2)}) copy-start(f32[128]{0:T(128)S(1)} %broadcast_multiply_fusion.8) | copy-start | bytes 1540
  396.7 41.7 %copy-start.157 = (f32[128]{0:T(128)}, f32[128]{0:T(128)S(1)}, u32[]{:S(2)}) copy-start(f32[128]{0:T(128)S(1)} %add_rsqrt_fusion.2) | copy-start | bytes 1540
  515.8 21.1 %copy-start.152 = (f32[128]{0:T(128)S(1)}, f32[128]{0:T(128)}, u32[]{:S(2)}) copy-start(f32[128]{0:T(128)} %copy-done.151) | copy-start | bytes 1540
  515.8 21.2 %copy-start.158 = (f32[128]{0:T(128)S(1)}, f32[128]{0:T(128)}, u32[]{:S(2)}) copy-start(f32[128]{0:T(128)} %copy-done.157) | copy-start | bytes 1540
  515.8 22.1 %copy-start.155 = (f32[128]{0:T(128)S(1)}, f32[128]{0:T(128)}, u32[]{:S(2)}) copy-start(f32[128]{0:T(128)} %copy-done.154) | copy-start | bytes 1540
  719.0 422.1 %all-reduce.4.cloned.1.call-start = ((), (), s32[]{:S(2)}) async-start(), calls=%async_computation | async-start | bytes 1703936 | tf_op jit(solution)/shard_map/psum | solution.py:507
  724.6 20.4 %copy-start.29 = (f32[128,2048]{1,0:T(8,128)S(1)}, f32[128,2048]{1,0:T(8,128)}, u32[]{:S(2)}) copy-start(f32[128,2048]{1,0:T(8,128)} %get-tuple-element.103) | copy-start | bytes 3145732
  724.7 20.4 %copy-start.30 = (f32[128,2048]{1,0:T(8,128)S(1)}, f32[128,2048]{1,0:T(8,128)}, u32[]{:S(2)}) copy-start(f32[128,2048]{1,0:T(8,128)} %get-tuple-element.116) | copy-start | bytes 3145732
  724.7 20.4 %copy-start.31 = (f32[128,2048]{1,0:T(8,128)S(1)}, f32[128,2048]{1,0:T(8,128)}, u32[]{:S(2)}) copy-start(f32[128,2048]{1,0:T(8,128)} %get-tuple-element.117) | copy-start | bytes 3145732
  724.7 20.4 %copy-start.32 = (f32[128,2048]{1,0:T(8,128)S(1)}, f32[128,2048]{1,0:T(8,128)}, u32[]{:S(2)}) copy-start(f32[128,2048]{1,0:T(8,128)} %get-tuple-element.118) | copy-start | bytes 3145732
  724.7 20.4 %copy-start.33 = (f32[128,2048]{1,0:T(8,128)S(1)}, f32[128,2048]{1,0:T(8,128)}, u32[]{:S(2)}) copy-start(f32[128,2048]{1,0:T(8,128)} %get-tuple-element.119) | copy-start | bytes 3145732
  724.7 20.4 %copy-start.34 = (f32[128,2048]{1,0:T(8,128)S(1)}, f32[128,2048]{1,0:T(8,128)}, u32[]{:S(2)}) copy-start(f32[128,2048]{1,0:T(8,128)} %get-tuple-element.120) | copy-start | bytes 3145732
  734.7 15.5 %copy-start.21 = (f32[128,2048]{1,0:T(8,128)S(1)}, f32[128,2048]{1,0:T(8,128)}, u32[]{:S(2)}) copy-start(f32[128,2048]{1,0:T(8,128)} %get-tuple-element.114) | copy-start | bytes 3145732
  734.7 15.5 %copy-start.22 = (f32[128,2048]{1,0:T(8,128)S(1)}, f32[128,2048]{1,0:T(8,128)}, u32[]{:S(2)}) copy-start(f32[128,2048]{1,0:T(8,128)} %get-tuple-element.115) | copy-start | bytes 3145732
  1041.0 40.2 %copy-start.161 = (bf16[100,100]{1,0:T(8,128)(2,1)S(1)}, bf16[100,100]{1,0:T(8,128)(2,1)}, u32[]{:S(2)}) copy-start(bf16[100,100]{1,0:T(8,128)(2,1)} %param.24) | copy-start | bytes 60004
  1041.0 40.2 %copy-start.162 = (f32[100]{0:T(128)S(1)}, f32[100]{0:T(128)}, u32[]{:S(2)}) copy-start(f32[100]{0:T(128)} %param.25) | copy-start | bytes 1204
  1041.0 41.1 %copy-start.91 = (f32[8,12,128]{2,1,0:T(8,128)S(1)}, f32[8,12,128]{2,1,0:T(8,128)}, u32[]{:S(2)}) copy-start(f32[8,12,128]{2,1,0:T(8,128)} %get-tuple-element.29) | copy-start | bytes 147460
  1141.1 13.0 %copy-start.163 = (f32[100]{0:T(128)S(1)}, f32[100]{0:T(128)}, u32[]{:S(2)}) copy-start(f32[100]{0:T(128)} %get-tuple-element.237) | copy-start | bytes 1204
  1141.1 13.5 %copy-start.1 = (bf16[2048,100]{0,1:T(8,128)(2,1)S(1)}, bf16[2048,100]{0,1:T(8,128)(2,1)}, u32[]{:S(2)}) copy-start(bf16[2048,100]{0,1:T(8,128)(2,1)} %param.23) | copy-start | bytes 1228804
  (154 other events, 1051.8 us)
Sparse Core Ops, SparseCore 0:
  719.1 151.1 all-reduce.5
  876.4 264.6 all-reduce.3

commit v2 on v1

v2 whole, which is shorter than its diff:
```python
import jax
import jax.numpy as jnp
from jax import lax
from jax.experimental import pallas as pl
from jax.experimental.pallas import tpu as pltpu
from jax.sharding import PartitionSpec as P

HD = 128
ROT = 32


EPSILON = 1e-05
NEGATIVE = -1e30
HIGHEST = lax.Precision.HIGHEST


def norm_rows(values):
    row_mean = jnp.mean(values, axis=-1, keepdims=True)
    centered = values - row_mean
    inv_std = lax.rsqrt(jnp.mean(centered * centered, axis=-1, keepdims=True) + EPSILON)
    return (centered * inv_std, inv_std)


def norm_back(grad_unit, norm_unit, inv_std):
    return inv_std * (
        grad_unit
        - jnp.mean(grad_unit, axis=-1, keepdims=True)
        - norm_unit * jnp.mean(grad_unit * norm_unit, axis=-1, keepdims=True)
    )


def gelu_slope(values):
    return (
        0.5 * (1.0 + lax.erf(values * 0.7071067811865476))
        + values * jnp.exp(-0.5 * values * values) * 0.3989422804014327
    )


def rotary_tables(length, rotated):
    half_rot = rotated // 2
    frequency = 10000.0 ** (-2.0 * jnp.arange(half_rot, dtype=jnp.float32) / rotated)
    angles = jnp.arange(length, dtype=jnp.float32)[:, None] * frequency[None, :]
    return (jnp.cos(angles), jnp.sin(angles))


def rotate(values, cosine, sine_table, direction):
    half_rot = cosine.shape[1]
    first_half = values[..., :half_rot]
    second_half = values[..., half_rot : 2 * half_rot]
    cos_part = cosine[:, None, :]
    sin_part = direction * sine_table[:, None, :]
    return jnp.concatenate(
        [
            first_half * cos_part - second_half * sin_part,
            second_half * cos_part + first_half * sin_part,
            values[..., 2 * half_rot :],
        ],
        axis=-1,
    )


def contract(left_side, right_side, left_dim, right_dim):
    return lax.dot_general(
        left_side,
        right_side,
        (((left_dim,), (right_dim,)), ((), ())),
        preferred_element_type=jnp.float32,
    )


MESH = pl.DeviceIdType.MESH
ANY = pl.BlockSpec(memory_space=pl.ANY)
BF16 = jnp.bfloat16
BLOCK = 128


def coords():
    hist = lax.axis_index("hist")
    tok = lax.axis_index("tok")
    return hist // 2, hist % 2, tok // 8, (tok // 2) % 4, tok % 2


def device(x, zl, zh, y, c):
    return (x * 2 + zl, zh * 8 + y * 2 + c)


def greet(peers):
    barrier = pltpu.get_barrier_semaphore()
    for peer in peers:
        pl.semaphore_signal(barrier, inc=1, device_id=peer, device_id_type=MESH)
    pl.semaphore_wait(barrier, len(peers))


def remote(src, dst, send_sem, recv_sem, peer):
    return pltpu.make_async_remote_copy(
        src_ref=src,
        dst_ref=dst,
        send_sem=send_sem,
        recv_sem=recv_sem,
        device_id=peer,
        device_id_type=MESH,
    )


def comm_call(kernel, out_shapes, sems, collective_id, name, *args):
    return pl.pallas_call(
        kernel,
        out_shape=out_shapes,
        in_specs=[ANY] * len(args),
        out_specs=[ANY] * len(out_shapes),
        scratch_shapes=[
            pltpu.SemaphoreType.DMA((sems,)),
            pltpu.SemaphoreType.DMA((sems,)),
            pltpu.SemaphoreType.DMA((4,)),
        ],
        compiler_params=pltpu.CompilerParams(collective_id=collective_id, has_side_effects=True),
        name=name,
    )(*args)


def shape(dims, dtype=BF16):
    return jax.ShapeDtypeStruct(dims, dtype)


def x_peers(x, zl, zh, y, c):
    return [((x + k) % 4, device((x + k) % 4, zl, zh, y, c)) for k in (1, 3, 2)]


def z_peers(x, zl, zh, y, c):
    places = [(zh * 2 + zl + k) % 4 for k in (1, 3, 2)]
    return [(place, device(x, place % 2, place // 2, y, c)) for place in places]


def y_peers(x, zl, zh, y, c):
    return [((y + k) % 4, device(x, zl, zh, (y + k) % 4, c)) for k in (1, 3, 2)]


VMEM = pl.BlockSpec(memory_space=pltpu.VMEM)
SIDE_ROWS = 136


def exchange(src, slots, mine, peers, send, recv, first):
    copies = []
    for k, (place, peer) in enumerate(peers):
        part = src(place) if callable(src) else src
        copies.append(remote(part, slots.at[mine], send.at[first + k], recv.at[first + k], peer))
        copies[-1].start()
    return copies


def gather_x(shard, collective_id, name, down=None, up=None):
    n, rows, width = shard.shape
    side = 0 if down is None and up is None else 1

    def kernel(*refs):
        src, dst = refs[0], refs[1 + side]
        send, recv, local, sends, recvs = refs[2 + 2 * side : 7 + 2 * side]
        x, zl, zh, y, c = coords()
        z = zh * 2 + zl
        peers = x_peers(x, zl, zh, y, c)
        along_z = z_peers(x, zl, zh, y, c)
        along_y = y_peers(x, zl, zh, y, c)
        sibling = device(x, zl, zh, y, 1 - c)
        greeted = [peer for _, peer in peers]
        if side:
            greeted = greeted + [peer for _, peer in along_z + along_y]
        if down is not None:
            greeted = greeted + [sibling]
        greet(greeted)
        copies = []
        if down is not None:
            given, result = refs[1], refs[3]
            y_slots, z_part, z_slots, c_part, c_slot = refs[9:]
            first = exchange(lambda py: given.at[py], y_slots, y, along_y, sends, recvs, 0)
        if up is not None:
            given, result = refs[1], refs[3]
            x_slots, total = refs[9:]
            first = exchange(given, x_slots, x, peers, sends, recvs, 0)
        for j in range(n):
            for k, (_, peer) in enumerate(peers):
                i = j * 3 + k
                copies.append(remote(src.at[j], dst.at[j, x], send.at[i], recv.at[i], peer))
                copies[-1].start()
        own = pltpu.make_async_copy(src, dst.at[:, x], local.at[0])
        own.start()
        if down is not None:
            y_slots[y] = given[y]
            for copy in first:
                copy.wait()
            z_part[...] = y_slots[0] + y_slots[1] + y_slots[2] + y_slots[3]
            second = exchange(lambda pz: z_part.at[pz], z_slots, z, along_z, sends, recvs, 3)
            z_slots[z] = z_part[z]
            for copy in second:
                copy.wait()
            c_part[...] = z_slots[0] + z_slots[1] + z_slots[2] + z_slots[3]
            third = remote(c_part, c_slot, sends.at[6], recvs.at[6], sibling)
            third.start()
            third.wait()
            result[...] = c_part[...] + c_slot[...]
        if up is not None:
            x_slots[x] = given[...]
            for copy in first:
                copy.wait()
            total[y, z] = x_slots[0] + x_slots[1] + x_slots[2] + x_slots[3]
            second = exchange(total.at[y, z], total.at[y], z, along_z, sends, recvs, 3)
            for copy in second:
                copy.wait()
            third = exchange(total.at[y], total, y, along_y, sends, recvs, 6)
            for copy in third:
                copy.wait()
            result[...] = total[...]
        own.wait()
        for copy in copies:
            copy.wait()

    in_specs, args = [ANY], [shard]
    out_specs, outs = [ANY], [shape((n, 4, rows, width))]
    scratch = [
        pltpu.SemaphoreType.DMA((3 * n,)),
        pltpu.SemaphoreType.DMA((3 * n,)),
        pltpu.SemaphoreType.DMA((4,)),
        pltpu.SemaphoreType.DMA((9,)),
        pltpu.SemaphoreType.DMA((9,)),
    ]
    if side:
        in_specs, out_specs = [ANY, VMEM], [ANY, VMEM]
        args = [shard, down if up is None else up]
        piece = (SIDE_ROWS, 128)
        whole = (4, 4) + piece
        outs = outs + [shape(piece if up is None else whole, jnp.float32)]
        dims = (whole, (4,) + piece, (4,) + piece, piece, piece) if up is None else ((4,) + piece, whole)
        scratch = scratch + [pltpu.VMEM(d, jnp.float32) for d in dims]
    result = pl.pallas_call(
        kernel,
        out_shape=outs,
        in_specs=in_specs,
        out_specs=out_specs,
        scratch_shapes=scratch,
        compiler_params=pltpu.CompilerParams(
            collective_id=collective_id, has_side_effects=True, vmem_limit_bytes=24 * 2**20
        ),
        name=name,
    )(*args)
    return result if side else result[0]


def scatter_x(parts, collective_id, name):
    n, _, rows, width = parts.shape

    def kernel(src, dst, send, recv, local):
        x, zl, zh, y, c = coords()
        peers = x_peers(x, zl, zh, y, c)
        greet([peer for _, peer in peers])
        copies = []
        for j in range(n):
            for k, (px, peer) in enumerate(peers):
                i = j * 3 + k
                copies.append(remote(src.at[j, px], dst.at[j, x], send.at[i], recv.at[i], peer))
                copies[-1].start()
        own = pltpu.make_async_copy(src.at[:, x], dst.at[:, x], local.at[0])
        own.start()
        own.wait()
        for copy in copies:
            copy.wait()

    return comm_call(kernel, [shape(parts.shape)], 3 * n, collective_id, name, parts)[0]


def swap_z(mine, collective_id, name):
    def kernel(src, dst, send, recv, local):
        x, zl, zh, y, c = coords()
        peer = device(x, 1 - zl, zh, y, c)
        greet([peer])
        copy = remote(src, dst, send.at[0], recv.at[0], peer)
        copy.start()
        copy.wait()

    return comm_call(kernel, [shape(mine.shape)], 1, collective_id, name, mine)[0]


def hist_peers(x, zl):
    steps = ((0, 1), (1, 0), (3, 0), (1, 1), (3, 1), (2, 0), (2, 1))
    return [((x + dx) % 4, (zl + dz) % 2) for dx, dz in steps]


def collect(history, small, large):
    slots, _, width = history.shape

    def kernel(hist, wa, wb, own_hist, full_a, full_b, send, recv, local):
        x, zl, zh, y, c = coords()
        place = x * 2 + zl
        partner = device(x, 1 - zl, zh, y, c)
        across = device(x, 1 - zl, 1 - zh, y, c)
        sibling = device(x, zl, zh, y, 1 - c)
        rows_of = [device(x, zl, zh, (y + k) % 4, c) for k in (1, 3, 2)]
        others = hist_peers(x, zl)
        hist_devices = [device(px, pz, zh, y, c) for px, pz in others]
        greet(hist_devices + [across, sibling] + rows_of)

        def view(ref, b_zl, b_zh, b_y, b_c):
            wide = ref.shape[2] // 2
            row = (b_zh * 8 + b_y * 2 + b_c) * BLOCK
            return ref.at[
                :, pl.ds(pl.multiple_of(row, BLOCK), BLOCK), pl.ds(pl.multiple_of(b_zl * wide, wide), wide)
            ]

        fulls = (full_a, full_b)
        z_of = [(zl, zh), (1 - zl, zh), (1 - zl, 1 - zh), (zl, 1 - zh)]
        base = 7 * slots

        def arrived(zi, k, sib=0):
            steps = (0, 1, 3, 2)
            by = (y + 4 - steps[k]) % 4
            bc = 1 - c if sib else c
            out = []
            for a, full in enumerate(fulls):
                ref = view(full, *z_of[zi], by, bc)
                out.append((ref, base + ((zi * 4 + k) * 2 + sib) * 2 + a))
            return out

        def wait_block(zi, k, sib=0):
            for ref, i in arrived(zi, k, sib):
                remote(ref, ref, send.at[i], recv.at[i], sibling).wait_recv()

        started = []

        def push(src, dst, i, peer):
            copy = remote(src, dst, send.at[i], recv.at[i], peer)
            copy.start()
            started.append(copy)

        own_blocks = [view(full, zl, zh, y, c) for full in fulls]
        for a, src in enumerate((wa, wb)):
            push(src, own_blocks[a], base + (1 * 4 * 2) * 2 + a, partner)
        for a, src in enumerate((wa, wb)):
            push(src, own_blocks[a], base + (2 * 4 * 2) * 2 + a, across)
        for j in range(slots):
            for k, (px, pz) in enumerate(others):
                rows = pl.ds(pl.multiple_of((px * 2 + pz) * BLOCK, BLOCK), BLOCK)
                push(hist.at[j, rows], own_hist.at[place, j], k * slots + j, hist_devices[k])
        locals_ = [
            pltpu.make_async_copy(
                hist.at[:, pl.ds(pl.multiple_of(place * BLOCK, BLOCK), BLOCK)], own_hist.at[place], local.at[0]
            ),
            pltpu.make_async_copy(wa, own_blocks[0], local.at[1]),
            pltpu.make_async_copy(wb, own_blocks[1], local.at[2]),
        ]
        for copy in locals_:
            copy.start()

        def spread(zi, sources):
            for a, src in enumerate(sources):
                dst = view(fulls[a], *z_of[zi], y, c)
                for k, peer in enumerate(rows_of):
                    push(src, dst, base + ((zi * 4 + k + 1) * 2) * 2 + a, peer)
                push(src, dst, base + ((zi * 4) * 2 + 1) * 2 + a, sibling)

        spread(0, (wa, wb))
        wait_block(1, 0)
        for a, (ref, _) in enumerate(arrived(1, 0)):
            push(ref, ref, base + (3 * 4 * 2) * 2 + a, across)
        spread(1, [ref for ref, _ in arrived(1, 0)])
        wait_block(2, 0)
        spread(2, [ref for ref, _ in arrived(2, 0)])
        wait_block(3, 0)
        spread(3, [ref for ref, _ in arrived(3, 0)])
        for zi in range(4):
            for k in range(1, 4):
                wait_block(zi, k)
                for a, (ref, _) in enumerate(arrived(zi, k)):
                    push(ref, ref, base + ((zi * 4 + k) * 2 + 1) * 2 + a, sibling)
        for zi in range(4):
            for k in range(4):
                wait_block(zi, k, 1)
        for k, (px, pz) in enumerate(others):
            for j in range(slots):
                i = k * slots + j
                ref = own_hist.at[px * 2 + pz, j]
                remote(ref, ref, send.at[i], recv.at[i], sibling).wait_recv()
        for copy in started:
            copy.wait_send()
        for copy in locals_:
            copy.wait()

    n_a, rows_a, cols_a = small.shape
    n_b, rows_b, cols_b = large.shape
    return comm_call(
        kernel,
        [
            shape((8, slots, BLOCK, width)),
            shape((n_a, rows_a * 16, cols_a * 2)),
            shape((n_b, rows_b * 16, cols_b * 2)),
        ],
        7 * slots + 64,
        1,
        "collect",
        history,
        small,
        large,
    )


def send_hist(array, dx, dz=0):
    pairs = [(h, (h // 2 + dx) % 4 * 2 + (h % 2 + dz) % 2) for h in range(8)]
    return lax.ppermute(array, "hist", pairs)


def send_tok(array, dzh=0, dy=0, dc=0):
    pairs = [
        (t, (t // 8 + dzh) % 2 * 8 + (t // 2 % 4 + dy) % 4 * 2 + (t % 2 + dc) % 2) for t in range(16)
    ]
    return lax.ppermute(array, "tok", pairs)


def dot_nt(left, right):
    return lax.dot_general(left, right, (((1,), (1,)), ((), ())), preferred_element_type=jnp.float32)


def dot_nn(left, right):
    return lax.dot_general(left, right, (((1,), (0,)), ((), ())), preferred_element_type=jnp.float32)


def dot_tn(left, right):
    return lax.dot_general(left, right, (((0,), (0,)), ((), ())), preferred_element_type=jnp.float32)


def attend(queries, keys, values, other_keys, other_values, query_at, key_at):
    rows, cols = queries.shape
    heads = cols // HD
    scale = HD ** (-0.5)
    tall = 256

    def kernel(q, k, v, ok, ov, qa, ka, out, lse):
        for r in range(rows // tall):
            at = pl.ds(r * tall, tall)
            query_pos, query_doc = qa[at, 0:1], qa[at, 1:2]
            scores = []
            for half, key in enumerate((k, ok)):
                allowed = (ka[2 * half : 2 * half + 1, :] <= query_pos) & (
                    ka[2 * half + 1 : 2 * half + 2, :] == query_doc
                )
                scores.append(jnp.where(allowed, dot_nt(q[at, :], key[...]) * scale, NEGATIVE))
            top = jnp.maximum(
                jnp.max(scores[0], axis=1, keepdims=True), jnp.max(scores[1], axis=1, keepdims=True)
            )
            shifted = [jnp.exp(part - top) for part in scores]
            total = jnp.sum(shifted[0], axis=1, keepdims=True) + jnp.sum(shifted[1], axis=1, keepdims=True)
            share = 1.0 / total
            result = dot_nn((shifted[0] * share).astype(BF16), v[...])
            result = result + dot_nn((shifted[1] * share).astype(BF16), ov[...])
            out[at, :] = result.astype(BF16)
            lse[0, at, :] = top + jnp.log(total)

    head = pl.BlockSpec((rows, HD), lambda h: (0, h))
    return pl.pallas_call(
        kernel,
        grid=(heads,),
        out_shape=[shape((rows, cols)), shape((heads, rows, 1), jnp.float32)],
        in_specs=[head] * 5
        + [pl.BlockSpec(query_at.shape, lambda h: (0, 0)), pl.BlockSpec(key_at.shape, lambda h: (0, 0))],
        out_specs=[head, pl.BlockSpec((1, rows, 1), lambda h: (h, 0, 0))],
        compiler_params=pltpu.CompilerParams(vmem_limit_bytes=40 * 2**20),
        name="attend",
    )(queries, keys, values, other_keys, other_values, query_at, key_at)


def attend_back(queries, keys, values, other_keys, other_values, query_at, key_at, log_totals, out_cot):
    rows, cols = queries.shape
    heads = cols // HD
    scale = HD ** (-0.5)
    tall = 256

    def kernel(q, k, v, ok, ov, qa, ka, lse, cot, dq, dk, dv, dok, dov, key_sum, value_sum):
        for r in range(rows // tall):
            at = pl.ds(r * tall, tall)
            query_pos, query_doc = qa[at, 0:1], qa[at, 1:2]
            probs, prob_grads = [], []
            for half, (key, value) in enumerate(((k, v), (ok, ov))):
                allowed = (ka[2 * half : 2 * half + 1, :] <= query_pos) & (
                    ka[2 * half + 1 : 2 * half + 2, :] == query_doc
                )
                scores = jnp.where(allowed, dot_nt(q[at, :], key[...]) * scale, NEGATIVE)
                probs.append(jnp.exp(scores - lse[0, at, :]))
                prob_grads.append(dot_nt(cot[at, :], value[...]))
            row_dot = sum(jnp.sum(p * g, axis=1, keepdims=True) for p, g in zip(probs, prob_grads))
            query_grad = jnp.zeros((tall, HD), jnp.float32)
            for half, (p, g) in enumerate(zip(probs, prob_grads)):
                score_cot = (p * (g - row_dot)).astype(BF16)
                key = (k, ok)[half]
                query_grad = query_grad + dot_nn(score_cot, key[...])
                key_part = dot_tn(score_cot, q[at, :])
                value_part = dot_tn(p.astype(BF16), cot[at, :])
                if r == 0:
                    key_sum[half] = key_part
                    value_sum[half] = value_part
                else:
                    key_sum[half] += key_part
                    value_sum[half] += value_part
            dq[at, :] = query_grad * scale
        dk[...] = key_sum[0] * scale
        dv[...] = value_sum[0]
        dok[...] = (key_sum[1] * scale).astype(BF16)
        dov[...] = value_sum[1].astype(BF16)

    head = pl.BlockSpec((rows, HD), lambda h: (0, h))
    return pl.pallas_call(
        kernel,
        grid=(heads,),
        out_shape=[shape((rows, cols), jnp.float32)] * 3 + [shape((rows, cols))] * 2,
        in_specs=[head] * 5
        + [pl.BlockSpec(query_at.shape, lambda h: (0, 0)), pl.BlockSpec(key_at.shape, lambda h: (0, 0))]
        + [pl.BlockSpec((1, rows, 1), lambda h: (h, 0, 0)), head],
        out_specs=[head] * 5,
        scratch_shapes=[pltpu.VMEM((2, rows, HD), jnp.float32)] * 2,
        compiler_params=pltpu.CompilerParams(vmem_limit_bytes=40 * 2**20),
        name="attend_back",
    )(queries, keys, values, other_keys, other_values, query_at, key_at, log_totals, out_cot)


def erf(value):
    value = jnp.clip(value, -4.0, 4.0)
    square = value * value
    top = jnp.full_like(value, -2.72614225801306e-10)
    for factor in (
        2.77068142495902e-08,
        -2.10102402082508e-06,
        -5.69250639462346e-05,
        -7.34990630326855e-04,
        -2.95459980854025e-03,
        -1.60960333262415e-02,
    ):
        top = top * square + factor
    bottom = jnp.full_like(value, -1.45660718464996e-05)
    for factor in (-2.13374055278905e-04, -1.68282697438203e-03, -7.37332916720468e-03, -1.42647390514189e-02):
        bottom = bottom * square + factor
    return value * top / bottom


def gelu_both(value):
    share = 0.5 * (1.0 + erf(value * 0.7071067811865476))
    bell = jnp.exp(-0.5 * value * value) * 0.3989422804014327
    return value * share, share + value * bell


def row_mean(value):
    return jnp.mean(value, axis=1, keepdims=True)


def middle(heads, small, large, stream, gains, da_in, da_out, da_bias, out_grad, mix_cot_in):
    rows_all, head_cols = heads.shape
    width, hidden = large.shape[1:]
    step = 16
    half = BLOCK // 2
    tile = 2 * BLOCK
    tiles = width // tile

    def kernel(
        heads, small, large, stream, gains, da_in, da_out, da_bias, out_grad, mix_cot_in,
        block_out, mix_next, residual_grad, heads_cot, gain_grads, side_sum, other, out_proj_grad, up_sum, down_sum,
        w_out, w_up, w_down, mid_all, active, slope, cot_all, up_cot, attn_cot,
        part, got1, got3, own, residual, unit, total, flat, aux, inv, grad_stage, sums,
        y_slots, z_part, z_slots, c_part, c_slot, x_slots, result,
        load, send, recv, gsend, grecv, gkeep, sends, recvs, dload,
    ):
        x, zl, zh, y, c = coords()
        z = zh * 2 + zl
        along_z, along_y = z_peers(x, zl, zh, y, c), y_peers(x, zl, zh, y, c)
        sibling = device(x, zl, zh, y, 1 - c)
        steps = (1, 3, 2)
        places = {k: (x + k) % 4 for k in steps}
        peers = {k: device(places[k], zl, zh, y, c) for k in steps}
        right, left, far = places[1], places[3], places[2]
        loads = [
            pltpu.make_async_copy(small.at[3], w_out, load.at[0]),
            pltpu.make_async_copy(large.at[0], w_up, load.at[1]),
            pltpu.make_async_copy(large.at[1], w_down, load.at[2]),
        ]
        for copy in loads:
            copy.start()
        greet([peers[k] for k in steps] + [peer for _, peer in along_z + along_y] + [sibling])

        def block(place):
            return pl.ds(pl.multiple_of(place * BLOCK, BLOCK), BLOCK)

        def chunks(work, place=0):
            def one(r, carry):
                begin = r * step
                work(
                    pl.ds(pl.multiple_of(begin, step), step),
                    pl.ds(pl.multiple_of(place * BLOCK + begin, step), step),
                )
                return carry

            lax.fori_loop(0, BLOCK // step, one, 0)

        sent = []
        given = ({}, {}, {})

        def arrived(stage, got):
            for k in steps:
                i = stage * 3 + k - 1
                remote(got.at[k - 1], got.at[k - 1], send.at[i], recv.at[i], sibling).wait_recv()

        def push(src, dst, i, peer):
            copy = remote(src, dst, send.at[i], recv.at[i], peer)
            copy.start()
            sent.append(copy)
            return copy

        def give_part(stage, k, got, product):
            if k == 0:
                own[...] = product
                return
            slot = stage % 2
            if stage == 2:
                given[0][k].wait_send()
            part[slot, k - 1] = product.astype(BF16)
            given[stage][k] = push(part.at[slot, k - 1], got.at[k - 1], stage * 3 + k - 1, peers[k])

        def spread(buf, base):
            def piece(place, top):
                begin = pl.multiple_of(place * BLOCK + (0 if top else half), half)
                return buf.at[pl.ds(begin, half)]

            first = [
                push(piece(x, True), piece(x, True), base, peers[1]),
                push(piece(x, False), piece(x, False), base + 2, peers[3]),
                push(piece(x, False), piece(x, False), base + 1, peers[1]),
                push(piece(x, True), piece(x, True), base + 3, peers[3]),
            ]

            def forward():
                first[0].wait_recv()
                one = push(piece(left, True), piece(left, True), base + 4, peers[1])
                first[1].wait_recv()
                two = push(piece(right, False), piece(right, False), base + 5, peers[3])
                return one, two

            return first, forward

        def gathered(buf, base, work):
            first, forward = spread(buf, base)
            work(0, x)
            one, two = forward()
            first[2].wait_recv()
            work(3, left)
            first[3].wait_recv()
            work(1, right)
            one.wait_recv()
            two.wait_recv()
            work(2, far)

        loads[0].wait()
        for k in (2, 1, 3, 0):
            place = x if k == 0 else places[k]
            give_part(0, k, got1, dot_nt(heads[block(place), :], w_out[...]))
        arrived(0, got1)

        def to_mid(at, there):
            value = stream[3, at, :] + own[at, :]
            for k in range(3):
                value = value + got1[k, at, :].astype(jnp.float32)
            residual[at, :] = value
            centered = value - row_mean(value)
            scale = lax.rsqrt(row_mean(centered * centered) + EPSILON)
            inv[at, :BLOCK] = jnp.broadcast_to(scale, (step, BLOCK))
            normed = centered * scale
            unit[at, :] = normed
            mid_all[there, :] = (normed * gains[3:4, :]).astype(BF16)

        chunks(to_mid, x)

        waited = []

        def feed(k, place):
            if not waited:
                loads[1].wait()
            total[...] = dot_nn(mid_all[block(place), :], w_up[...])

            def bend(at, there):
                value, change = gelu_both(total[at, :])
                active[there, :] = value.astype(BF16)
                slope[there, :] = change.astype(slope.dtype)

            chunks(bend, place)
            if not waited:
                loads[2].wait()
                waited.append(True)
            give_part(1, k, got3, dot_nt(active[block(place), :], w_down[...]))

        gathered(mid_all, 9, feed)
        arrived(1, got3)

        def to_out(at, _):
            value = residual[at, :] + own[at, :]
            for k in range(3):
                value = value + got3[k, at, :].astype(jnp.float32)
            block_out[at, :] = value.astype(BF16)
            scale = lax.rsqrt(row_mean(value * value) + EPSILON)
            inv[at, BLOCK:] = jnp.broadcast_to(scale, (step, BLOCK))
            residual[at, :] = value * scale
            flat[at, :] = (value * scale * gains[4:5, :]).astype(BF16)

        chunks(to_out)
        inner_act, inner_slope = gelu_both(dot_nn(flat[...], da_in[...]))
        inner_act = inner_act.astype(BF16)
        mix_next[...] = dot_nn(inner_act, da_out[...]) + da_bias[...]
        mix_cot = mix_cot_in[...].astype(BF16)
        inner_cot = (dot_nt(mix_cot, da_out[...]) * inner_slope).astype(BF16)
        aux[...] = dot_nt(inner_cot, da_in[...])
        sums[...] = jnp.zeros_like(sums)

        def to_cot(at, there):
            rms_unit = residual[at, :]
            grad = aux[at, :]
            product = grad * rms_unit
            sums[0] += product[:8] + product[8:]
            scaled = grad * gains[4:5, :]
            scale = inv[at, BLOCK : BLOCK + 1]
            value = out_grad[at, :].astype(jnp.float32) + scale * (
                scaled - rms_unit * row_mean(scaled * rms_unit)
            )
            residual[at, :] = value
            cot_all[there, :] = value.astype(BF16)

        chunks(to_cot, x)

        def small_grads():
            grad = dot_tn(flat[...], inner_cot)
            c_rows = SIDE_ROWS
            bias = jnp.sum(mix_cot_in[...], axis=0, keepdims=True)
            tail = jnp.concatenate(
                [
                    dot_tn(inner_act, mix_cot)[:104],
                    jnp.where(lax.broadcasted_iota(jnp.int32, (24, BLOCK), 0) == 0, bias, 0.0),
                ],
                axis=0,
            )
            whole = jnp.concatenate([grad, tail], axis=0)
            for py in range(4):
                for pz in range(4):
                    begin = (py * 4 + pz) * c_rows
                    result[py, pz] = whole[begin : begin + c_rows]

        side = {}

        def side_start():
            small_grads()
            side[0] = exchange(lambda py: result.at[py], y_slots, y, along_y, sends, recvs, 0)
            y_slots[y] = result[y]

        def side_z():
            for copy in side[0]:
                copy.wait()
            z_part[...] = y_slots[0] + y_slots[1] + y_slots[2] + y_slots[3]
            side[1] = exchange(lambda pz: z_part.at[pz], z_slots, z, along_z, sends, recvs, 3)
            z_slots[z] = z_part[z]

        def side_core():
            for copy in side[1]:
                copy.wait()
            c_part[...] = z_slots[0] + z_slots[1] + z_slots[2] + z_slots[3]
            side[2] = remote(c_part, c_slot, sends.at[6], recvs.at[6], sibling)
            side[2].start()

        def side_x():
            side[2].wait()
            x_slots[x] = c_part[...] + c_slot[...]
            along_x = [(places[k], peers[k]) for k in steps]
            side[3] = exchange(x_slots.at[x], x_slots, x, along_x, sends, recvs, 7)

        def side_up_z():
            for copy in side[3]:
                copy.wait()
            side_sum[y, z] = x_slots[0] + x_slots[1] + x_slots[2] + x_slots[3]
            side[4] = exchange(side_sum.at[y, z], side_sum.at[y], z, along_z, sends, recvs, 10)

        def side_up_y():
            for copy in side[4]:
                copy.wait()
            side[5] = exchange(side_sum.at[y], side_sum, y, along_y, sends, recvs, 13)

        def feed_back(k, place):
            total[...] = dot_nn(cot_all[block(place), :], w_down[...])

            def bend(at, there):
                up_cot[there, :] = (total[at, :] * slope[there, :].astype(jnp.float32)).astype(BF16)

            chunks(bend, place)
            give_part(2, k, got1, dot_nt(up_cot[block(place), :], w_up[...]))

        first, forward = spread(cot_all, 15)
        side_start()
        feed_back(0, x)
        one, two = forward()
        first[2].wait_recv()
        feed_back(3, left)
        first[3].wait_recv()
        feed_back(1, right)
        side_z()
        one.wait_recv()
        two.wait_recv()
        feed_back(2, far)
        side_core()

        def weight_grad(which, left_side, right_side):
            def copies(m):
                slot = lax.rem(m, 2)
                mine = grad_stage.at[slot, pl.ds(pl.multiple_of(c * BLOCK, BLOCK), BLOCK)]
                theirs = grad_stage.at[slot, pl.ds(pl.multiple_of((1 - c) * BLOCK, BLOCK), BLOCK)]
                i = which * tiles + m
                stays = (w_up, w_down)[which].at[pl.ds(pl.multiple_of(m * BLOCK, BLOCK), BLOCK)]
                return (
                    pltpu.make_async_copy(mine, stays, gkeep.at[slot]),
                    remote(theirs, other.at[which, m], gsend.at[i], grecv.at[i], sibling),
                )

            def finish(m):
                stay, go = copies(m)
                stay.wait()
                go.wait_send()

            def one(m, carry):
                @pl.when(m >= 2)
                def _():
                    finish(m - 2)

                cols = pl.ds(pl.multiple_of(m * tile, tile), tile)
                grad_stage[lax.rem(m, 2)] = dot_tn(left_side[:, cols], right_side[...]).astype(BF16)
                for copy in copies(m):
                    copy.start()
                return carry

            lax.fori_loop(0, tiles, one, 0)
            finish(tiles - 2)
            finish(tiles - 1)

        def other_came(which):
            def one(m, carry):
                i = which * tiles + m
                remote(other.at[which, m], other.at[which, m], gsend.at[i], grecv.at[i], sibling).wait_recv()
                return carry

            return one

        def fetch_other(which):
            lax.fori_loop(0, tiles, other_came(which), 0)
            for m in range(tiles):
                fetch(which, m).start()

        def fetch(which, m):
            there = (w_up, w_down)[which].at[pl.ds((tiles + m) * BLOCK, BLOCK)]
            return pltpu.make_async_copy(other.at[which, m], there, dload.at[which * tiles + m])

        def add_cores(which):
            whole = (w_up, w_down)[which]
            for m in range(tiles):
                fetch(which, m).wait()

            def one(r, carry):
                at = pl.ds(pl.multiple_of(r * step, step), step)
                there = pl.ds(pl.multiple_of(tiles * BLOCK + r * step, step), step)
                whole[at, :] = (whole[at, :].astype(jnp.float32) + whole[there, :].astype(jnp.float32)).astype(BF16)
                return carry

            lax.fori_loop(0, tiles * BLOCK // step, one, 0)
            done = pltpu.make_async_copy(
                whole.at[pl.ds(0, tiles * BLOCK)], (up_sum, down_sum)[which], gkeep.at[2 + which]
            )
            done.start()
            return done

        weight_grad(1, cot_all, active)
        side_x()
        arrived(2, got1)

        def to_residual(at, there):
            grad = own[at, :]
            for k in range(3):
                grad = grad + got1[k, at, :].astype(jnp.float32)
            mid_unit = unit[at, :]
            product = grad * mid_unit
            sums[1] += product[:8] + product[8:]
            scaled = grad * gains[3:4, :]
            scale = inv[at, 0:1]
            value = residual[at, :] + scale * (
                scaled - row_mean(scaled) - mid_unit * row_mean(scaled * mid_unit)
            )
            residual_grad[at, :] = value
            attn_cot[there, :] = value.astype(BF16)

        chunks(to_residual, x)
        first, forward = spread(attn_cot, 21)

        def head_back(place):
            heads_cot[block(place), :] = dot_nn(attn_cot[block(place), :], w_out[...]).astype(BF16)

        side_up_z()
        head_back(x)
        one, two = forward()
        fetch_other(1)
        weight_grad(0, mid_all, up_cot)
        side_up_y()
        down_done = add_cores(1)
        fetch_other(0)
        gain_grads[...] = jnp.sum(sums[...], axis=1)
        first[2].wait_recv()
        head_back(left)
        first[3].wait_recv()
        head_back(right)
        one.wait_recv()
        two.wait_recv()
        head_back(far)

        def out_grad_copy(m):
            rows = pl.ds(pl.multiple_of(m * tile, tile), tile)
            slot = lax.rem(m, 2)
            return pltpu.make_async_copy(
                grad_stage.at[slot, :, pl.ds(0, head_cols)], out_proj_grad.at[rows], gkeep.at[slot]
            )

        def out_grad_tile(m, carry):
            @pl.when(m >= 2)
            def _():
                out_grad_copy(m - 2).wait()

            cols = pl.ds(pl.multiple_of(m * tile, tile), tile)
            grad_stage[lax.rem(m, 2), :, :head_cols] = dot_tn(attn_cot[:, cols], heads[...]).astype(BF16)
            out_grad_copy(m).start()
            return carry

        lax.fori_loop(0, tiles, out_grad_tile, 0)
        out_grad_copy(tiles - 2).wait()
        out_grad_copy(tiles - 1).wait()
        for copy in side[5]:
            copy.wait()
        up_done = add_cores(0)
        down_done.wait()
        up_done.wait()
        for i, copy in enumerate(sent):
            if all(copy is not first for first in given[0].values()):
                copy.wait_send()

    f32 = jnp.float32
    vmem = pltpu.VMEM
    piece = (SIDE_ROWS, 128)
    return pl.pallas_call(
        kernel,
        out_shape=[
            shape((BLOCK, width)),
            shape((BLOCK, BLOCK), f32),
            shape((BLOCK, width), f32),
            shape(heads.shape),
            shape((2, width), f32),
            shape((4, 4) + piece, f32),
            shape((2, tiles, BLOCK, hidden)),
            shape((width, head_cols)),
            shape((tiles * BLOCK, hidden)),
            shape((tiles * BLOCK, hidden)),
        ],
        in_specs=[VMEM, ANY, ANY] + [VMEM] * 7,
        out_specs=[VMEM] * 6 + [ANY] * 4,
        scratch_shapes=[
            vmem((width, head_cols), BF16),
            vmem((width, hidden), BF16),
            vmem((width, hidden), BF16),
            vmem((rows_all, width), BF16),
            vmem((rows_all, hidden), BF16),
            vmem((rows_all, hidden), f32),
            vmem((rows_all, width), BF16),
            vmem((rows_all, hidden), BF16),
            vmem((rows_all, width), BF16),
            vmem((2, 3, BLOCK, width), BF16),
            vmem((3, BLOCK, width), BF16),
            vmem((3, BLOCK, width), BF16),
            vmem((BLOCK, width), f32),
            vmem((BLOCK, width), f32),
            vmem((BLOCK, width), f32),
            vmem((BLOCK, width), f32),
            vmem((BLOCK, width), BF16),
            vmem((BLOCK, width), f32),
            vmem((BLOCK, 2 * BLOCK), f32),
            vmem((2, tile, hidden), BF16),
            vmem((2, 8, width), f32),
            vmem((4, 4) + piece, f32),
            vmem((4,) + piece, f32),
            vmem((4,) + piece, f32),
            vmem(piece, f32),
            vmem(piece, f32),
            vmem((4,) + piece, f32),
            vmem((4, 4) + piece, f32),
            pltpu.SemaphoreType.DMA((3,)),
            pltpu.SemaphoreType.DMA((27,)),
            pltpu.SemaphoreType.DMA((27,)),
            pltpu.SemaphoreType.DMA((2 * tiles,)),
            pltpu.SemaphoreType.DMA((2 * tiles,)),
            pltpu.SemaphoreType.DMA((4,)),
            pltpu.SemaphoreType.DMA((16,)),
            pltpu.SemaphoreType.DMA((16,)),
            pltpu.SemaphoreType.DMA((2 * tiles,)),
        ],
        compiler_params=pltpu.CompilerParams(
            collective_id=4, has_side_effects=True, vmem_limit_bytes=62 * 2**20
        ),
        name="middle",
    )(heads, small, large, stream, gains, da_in, da_out, da_bias, out_grad, mix_cot_in)


def inward(grads, gives, small, normed, out_proj_grad, streams, residual_grad, gains, late_gains, tables, down):
    rows_all, cols = grads[0].shape
    width = streams.shape[2]
    step = 16
    half = BLOCK // 2
    tile = 2 * BLOCK
    tiles = width // tile
    hidden = down.shape[3]

    def kernel(
        dq, dk, dv, give_k, give_v, small, normed, out_proj_grad, streams, residual_grad, gains, late, tables,
        down,
        stream_cot, gain_grads, small_sum, down_sum,
        weights, inputs, cots, got_k, got_v, far_part, near, hop, got, own, grad, swapped, sums, down_y,
        load, send, recv, ssend, srecv, gsend, grecv, local,
    ):
        x, zl, zh, y, c = coords()
        z = zh * 2 + zl
        along_y = y_peers(x, zl, zh, y, c)
        partner = device(x, 1 - zl, zh, y, c)
        sibling = device(x, zl, zh, y, 1 - c)
        places = {k: (x + k) % 4 for k in (1, 2, 3)}
        peers = {k: device(places[k], zl, zh, y, c) for k in (1, 3)}
        loads = [pltpu.make_async_copy(small.at[i], weights.at[i], load.at[i]) for i in range(3)]
        loads += [pltpu.make_async_copy(normed.at[i], inputs.at[i], load.at[3 + i]) for i in range(3)]
        loads.append(pltpu.make_async_copy(out_proj_grad, grad.at[3], load.at[6]))
        for copy in loads:
            copy.start()
        greet([peers[1], peers[3], partner, sibling] + [peer for _, peer in along_y])
        sides = []

        def side(src, dst, peer):
            i = len(sides)
            sides.append(remote(src, dst, ssend.at[i], srecv.at[i], peer))
            sides[-1].start()

        side(give_k, got_k, partner)
        side(give_v, got_v, partner)
        for py, peer in along_y:
            side(down.at[:, py], down_y.at[y], peer)
        locals_ = [pltpu.make_async_copy(down.at[:, y], down_y.at[y], local.at[0])]
        for copy in locals_:
            copy.start()

        def block(place):
            return pl.ds(pl.multiple_of(place * BLOCK, BLOCK), BLOCK)

        def turn_back(value):
            def one(at):
                part = value(at)
                ahead, behind = pltpu.roll(part, HD - ROT // 2, 1), pltpu.roll(part, ROT // 2, 1)
                return part * tables[0, at, :] - ahead * tables[1, at, :] - behind * tables[2, at, :]

            return one

        def to_cots(i, value):
            def one(r, carry):
                at = pl.ds(pl.multiple_of(r * step, step), step)
                for h in range(cols // HD):
                    head = slice(h * HD, (h + 1) * HD)
                    cots[i, at, head] = value(at, head).astype(BF16)
                return carry

            lax.fori_loop(0, rows_all // step, one, 0)

        def turned(value):
            return lambda at, head: turn_back(lambda at: value(at, head))(at)

        started = []

        def push(src, dst, i, peer):
            started.append(remote(src, dst, send.at[i], recv.at[i], peer))
            started[-1].start()

        def far_sums(i):
            if i == 0:
                loads[0].wait()
            else:
                loads[i].wait()
            far_part[i] = dot_nt(cots[i, block(places[2]), :], weights[i]).astype(BF16)
            push(far_part.at[i, pl.ds(0, half)], hop.at[i, 0], i * 4, peers[1])
            push(far_part.at[i, pl.ds(half, half)], hop.at[i, 1], i * 4 + 1, peers[3])

        def near_sums(i):
            for k, side_of in ((1, 0), (3, 1)):
                product = dot_nt(cots[i, block(places[k]), :], weights[i])
                begin = side_of * half
                j = i * 4 + side_of
                remote(hop.at[i, side_of], hop.at[i, side_of], send.at[j], recv.at[j], sibling).wait_recv()
                near[i, side_of] = product.astype(BF16)
                merged = product[begin : begin + half] + hop[i, side_of].astype(jnp.float32)
                near[i, side_of, begin : begin + half] = merged.astype(BF16)
                push(near.at[i, side_of], got.at[i, side_of], i * 4 + 2 + side_of, peers[k])

        def own_sums(i):
            own[i] = dot_nt(cots[i, block(x), :], weights[i])

        swaps = []

        def weight_grad(i):
            if i < 3:
                loads[3 + i].wait()

                def one(m, carry):
                    at = pl.ds(pl.multiple_of(m * tile, tile), tile)
                    grad[i, at, :] = dot_tn(inputs[i, :, at], cots[i]).astype(BF16)
                    return carry

                lax.fori_loop(0, tiles, one, 0)
            else:
                loads[6].wait()
            for m in range(tiles):
                begin = pl.multiple_of(m * tile + (1 - c) * BLOCK, BLOCK)
                j = i * tiles + m
                swaps.append(
                    remote(grad.at[i, pl.ds(begin, BLOCK)], swapped.at[i, m], gsend.at[j], grecv.at[j], sibling)
                )
                swaps[-1].start()

        def add_cores(i):
            for m in range(tiles):
                swaps_of[i][m].wait()

            def one(r, carry):
                m, part = r // (BLOCK // step), lax.rem(r, BLOCK // step)
                at = pl.ds(pl.multiple_of(m * tile + c * BLOCK + part * step, step), step)
                there = pl.ds(pl.multiple_of(part * step, step), step)
                value = grad[i, at, :].astype(jnp.float32) + swapped[i, m, there, :].astype(jnp.float32)
                swapped[i, m, there, :] = value.astype(BF16)
                return carry

            lax.fori_loop(0, tiles * BLOCK // step, one, 0)
            locals_.append(pltpu.make_async_copy(swapped.at[i], small_sum.at[:, i], local.at[1 + i]))
            locals_[-1].start()

        swaps_of = {}

        def grads_of(i):
            begin = len(swaps)
            weight_grad(i)
            swaps_of[i] = swaps[begin:]

        to_cots(0, turned(lambda at, head: dq[at, head]))
        far_sums(0)
        near_sums(0)
        grads_of(3)
        grads_of(0)
        own_sums(0)
        sides[0].wait_recv()
        to_cots(1, turned(lambda at, head: dk[at, head] + got_k[at, head].astype(jnp.float32)))
        far_sums(1)
        sides[1].wait_recv()
        to_cots(2, lambda at, head: dv[at, head] + got_v[at, head].astype(jnp.float32))
        far_sums(2)
        near_sums(1)
        near_sums(2)
        grads_of(1)
        grads_of(2)
        own_sums(1)
        own_sums(2)
        for i in (3, 0, 1, 2):
            add_cores(i)
        sums[...] = jnp.zeros_like(sums)
        for i in range(3):
            for side_of in range(2):
                j = i * 4 + 2 + side_of
                remote(got.at[i, side_of], got.at[i, side_of], send.at[j], recv.at[j], sibling).wait_recv()

            def back(r, carry, i=i):
                at = pl.ds(pl.multiple_of(r * step, step), step)
                value = streams[i, at, :]
                centered = value - row_mean(value)
                scale = lax.rsqrt(row_mean(centered * centered) + EPSILON)
                unit = centered * scale
                above = own[i, at, :] + got[i, 0, at, :].astype(jnp.float32) + got[i, 1, at, :].astype(jnp.float32)
                product = above * unit
                sums[i] += product[:8] + product[8:]
                scaled = above * gains[i : i + 1, :]
                result = scale * (scaled - row_mean(scaled) - unit * row_mean(scaled * unit))
                stream_cot[i, at, :] = result.astype(BF16)
                return carry

            lax.fori_loop(0, BLOCK // step, back, 0)
        stream_cot[3] = residual_grad[...].astype(BF16)
        gain_grads[...] = jnp.zeros_like(gain_grads)
        for i in range(3):
            gain_grads[i : i + 1, :] = jnp.sum(sums[i], axis=0, keepdims=True)
        gain_grads[3:4, :] = late[1:2, :]
        gain_grads[4:5, :] = late[0:1, :]
        for copy in sides[2:] + locals_[:1]:
            copy.wait()
        for high in range(2):

            def add_y(r, carry, high=high):
                at = pl.ds(pl.multiple_of(r * step, step), step)
                value = down_y[0, high, at, :].astype(jnp.float32)
                for src in range(1, 4):
                    value = value + down_y[src, high, at, :].astype(jnp.float32)
                down_sum[high, at, :] = value.astype(BF16)
                return carry

            lax.fori_loop(0, BLOCK // step, add_y, 0)
        for copy in started + sides[:2]:
            copy.wait_send()
        for copy in locals_[1:]:
            copy.wait()

    f32 = jnp.float32
    vmem = pltpu.VMEM
    sem = pltpu.SemaphoreType.DMA
    return pl.pallas_call(
        kernel,
        out_shape=[
            shape((4, BLOCK, width)),
            shape((8, width), f32),
            shape((tiles, 4, BLOCK, cols)),
            shape((2, BLOCK, hidden)),
        ],
        in_specs=[VMEM] * 5 + [ANY] * 3 + [VMEM] * 5 + [ANY],
        out_specs=[VMEM, VMEM, ANY, VMEM],
        scratch_shapes=[
            vmem((3, width, cols), BF16),
            vmem((3, rows_all, width), BF16),
            vmem((3, rows_all, cols), BF16),
            vmem((rows_all, cols), BF16),
            vmem((rows_all, cols), BF16),
            vmem((3, BLOCK, width), BF16),
            vmem((3, 2, BLOCK, width), BF16),
            vmem((3, 2, half, width), BF16),
            vmem((3, 2, BLOCK, width), BF16),
            vmem((3, BLOCK, width), f32),
            vmem((4, width, cols), BF16),
            vmem((4, tiles, BLOCK, cols), BF16),
            vmem((3, 8, width), f32),
            vmem((4, 2, BLOCK, hidden), BF16),
            sem((7,)),
            sem((12,)),
            sem((12,)),
            sem((8,)),
            sem((8,)),
            sem((4 * tiles,)),
            sem((4 * tiles,)),
            sem((5,)),
        ],
        compiler_params=pltpu.CompilerParams(
            collective_id=5, has_side_effects=True, vmem_limit_bytes=60 * 2**20
        ),
        name="inward",
    )(
        *grads, *gives, small, normed, out_proj_grad, streams, residual_grad, gains, late_gains, tables, down
    )


def hand_out(own_hist, weights, stream_cot, gains, small, up, down):
    groups, n, rows, width = own_hist.shape
    cols = small.shape[3]
    thin = cols // 2
    hidden = up.shape[2] // 2
    step = 16
    lanes = 128

    def kernel(
        hist, w, cot, gains, small, up, down,
        out, omg, gains_out, small_out, up_out, down_out,
        held, stage, mixes, turned, x_slots, z_slots, y_slots, c_part, c_slot,
        small_y, small_part, small_z, up_y, up_part, up_z, down_z,
        load, send, recv, msend, mrecv, local, sends, recvs, ssend, srecv,
    ):
        x, zl, zh, y, c = coords()
        z = zh * 2 + zl
        place = x * 2 + zl
        others = hist_peers(x, zl)
        peers = [device(px, pz, zh, y, c) for px, pz in others]
        holders = [px * 2 + pz for px, pz in others] + [place]
        loads = []
        for k, holder in enumerate(holders):
            for j in range(n):
                i = k * n + j
                loads.append(pltpu.make_async_copy(hist.at[holder, j], held.at[k, j], load.at[i]))
        for j in range(n):
            for copy in loads[j::n]:
                copy.start()
        along_x, along_z = x_peers(x, zl, zh, y, c), z_peers(x, zl, zh, y, c)
        along_y = y_peers(x, zl, zh, y, c)
        sibling = device(x, zl, zh, y, 1 - c)
        others_z = [device(x, 1 - zl, 1 - zh, y, c), device(x, zl, 1 - zh, y, c)]
        greet(peers + others_z + [peer for _, peer in along_y] + [sibling])
        sides = []

        def side(src, dst, peer):
            i = len(sides)
            sides.append(remote(src, dst, ssend.at[i], srecv.at[i], peer))
            sides[-1].start()

        first = exchange(gains, x_slots, x, along_x, sends, recvs, 0)
        x_slots[x] = gains[...]
        for py, peer in along_y:
            for high in range(2):
                side(small.at[high * 4 + py], small_y.at[y, high], peer)
        for py, peer in along_y:
            for high in range(2):
                side(up.at[high * 4 + py], up_y.at[y, high], peer)
        for pz, peer in along_z:
            high, low = pz // 2, pz % 2
            side(down.at[high, :, pl.ds(pl.multiple_of(low * hidden, hidden), hidden)], down_z.at[z], peer)
        own_rows = pl.ds(pl.multiple_of(place * rows, rows), rows)
        locals_ = [
            pltpu.make_async_copy(small.at[y], small_y.at[y, 0], local.at[0]),
            pltpu.make_async_copy(small.at[4 + y], small_y.at[y, 1], local.at[1]),
            pltpu.make_async_copy(
                down.at[zh, :, pl.ds(pl.multiple_of(zl * hidden, hidden), hidden)], down_z.at[z], local.at[2]
            ),
            pltpu.make_async_copy(up.at[y], up_y.at[y, 0], local.at[3]),
            pltpu.make_async_copy(up.at[4 + y], up_y.at[y, 1], local.at[4]),
        ]
        for copy in locals_:
            copy.start()
        copies = []
        lane = lax.broadcasted_iota(jnp.int32, (step, lanes), 1)

        def entry_grads(k, j):
            holder = holders[k]
            loads[k * n + j].wait()

            def some_rows(r, carry):
                at = pl.ds(pl.multiple_of(r * step, step), step)
                factors = w[holder, j, at, :]
                factors = [jnp.broadcast_to(factors[:, s : s + 1], (step, lanes)) for s in range(4)]
                totals = [jnp.zeros((step, lanes), jnp.float32) for _ in range(4)]
                for block in range(width // lanes):
                    part = pl.ds(block * lanes, lanes)
                    entry = held[k, j, at, part].astype(jnp.float32)
                    mixed = jnp.zeros((step, lanes), jnp.float32)
                    for s in range(4):
                        piece = cot[s, at, part].astype(jnp.float32)
                        mixed = mixed + factors[s] * piece
                        totals[s] = totals[s] + entry * piece
                    stage[k, j, at, part] = mixed.astype(BF16)
                packed = jnp.zeros((step, lanes), jnp.float32)
                for s in range(4):
                    packed = jnp.where(lane == s, jnp.sum(totals[s], axis=1, keepdims=True), packed)
                mixes[at, :] = packed
                return carry

            lax.fori_loop(0, rows // step, some_rows, 0)
            turned[k, j] = jnp.transpose(mixes[...])[:8]
            if k < 7:
                i = k * n + j
                copies.append(remote(stage.at[k, j], out.at[j, own_rows], send.at[i], recv.at[i], peers[k]))
                copies[-1].start()
                if j == n - 1:
                    copies.append(remote(turned.at[k], omg.at[place], msend.at[k], mrecv.at[k], peers[k]))
                    copies[-1].start()

        for k in range(7):
            entry_grads(k, 0)
        for copy in first:
            copy.wait()
        z_slots[z] = x_slots[0] + x_slots[1] + x_slots[2] + x_slots[3]
        second = exchange(z_slots.at[z], z_slots, z, along_z, sends, recvs, 3)
        for j in range(1, n):
            for k in range(7):
                entry_grads(k, j)
        for j in range(n):
            entry_grads(7, j)
            locals_.append(pltpu.make_async_copy(stage.at[7, j], out.at[j, own_rows], local.at[5 + j]))
            locals_[-1].start()
        locals_.append(pltpu.make_async_copy(turned.at[7], omg.at[place], local.at[5 + n]))
        locals_[-1].start()
        for copy in second:
            copy.wait()
        y_slots[y] = z_slots[0] + z_slots[1] + z_slots[2] + z_slots[3]
        third = exchange(y_slots.at[y], y_slots, y, along_y, sends, recvs, 6)
        for copy in third:
            copy.wait()
        c_part[...] = y_slots[0] + y_slots[1] + y_slots[2] + y_slots[3]
        fourth = remote(c_part, c_slot, sends.at[9], recvs.at[9], sibling)
        fourth.start()
        fourth.wait()
        gains_out[...] = c_part[...] + c_slot[...]

        def add_four(parts, places, dst):
            def one(r, carry):
                at = pl.ds(pl.multiple_of(r * step, step), step)
                value = parts[(0,) + places + (at,)].astype(jnp.float32)
                for src in range(1, 4):
                    value = value + parts[(src,) + places + (at,)].astype(jnp.float32)
                dst[places + (at,)] = value.astype(dst.dtype)
                return carry

            lax.fori_loop(0, rows // step, one, 0)

        def to_z(parts, slots, wide, first_sem):
            cut = [slice(None)] * (len(parts.shape) - 2)

            def piece(high, low):
                return parts.at[tuple([high] + cut + [pl.ds(pl.multiple_of(low * wide, wide), wide)])]

            out_copies = []
            for k, (pz, peer) in enumerate(along_z):
                i = first_sem + k
                out_copies.append(remote(piece(pz // 2, pz % 2), slots.at[z], ssend.at[i], srecv.at[i], peer))
            out_copies.append(pltpu.make_async_copy(piece(zh, zl), slots.at[z], local.at[6 + n + first_sem // 18]))
            for copy in out_copies:
                copy.start()
            return out_copies

        for copy in sides[:6] + locals_[:2]:
            copy.wait()
        for high in range(2):
            for i in range(4):
                add_four(small_y, (high, i), small_part)
        small_last = to_z(small_part, small_z, thin, 15)
        for copy in sides[6:12] + locals_[3:5]:
            copy.wait()
        for high in range(2):
            add_four(up_y, (high,), up_part)
        up_last = to_z(up_part, up_z, hidden, 18)
        for copy in sides[12:] + locals_[2:3]:
            copy.wait()
        add_four(down_z, (), down_out)
        for copy in small_last:
            copy.wait()
        for i in range(4):
            add_four(small_z, (i,), small_out)
        for copy in up_last:
            copy.wait()
        add_four(up_z, (), up_out)
        for copy in copies + locals_[5:]:
            copy.wait()

    f32 = jnp.float32
    vmem = pltpu.VMEM
    sem = pltpu.SemaphoreType.DMA
    return pl.pallas_call(
        kernel,
        out_shape=[
            shape((n, groups * rows, width)),
            shape((groups, n, 8, lanes), f32),
            shape(gains.shape, f32),
            shape((4, BLOCK, thin), f32),
            shape((BLOCK, hidden), f32),
            shape((BLOCK, hidden), f32),
        ],
        in_specs=[ANY, VMEM, VMEM, VMEM, ANY, ANY, ANY],
        out_specs=[ANY, ANY, VMEM, VMEM, VMEM, VMEM],
        scratch_shapes=[
            vmem((groups, n, rows, width), BF16),
            vmem((groups, n, rows, width), BF16),
            vmem((rows, lanes), f32),
            vmem((groups, n, 8, lanes), f32),
            vmem((4,) + gains.shape, f32),
            vmem((4,) + gains.shape, f32),
            vmem((4,) + gains.shape, f32),
            vmem(gains.shape, f32),
            vmem(gains.shape, f32),
            vmem((4, 2, 4, BLOCK, cols), BF16),
            vmem((2, 4, BLOCK, cols), BF16),
            vmem((4, 4, BLOCK, thin), BF16),
            vmem((4, 2, BLOCK, 2 * hidden), BF16),
            vmem((2, BLOCK, 2 * hidden), BF16),
            vmem((4, BLOCK, hidden), BF16),
            vmem((4, BLOCK, hidden), BF16),
            sem((groups * n,)),
            sem((7 * n,)),
            sem((7 * n,)),
            sem((7,)),
            sem((7,)),
            sem((n + 8,)),
            sem((10,)),
            sem((10,)),
            sem((21,)),
            sem((21,)),
        ],
        compiler_params=pltpu.CompilerParams(
            collective_id=6, has_side_effects=True, vmem_limit_bytes=56 * 2**20
        ),
        name="hand_out",
    )(own_hist, weights, stream_cot, gains, small, up, down)


def body(
    history,
    layer_ids,
    mix_weights,
    doc_ids,
    gains,
    w_qkv,
    w_out,
    w_up,
    w_down,
    da_in,
    da_out,
    da_bias,
    out_grad,
    mix_grad_in,
):
    place = lax.axis_index("hist")
    low_z = place % 2
    slots, seq_len, width = history.shape
    small = jnp.concatenate([jnp.transpose(w_qkv, (1, 0, 2)), w_out[None]], axis=0)
    large = jnp.stack([w_up, w_down], axis=0)
    own_hist, full_small, full_large = collect(history, small, large)
    w_q, w_k, w_v, full_out = (full_small[i] for i in range(4))
    full_up, full_down = full_large[0], full_large[1]
    flat_hist = own_hist.reshape(8 * slots, BLOCK, width)

    own_mix = lax.dynamic_slice_in_dim(mix_weights, place * BLOCK, BLOCK, 2)
    pick = (layer_ids[:, None] == jnp.arange(own_mix.shape[1], dtype=jnp.int32)[None, :]).astype(jnp.float32)
    slot_weights = jnp.einsum("jl,slt->sjt", pick, own_mix, precision=HIGHEST)
    owned = jnp.zeros((4, BLOCK, width), jnp.float32)
    for j in range(8 * slots):
        owned = owned + slot_weights[:, j, :, None] * flat_hist[j][None].astype(jnp.float32)

    norm_unit, inv_std = norm_rows(owned[:3])
    normed = (norm_unit * gains[:3, None, :]).astype(BF16)
    gathered = gather_x(normed, 2, "gather_normed").reshape(3, 4 * BLOCK, width)
    rows_here = 4 * BLOCK
    heads_cols = full_out.shape[1]
    cosine, sine_table = rotary_tables(seq_len, ROT)

    def here(table, side=low_z):
        return lax.dynamic_index_in_dim(table.reshape(4, 2, BLOCK, -1), side, 1, False).reshape(rows_here, -1)

    cos_here, sin_here = here(cosine), here(sine_table)
    nothing = jnp.zeros_like(sin_here)
    rest = jnp.zeros((rows_here, HD - ROT), jnp.float32)
    tables = [
        jnp.tile(jnp.concatenate(parts, axis=1), (1, heads_cols // HD))
        for parts in ((cos_here, cos_here, rest + 1.0), (-sin_here, nothing, rest), (nothing, sin_here, rest))
    ]

    def turn(values, direction):
        ahead, behind = jnp.roll(values, -ROT // 2, axis=1), jnp.roll(values, ROT // 2, axis=1)
        return values * tables[0] + direction * (ahead * tables[1] + behind * tables[2])

    def project(which, weight):
        return jnp.dot(gathered[which], weight, preferred_element_type=jnp.float32)

    keys = turn(project(1, w_k), 1.0).astype(BF16)
    values = project(2, w_v).astype(BF16)
    other_keys, other_values = send_hist(keys, 0, 1), send_hist(values, 0, 1)
    queries = turn(project(0, w_q), 1.0).astype(BF16)
    places = jnp.stack([jnp.arange(seq_len, dtype=jnp.int32), doc_ids], axis=1)
    query_at, other_at = here(places), here(places, 1 - low_z)
    key_at = jnp.concatenate([query_at.T, other_at.T], axis=0)
    attention = (queries, keys, values, other_keys, other_values, query_at, key_at)
    heads_flat, log_totals = attend(*attention)

    mixers = da_out.shape[0]
    spare = BLOCK - mixers
    (
        block_out,
        mix_next,
        residual_grad,
        heads_cot,
        late_gains,
        side,
        _,
        out_proj_grad,
        up_sum,
        down_sum,
    ) = middle(
        heads_flat,
        full_small,
        full_large,
        owned,
        gains,
        jnp.pad(da_in, ((0, 0), (0, spare))),
        jnp.pad(da_out, ((0, spare), (0, spare))),
        jnp.pad(da_bias, (0, spare))[None],
        out_grad,
        jnp.pad(mix_grad_in, ((0, 0), (0, spare))),
    )
    side = side.reshape(16 * SIDE_ROWS, BLOCK)[:, :mixers]
    da_in_sum, da_out_sum, bias_sum = side[:width], side[width : width + mixers], side[width + 104]

    *grads, key_give, value_give = attend_back(*attention, log_totals, heads_cot)
    stream_cot, gains_local, small_sum, down_sum = inward(
        grads,
        (key_give, value_give),
        full_small,
        gathered,
        out_proj_grad,
        owned,
        residual_grad,
        gains,
        late_gains,
        jnp.stack([table[:, :HD] for table in tables]),
        down_sum.reshape(2, 4, BLOCK, -1),
    )
    columns = jnp.transpose(slot_weights.reshape(4, 8, slots, BLOCK), (1, 2, 3, 0))
    history_grad, mix_out, gains_sum, small_sum, up_sum, down_sum = hand_out(
        own_hist, columns, stream_cot, gains_local, small_sum, up_sum.reshape(8, BLOCK, -1), down_sum
    )
    mix_grad = jnp.transpose(mix_out[:, :, :4], (2, 1, 0, 3)).reshape(4, slots, seq_len)
    return (
        block_out,
        mix_next[:, :mixers],
        history_grad,
        mix_grad,
        gains_sum[: gains.shape[0]],
        jnp.transpose(small_sum[:3], (1, 0, 2)),
        small_sum[3],
        up_sum,
        down_sum,
        da_in_sum,
        da_out_sum,
        bias_sum,
    )


def solution(mesh):
    return jax.shard_map(
        body,
        mesh=mesh,
        in_specs=(
            P("hist", "tok", None),
            P(),
            P(None, None, "tok"),
            P("tok"),
            P(),
            P("tok", None, "hist"),
            P("tok", "hist"),
            P("tok", "hist"),
            P("tok", "hist"),
            P(),
            P(),
            P(),
            P(("tok", "hist"), None),
            P(("tok", "hist"), None),
        ),
        out_specs=(
            P(("tok", "hist"), None),
            P(("tok", "hist"), None),
            P("hist", "tok", None),
            P(None, "hist", "tok"),
            P(),
            P("tok", None, "hist"),
            P("tok", "hist"),
            P("tok", "hist"),
            P("tok", "hist"),
            P(),
            P(),
            P(),
        ),
        check_vma=False,
    )
```

time: 1170 us -> 783 us (0.67)
  other arithmetic: 151 us -> 24.6 us
  matrix products: 134 us -> 11 us
  waiting for transfers between devices: 57 us -> 0.01 us
  local copies, waits for them, and re-layouts: 102 us -> 61.5 us
  Pallas kernels: 701 us -> 675 us
  between operations: 17 us -> 1.41 us
    pallas_call x14 -> x1, Pallas kernels: 701 us -> 165 us  [comm_call(): pl.pallas_call(kernel, out_shape=out_shapes, in_specs=[ANY] * len(args),...]
    pallas_call x0 -> x6, Pallas kernels: none -> 510 us  [the longest x1 182 us: hand_out(): pl.pallas_call(kernel, out_shape=[shape((n, groups * rows, width)), shape...]
    dot_general x29 -> x3, matrix products: 125 us -> 10.1 us  [project(): return jnp.dot(gathered[which], weight, preferred_element_type=jnp.float32)]
    reduce_sum x16 -> x0, other arithmetic: 57.5 us -> none  [the longest x2 20.1 us: body(): jnp.sum(slot_weights[:, j, :, None] * stream_wide, axis=0).astype(BF16)]
    psum x2 -> x0, waiting for transfers between devices: 57 us -> none  [the longest x1 57 us: body(): lax.psum((da_in_grad, da_out_grad, bias_grad), ('hist', 'tok'))]
    convert_element_type x5 -> x1, other arithmetic: 27.5 us -> 2.58 us  [body(): keys = turn(project(1, w_k), 1.0).astype(BF16)]
    another operation x9 -> x3, other arithmetic: 22.3 us -> 1.01 us  [the longest x1 0.96 us: body(): jnp.stack([table[:, :HD] for table in tables])]
    another operation x10 -> x5, local copies, waits for them, and re-layouts: 19.1 us -> 1.65 us  [the longest x2 1.1 us: body(): jnp.stack([table[:, :HD] for table in tables])]
  transfers between devices with their start and end apart: 2 -> 2, of which waited for: 1 -> 0; matrix products, arithmetic and copies ran while one was open for 11% -> 4% of each run, Pallas kernels for 20% -> 0%
where the time goes in v2:
time: 783 us; the launch traced here: 776 us
  Pallas kernels  675 us (86%)
  local copies, waits for them, and re-layouts  61.5 us (8%)
  other arithmetic  24.6 us (3%)
  matrix products  11 us (1%)
    pallas_call x1, Pallas kernels, hand_out(): pl.pallas_call(kernel, out_shape=[shape((n, groups * rows, width)), shape...  182 us
    pallas_call x1, Pallas kernels, middle(): pl.pallas_call(kernel, out_shape=[shape((BLOCK, width)), shape((BLOCK, BL...  169 us
    pallas_call x1, Pallas kernels, comm_call(): pl.pallas_call(kernel, out_shape=out_shapes, in_specs=[ANY] * len(args),...  165 us
    pallas_call x1, Pallas kernels, gather_x(): pl.pallas_call(kernel, out_shape=outs, in_specs=in_specs, out_specs=out_s...  74.7 us
    pallas_call x1, Pallas kernels, inward(): pl.pallas_call(kernel, out_shape=[shape((4, BLOCK, width)), shape((8, wid...  66.7 us
    unnamed x86, local copies, waits for them, and re-layouts  36.9 us
  transfers between devices with their start and end apart: 2, of which 0 were waited for; matrix products, arithmetic and copies ran while one was open for 4% of the time, Pallas kernels for 0%

profile of v2, /device:TPU:1, one launch (start us, length us, event | category | flops | bytes accessed | tf_op | source)
XLA Modules:
  0.0 775.6 jit_solution(15681063142230058308)
XLA Ops:
  2.6 1.7 pad_maximum_fusion.2.wa
  4.3 1.9 pad_maximum_fusion.1.wb
  6.1 164.8 %collect.1 = (bf16[8,3,128,2048]{3,2,1,0:T(8,128)(2,1)}, bf16[4,2048,512]{2,1,0:T(8,128)(2,1)}, bf16[2,2048,2048]{2,1,0:T(8,128)(2,1)}) custom-call(bf16[3,1024,2048]{2,1,0:T(8,128)(2,1)} %hist.1, bf16[4,128,256]{2,1,0:T(8,128)(2,1)} %pad_maximum_fusion.2.wa, bf16[2,128,1024]{2,1,0:T(8,128)(2,1)} %pad_maximum_fusion.1.wb), custom_call_target="tpu_custom_call" | custom-call | tf_op jit(solution)/shard_map/collect/pallas_call | solution.py:106
  170.9 2.4 fusion.40
  173.3 5.4 fusion.41
  178.7 7.6 multiply_add_fusion.stream.streams
  188.3 74.7 %gather_normed.1 = bf16[3,4,128,2048]{3,2,1,0:T(8,128)(2,1)S(1)} custom-call(bf16[3,128,2048]{2,1,0:T(8,128)(2,1)S(1)} %multiply_convert_fusion.refs_0_), custom_call_target="tpu_custom_call" | custom-call | tf_op jit(solution)/shard_map/gather_normed/pallas_call | solution.py:233
  263.0 3.5 fusion.52
  267.2 2.8 fusion.9.v
  271.0 3.5 fusion.2
  274.5 3.8 fusion.4
  279.6 2.7 fusion.54
  285.3 2.6 fusion.17
  289.6 2.3 copy.89
  291.9 2.3 copy.90
  296.9 2.0 copy.54
  299.5 1.9 pad.16.da_in
  303.5 6.6 attend.1
  312.8 169.4 %middle.1 = (bf16[128,2048]{1,0:T(8,128)(2,1)}, f32[128,128]{1,0:T(8,128)}, f32[128,2048]{1,0:T(8,128)}, bf16[512,512]{1,0:T(8,128)(2,1)}, f32[2,2048]{1,0:T(2,1...) custom-call(bf16[512,512]{1,0:T(8,128)(2,1)} %copy-done.14, ...), custom_call_target="tpu_custom_call" | custom-call | tf_op jit(solution)/shard_map/middle/pallas_call | solution.py:947
  490.5 10.7 %attend_back.1 = (f32[512,512]{1,0:T(8,128)S(1)}, f32[512,512]{1,0:T(8,128)S(1)}, f32[512,512]{1,0:T(8,128)S(1)}, bf16[512,512]{1,0:T(8,128)(2,1)S(1)}, bf16[512,512]{1,0:T(8,128)(2,1)S(1)}) custom-call(bf16[512,512]{1,0:T(8,128)(2,1)S(1)} %get-tuple-element.124.q, bf16[512,512]{1,0:T(8,128)(2,1)S(1)} %get-tuple-element.123.k, ...), custom_call_target="tpu_custom_call" | custom-call | tf_op jit(solution)/shard_map/attend_back/pallas_call | solution.py:506
  505.7 66.7 %inward.1 = (bf16[4,128,2048]{2,1,0:T(8,128)(2,1)}, f32[8,2048]{1,0:T(8,128)}, bf16[8,4,128,512]{3,2,1,0:T(8,128)(2,1)}, bf16[2,128,2048]{2,1,0:T(8,128)(2,1)}) custom-call(f32[512,512]{1,0:T(8,128)} %copy-done.9, f32[512,512]{1,0:T(8,128)} %copy-done.10, f32[512,512]{1,0:T(8,128)} %copy-done.11, bf16[512,512]{1,0:T(8,128)(2,1)} %copy-done.12, ...), custom_call_target="tpu_custom_call" | custom-call | tf_op jit(solution)/shard_map/inward/pallas_call | solution.py:1219
  572.4 182.2 %hand_out.1 = (bf16[3,1024,2048]{2,1,0:T(8,128)(2,1)}, f32[8,3,8,128]{3,2,1,0:T(8,128)}, f32[8,2048]{1,0:T(8,128)}, f32[4,128,256]{2,1,0:T(8,128)}, f32[128,1024]{1,0:T(8,128)}, /*index=5*/f32[128,1024]{1,0:T(8,128)}) custom-call(bf16[8,3,128,2048]{3,2,1,0:T(8,128)(2,1)} %get-tuple-element.41.hist, f32[8,3,128,4]{3,2,1,0:T(8,128)} %bitcast.257, ...), custom_call_target="tpu_custom_call" | custom-call | tf_op jit(solution)/shard_map/hand_out/pallas_call | solution.py:1443
  756.1 1.8 slice_bitcast_fusion.24
  762.2 10.8 %copy.100 = bf16[3,1024,2048]{2,1,0:T(8,128)(2,1)} copy(bf16[3,1024,2048]{2,1,0:T(8,128)(2,1)} %get-tuple-element.183) | data formatting | bytes 25165824
  (128 shorter events, 40.1 us)
Async XLA Ops:
  263.0 4.2 copy-start.2
  270.0 33.5 %collective-permute-start.1 = (bf16[512,512]{1,0:T(8,128)(2,1)S(1)}, bf16[512,512]{1,0:T(8,128)(2,1)S(1)}, u32[]{:S(2)}, u32[]{:S(2)}) collective-permute-start(bf16[512,512]{1,0:T(8,128)(2,1)S(1)} %fusion.9.v), channel_id=1, source_target_pairs={{0,16},{16,0},{32,48},{48,32},{64,80},{80,64},{96,112},{112,96},{1... | collective-permute-start | bytes 1572872 | tf_op jit(solution)/shard_map/ppermute | solution.py:405
  274.5 5.1 copy-start.17
  278.3 3.9 copy-start.19
  282.4 2.2 copy-start.18
  282.4 2.2 copy-start.20
  282.4 2.2 copy-start.23
  282.4 2.2 copy-start.24
  282.4 2.5 copy-start.25
  282.4 2.9 copy-start.26
  284.2 3.7 copy-start.21
  284.6 3.3 copy-start.22
  285.3 3.8 copy-start.35
  287.9 15.6 %collective-permute-start = (bf16[512,512]{1,0:T(8,128)(2,1)S(1)}, bf16[512,512]{1,0:T(8,128)(2,1)S(1)}, u32[]{:S(2)}, u32[]{:S(2)}) collective-permute-start(bf16[512,512]{1,0:T(8,128)(2,1)S(1)} %get-tuple-element.123.k), channel_id=1, source_target_pairs={{0,16},{16,0},{32,48},{48,32},{64,80},{80,64},{96,112},{112,96},{1... | collective-permute-start | bytes 1572872 | tf_op jit(solution)/shard_map/ppermute | solution.py:405
  289.0 6.9 copy-start.34
  289.0 7.0 copy-start.32
  289.1 9.8 %copy-start.33 = (bf16[100,100]{1,0:T(8,128)(2,1)S(1)}, bf16[100,100]{1,0:T(8,128)(2,1)}, u32[]{:S(2)}) copy-start(bf16[100,100]{1,0:T(8,128)(2,1)} %param.24) | copy-start | bytes 60004
  303.5 6.7 copy-start.5
  572.4 185.5 %copy-start.30 = (f32[128,128]{1,0:T(8,128)S(1)}, f32[128,128]{1,0:T(8,128)}, u32[]{:S(2)}) copy-start(f32[128,128]{1,0:T(8,128)} %get-tuple-element.46) | copy-start | bytes 196612
  572.4 189.0 %copy-start.27 = (bf16[128,2048]{1,0:T(8,128)(2,1)S(1)}, bf16[128,2048]{1,0:T(8,128)(2,1)}, u32[]{:S(2)}) copy-start(bf16[128,2048]{1,0:T(8,128)(2,1)} %get-tuple-element.181) | copy-start | bytes 1572868
  762.2 10.9 %copy-start.31 = (f32[8,2048]{1,0:T(8,128)S(1)}, f32[8,2048]{1,0:T(8,128)}, u32[]{:S(2)}) copy-start(f32[8,2048]{1,0:T(8,128)} %get-tuple-element.65) | copy-start | bytes 196612
  762.2 11.5 %copy-start.29 = (f32[128,1024]{1,0:T(8,128)S(1)}, f32[128,1024]{1,0:T(8,128)}, u32[]{:S(2)}) copy-start(f32[128,1024]{1,0:T(8,128)} %get-tuple-element.188) | copy-start | bytes 1572868
  762.2 12.3 %copy-start.28 = (f32[128,1024]{1,0:T(8,128)S(1)}, f32[128,1024]{1,0:T(8,128)}, u32[]{:S(2)}) copy-start(f32[128,1024]{1,0:T(8,128)} %get-tuple-element.189) | copy-start | bytes 1572868
  762.2 13.1 %copy-start.1 = (f32[4,24,1024]{2,1,0:T(8,128)S(1)}, f32[4,24,1024]{2,1,0:T(8,128)}, u32[]{:S(2)}) copy-start(f32[4,24,1024]{2,1,0:T(8,128)} %param.16) | copy-start | bytes 1179652
  (15 other events, 15.2 us)

commit v3 on v2

--- a/solution.py
+++ b/solution.py
@@ -148,268 +148,260 @@
     return copies
 
 
-def gather_x(shard, collective_id, name, down=None, up=None):
-    n, rows, width = shard.shape
-    side = 0 if down is None and up is None else 1
-
-    def kernel(*refs):
-        src, dst = refs[0], refs[1 + side]
-        send, recv, local, sends, recvs = refs[2 + 2 * side : 7 + 2 * side]
-        x, zl, zh, y, c = coords()
-        z = zh * 2 + zl
-        peers = x_peers(x, zl, zh, y, c)
-        along_z = z_peers(x, zl, zh, y, c)
-        along_y = y_peers(x, zl, zh, y, c)
-        sibling = device(x, zl, zh, y, 1 - c)
-        greeted = [peer for _, peer in peers]
-        if side:
-            greeted = greeted + [peer for _, peer in along_z + along_y]
-        if down is not None:
-            greeted = greeted + [sibling]
-        greet(greeted)
-        copies = []
-        if down is not None:
-            given, result = refs[1], refs[3]
-            y_slots, z_part, z_slots, c_part, c_slot = refs[9:]
-            first = exchange(lambda py: given.at[py], y_slots, y, along_y, sends, recvs, 0)
-        if up is not None:
-            given, result = refs[1], refs[3]
-            x_slots, total = refs[9:]
-            first = exchange(given, x_slots, x, peers, sends, recvs, 0)
-        for j in range(n):
-            for k, (_, peer) in enumerate(peers):
-                i = j * 3 + k
-                copies.append(remote(src.at[j], dst.at[j, x], send.at[i], recv.at[i], peer))
-                copies[-1].start()
-        own = pltpu.make_async_copy(src, dst.at[:, x], local.at[0])
-        own.start()
-        if down is not None:
-            y_slots[y] = given[y]
-            for copy in first:
-                copy.wait()
-            z_part[...] = y_slots[0] + y_slots[1] + y_slots[2] + y_slots[3]
-            second = exchange(lambda pz: z_part.at[pz], z_slots, z, along_z, sends, recvs, 3)
-            z_slots[z] = z_part[z]
-            for copy in second:
-                copy.wait()
-            c_part[...] = z_slots[0] + z_slots[1] + z_slots[2] + z_slots[3]
-            third = remote(c_part, c_slot, sends.at[6], recvs.at[6], sibling)
-            third.start()
-            third.wait()
-            result[...] = c_part[...] + c_slot[...]
-        if up is not None:
-            x_slots[x] = given[...]
-            for copy in first:
-                copy.wait()
-            total[y, z] = x_slots[0] + x_slots[1] + x_slots[2] + x_slots[3]
-            second = exchange(total.at[y, z], total.at[y], z, along_z, sends, recvs, 3)
-            for copy in second:
-                copy.wait()
-            third = exchange(total.at[y], total, y, along_y, sends, recvs, 6)
-            for copy in third:
-                copy.wait()
-            result[...] = total[...]
-        own.wait()
-        for copy in copies:
-            copy.wait()
-
-    in_specs, args = [ANY], [shard]
-    out_specs, outs = [ANY], [shape((n, 4, rows, width))]
-    scratch = [
-        pltpu.SemaphoreType.DMA((3 * n,)),
-        pltpu.SemaphoreType.DMA((3 * n,)),
-        pltpu.SemaphoreType.DMA((4,)),
-        pltpu.SemaphoreType.DMA((9,)),
-        pltpu.SemaphoreType.DMA((9,)),
-    ]
-    if side:
-        in_specs, out_specs = [ANY, VMEM], [ANY, VMEM]
-        args = [shard, down if up is None else up]
-        piece = (SIDE_ROWS, 128)
-        whole = (4, 4) + piece
-        outs = outs + [shape(piece if up is None else whole, jnp.float32)]
-        dims = (whole, (4,) + piece, (4,) + piece, piece, piece) if up is None else ((4,) + piece, whole)
-        scratch = scratch + [pltpu.VMEM(d, jnp.float32) for d in dims]
-    result = pl.pallas_call(
-        kernel,
-        out_shape=outs,
-        in_specs=in_specs,
-        out_specs=out_specs,
-        scratch_shapes=scratch,
-        compiler_params=pltpu.CompilerParams(
-            collective_id=collective_id, has_side_effects=True, vmem_limit_bytes=24 * 2**20
-        ),
-        name=name,
-    )(*args)
-    return result if side else result[0]
-
-
-def scatter_x(parts, collective_id, name):
-    n, _, rows, width = parts.shape
-
-    def kernel(src, dst, send, recv, local):
-        x, zl, zh, y, c = coords()
-        peers = x_peers(x, zl, zh, y, c)
-        greet([peer for _, peer in peers])
-        copies = []
-        for j in range(n):
-            for k, (px, peer) in enumerate(peers):
-                i = j * 3 + k
-                copies.append(remote(src.at[j, px], dst.at[j, x], send.at[i], recv.at[i], peer))
-                copies[-1].start()
-        own = pltpu.make_async_copy(src.at[:, x], dst.at[:, x], local.at[0])
-        own.start()
-        own.wait()
-        for copy in copies:
-            copy.wait()
-
-    return comm_call(kernel, [shape(parts.shape)], 3 * n, collective_id, name, parts)[0]
-
-
-def swap_z(mine, collective_id, name):
-    def kernel(src, dst, send, recv, local):
-        x, zl, zh, y, c = coords()
-        peer = device(x, 1 - zl, zh, y, c)
-        greet([peer])
-        copy = remote(src, dst, send.at[0], recv.at[0], peer)
-        copy.start()
-        copy.wait()
-
-    return comm_call(kernel, [shape(mine.shape)], 1, collective_id, name, mine)[0]
-
-
-def hist_peers(x, zl):
-    steps = ((0, 1), (1, 0), (3, 0), (1, 1), (3, 1), (2, 0), (2, 1))
-    return [((x + dx) % 4, (zl + dz) % 2) for dx, dz in steps]
-
-
-def collect(history, small, large):
-    slots, _, width = history.shape
-
-    def kernel(hist, wa, wb, own_hist, full_a, full_b, send, recv, local):
-        x, zl, zh, y, c = coords()
-        place = x * 2 + zl
-        partner = device(x, 1 - zl, zh, y, c)
-        across = device(x, 1 - zl, 1 - zh, y, c)
-        sibling = device(x, zl, zh, y, 1 - c)
-        rows_of = [device(x, zl, zh, (y + k) % 4, c) for k in (1, 3, 2)]
-        others = hist_peers(x, zl)
-        hist_devices = [device(px, pz, zh, y, c) for px, pz in others]
-        greet(hist_devices + [across, sibling] + rows_of)
-
-        def view(ref, b_zl, b_zh, b_y, b_c):
-            wide = ref.shape[2] // 2
-            row = (b_zh * 8 + b_y * 2 + b_c) * BLOCK
-            return ref.at[
-                :, pl.ds(pl.multiple_of(row, BLOCK), BLOCK), pl.ds(pl.multiple_of(b_zl * wide, wide), wide)
-            ]
-
-        fulls = (full_a, full_b)
-        z_of = [(zl, zh), (1 - zl, zh), (1 - zl, 1 - zh), (zl, 1 - zh)]
-        base = 7 * slots
-
-        def arrived(zi, k, sib=0):
-            steps = (0, 1, 3, 2)
-            by = (y + 4 - steps[k]) % 4
-            bc = 1 - c if sib else c
-            out = []
-            for a, full in enumerate(fulls):
-                ref = view(full, *z_of[zi], by, bc)
-                out.append((ref, base + ((zi * 4 + k) * 2 + sib) * 2 + a))
-            return out
-
-        def wait_block(zi, k, sib=0):
-            for ref, i in arrived(zi, k, sib):
-                remote(ref, ref, send.at[i], recv.at[i], sibling).wait_recv()
-
-        started = []
-
-        def push(src, dst, i, peer):
-            copy = remote(src, dst, send.at[i], recv.at[i], peer)
+def weight_gather(srcs, fulls, place, send, recv, base):
+    x, zl, zh, y, c = place
+    partner = device(x, 1 - zl, zh, y, c)
+    across = device(x, 1 - zl, 1 - zh, y, c)
+    sibling = device(x, zl, zh, y, 1 - c)
+    rows_of = [device(x, zl, zh, (y + k) % 4, c) for k in (1, 3, 2)]
+    z_of = [(zl, zh), (1 - zl, zh), (1 - zl, 1 - zh), (zl, 1 - zh)]
+    many = len(srcs)
+    started = []
+
+    def view(ref, b_zl, b_zh, b_y, b_c):
+        wide = ref.shape[2] // 2
+        row = (b_zh * 8 + b_y * 2 + b_c) * BLOCK
+        return ref.at[
+            :, pl.ds(pl.multiple_of(row, BLOCK), BLOCK), pl.ds(pl.multiple_of(b_zl * wide, wide), wide)
+        ]
+
+    def sem(zi, k, sib, a):
+        return base + ((zi * 4 + k) * 2 + sib) * many + a
+
+    def refs(zi, k, sib=0):
+        by = (y + 4 - (0, 1, 3, 2)[k]) % 4
+        return [view(full, *z_of[zi], by, 1 - c if sib else c) for full in fulls]
+
+    def push(src, dst, i, peer):
+        started.append(remote(src, dst, send.at[i], recv.at[i], peer))
+        started[-1].start()
+
+    def wait_block(zi, k, sib=0):
+        for a, ref in enumerate(refs(zi, k, sib)):
+            i = sem(zi, k, sib, a)
+            remote(ref, ref, send.at[i], recv.at[i], sibling).wait_recv()
+
+    def spread(zi, blocks):
+        for a, src in enumerate(blocks):
+            dst = view(fulls[a], *z_of[zi], y, c)
+            for k, peer in enumerate(rows_of):
+                push(src, dst, sem(zi, k + 1, 0, a), peer)
+            push(src, dst, sem(zi, 0, 1, a), sibling)
+
+    own = [view(full, zl, zh, y, c) for full in fulls]
+
+    def start(local, first):
+        for a, src in enumerate(srcs):
+            push(src, own[a], sem(1, 0, 0, a), partner)
+        for a, src in enumerate(srcs):
+            push(src, own[a], sem(2, 0, 0, a), across)
+        kept = [pltpu.make_async_copy(src, own[a], local.at[first + a]) for a, src in enumerate(srcs)]
+        for copy in kept:
             copy.start()
-            started.append(copy)
-
-        own_blocks = [view(full, zl, zh, y, c) for full in fulls]
-        for a, src in enumerate((wa, wb)):
-            push(src, own_blocks[a], base + (1 * 4 * 2) * 2 + a, partner)
-        for a, src in enumerate((wa, wb)):
-            push(src, own_blocks[a], base + (2 * 4 * 2) * 2 + a, across)
-        for j in range(slots):
-            for k, (px, pz) in enumerate(others):
-                rows = pl.ds(pl.multiple_of((px * 2 + pz) * BLOCK, BLOCK), BLOCK)
-                push(hist.at[j, rows], own_hist.at[place, j], k * slots + j, hist_devices[k])
-        locals_ = [
-            pltpu.make_async_copy(
-                hist.at[:, pl.ds(pl.multiple_of(place * BLOCK, BLOCK), BLOCK)], own_hist.at[place], local.at[0]
-            ),
-            pltpu.make_async_copy(wa, own_blocks[0], local.at[1]),
-            pltpu.make_async_copy(wb, own_blocks[1], local.at[2]),
-        ]
-        for copy in locals_:
-            copy.start()
-
-        def spread(zi, sources):
-            for a, src in enumerate(sources):
-                dst = view(fulls[a], *z_of[zi], y, c)
-                for k, peer in enumerate(rows_of):
-                    push(src, dst, base + ((zi * 4 + k + 1) * 2) * 2 + a, peer)
-                push(src, dst, base + ((zi * 4) * 2 + 1) * 2 + a, sibling)
-
-        spread(0, (wa, wb))
+        spread(0, srcs)
+        return kept
+
+    def relay_z():
         wait_block(1, 0)
-        for a, (ref, _) in enumerate(arrived(1, 0)):
-            push(ref, ref, base + (3 * 4 * 2) * 2 + a, across)
-        spread(1, [ref for ref, _ in arrived(1, 0)])
+        for a, ref in enumerate(refs(1, 0)):
+            push(ref, ref, sem(3, 0, 0, a), across)
+        spread(1, refs(1, 0))
         wait_block(2, 0)
-        spread(2, [ref for ref, _ in arrived(2, 0)])
+        spread(2, refs(2, 0))
         wait_block(3, 0)
-        spread(3, [ref for ref, _ in arrived(3, 0)])
-        for zi in range(4):
-            for k in range(1, 4):
-                wait_block(zi, k)
-                for a, (ref, _) in enumerate(arrived(zi, k)):
-                    push(ref, ref, base + ((zi * 4 + k) * 2 + 1) * 2 + a, sibling)
+        spread(3, refs(3, 0))
+
+    def relay_y(zi):
+        for k in range(1, 4):
+            wait_block(zi, k)
+            for a, ref in enumerate(refs(zi, k)):
+                push(ref, ref, sem(zi, k, 1, a), sibling)
+
+    def finish():
         for zi in range(4):
             for k in range(4):
                 wait_block(zi, k, 1)
-        for k, (px, pz) in enumerate(others):
-            for j in range(slots):
-                i = k * slots + j
-                ref = own_hist.at[px * 2 + pz, j]
-                remote(ref, ref, send.at[i], recv.at[i], sibling).wait_recv()
         for copy in started:
             copy.wait_send()
-        for copy in locals_:
+
+    greeted = [partner, across, sibling] + rows_of
+    return greeted, start, relay_z, relay_y, finish
+
+
+def collect(history, small, up, top_weights, bottom_weights):
+    slots, _, width = history.shape
+    half = BLOCK // 2
+    step = 16
+    lanes = 128
+
+    def kernel(
+        hist, wa, wb, tw, bw, streams, top_out, bottom_out, full_a, full_b,
+        top, bottom, acc, part_x, got_x, part_z, got_z,
+        wsend, wrecv, send, recv, local, store,
+    ):
+        here = coords()
+        x, zl, zh, y, c = here
+        partner = device(x, 1 - zl, zh, y, c)
+        peers = {k: device((x + k) % 4, zl, zh, y, c) for k in (1, 2, 3)}
+        greeted, start, relay_z, relay_y, finish = weight_gather((wa, wb), (full_a, full_b), here, wsend, wrecv, 0)
+        greet(greeted + [peers[1], peers[2], peers[3]])
+
+        def rows(k, other, low):
+            begin = ((x + k) % 4 * 2 + (1 - zl if other else zl)) * BLOCK + low * half
+            return hist.at[:, pl.ds(pl.multiple_of(begin, half), half)]
+
+        copies = []
+
+        def push(src, dst, i, peer):
+            copies.append(remote(src, dst, send.at[i], recv.at[i], peer))
+            copies[-1].start()
+
+        def came(ref, i):
+            remote(ref, ref, send.at[i], recv.at[i], partner).wait_recv()
+
+        own = []
+        for other in range(2):
+            own.append(pltpu.make_async_copy(rows(0, other, 0), top.at[other, 0], local.at[other]))
+        for k in range(4):
+            own.append(pltpu.make_async_copy(rows(k, 0, 1), bottom.at[k, 0], local.at[2 + k]))
+        for copy in own:
+            copy.start()
+        kept = start(local, 6)
+        for k in (2, 1, 3, 0):
+            push(rows(k, 1, 1), bottom.at[k, 1], k, partner)
+        for other in (1, 0):
+            for k in (1, 3, 2):
+                push(rows(k, other, 0), top.at[other, 4 - k], 4 + 3 * other + 3 - k, peers[k])
+
+        def mix(entries, factors_of, groups, into, offset):
+            def some_rows(r, carry):
+                at = pl.ds(pl.multiple_of(r * step, step), step)
+                there = pl.ds(pl.multiple_of(offset + r * step, step), step)
+                for g in range(groups):
+                    factors = [
+                        [jnp.broadcast_to(factors_of(g * 3 + e, at)[:, s : s + 1], (step, lanes)) for s in range(4)]
+                        for e in range(3)
+                    ]
+
+                    def some_cols(b, inner, g=g, factors=factors):
+                        cols = pl.ds(pl.multiple_of(b * lanes, lanes), lanes)
+                        entry = [entries(g, e)[at, cols].astype(jnp.float32) for e in range(3)]
+                        for s in range(4):
+                            value = factors[0][s] * entry[0] + factors[1][s] * entry[1] + factors[2][s] * entry[2]
+                            into[s, there, cols] = value if g == 0 else into[s, there, cols] + value
+                        return inner
+
+                    lax.fori_loop(0, width // lanes, some_cols, 0, unroll=4)
+                return carry
+
+            lax.fori_loop(0, half // step, some_rows, 0)
+
+        def mix_top(other, into, offset):
+            mix(lambda g, e: top.at[other, g, e], lambda i, at: tw[other, i, at, :], 4, into, offset)
+
+        def mix_bottom(k, into, offset):
+            mix(lambda g, e: bottom.at[k, g, e], lambda i, at: bw[k, i, at, :], 2, into, offset)
+
+        stores = []
+
+        def keep(src, dst):
+            stores.append(pltpu.make_async_copy(src, dst, store.at[len(stores)]))
+            stores[-1].start()
+
+        def bottom_sums(k):
+            came(bottom.at[k, 1], k)
+            own[2 + k].wait()
+            keep(bottom.at[k], bottom_out.at[k])
+            if k == 0:
+                mix_bottom(0, streams, half)
+                return
+            mix_bottom(k, acc, 0)
+            part_x[k - 1] = acc[...].astype(BF16)
+            push(part_x.at[k - 1], got_x.at[3 - k], 10 + 3 - k, peers[k])
+
+        relay_z()
+        bottom_sums(2)
+        own[1].wait()
+        for k in (1, 2, 3):
+            came(top.at[1, k], 4 + 3 + k - 1)
+        keep(top.at[1], top_out.at[1])
+        mix_top(1, acc, 0)
+        part_z[...] = acc[...].astype(BF16)
+        push(part_z, got_z, 13, partner)
+        bottom_sums(1)
+        relay_y(0)
+        bottom_sums(3)
+        own[0].wait()
+        for k in (1, 2, 3):
+            came(top.at[0, k], 4 + k - 1)
+        keep(top.at[0], top_out.at[0])
+        mix_top(0, streams, 0)
+        relay_y(1)
+        bottom_sums(0)
+        relay_y(2)
+        relay_y(3)
+        came(got_z, 13)
+
+        def add(r, carry, offset, parts):
+            at = pl.ds(pl.multiple_of(r * step, step), step)
+            there = pl.ds(pl.multiple_of(offset + r * step, step), step)
+            for s in range(4):
+                value = streams[s, there, :]
+                for part in parts:
+                    value = value + part(s, at)
+                streams[s, there, :] = value
+            return carry
+
+        def add_all(offset, parts):
+            lax.fori_loop(0, half // step, lambda r, carry: add(r, carry, offset, parts), 0)
+
+        add_all(0, [lambda s, at: got_z[s, at, :].astype(jnp.float32)])
+        for k in (1, 2, 3):
+            came(got_x.at[k - 1], 10 + k - 1)
+        add_all(half, [lambda s, at, k=k: got_x[k, s, at, :].astype(jnp.float32) for k in range(3)])
+        finish()
+        for copy in kept + stores:
             copy.wait()
+        for copy in copies:
+            copy.wait_send()
 
     n_a, rows_a, cols_a = small.shape
-    n_b, rows_b, cols_b = large.shape
-    return comm_call(
+    n_b, rows_b, cols_b = up.shape
+    vmem = pltpu.VMEM
+    sem = pltpu.SemaphoreType.DMA
+    top_shape, bottom_shape = (2, 4, slots, half, width), (4, 2, slots, half, width)
+    piece = (4, half, width)
+    return pl.pallas_call(
         kernel,
-        [
-            shape((8, slots, BLOCK, width)),
+        out_shape=[
+            shape((4, BLOCK, width), jnp.float32),
+            shape(top_shape),
+            shape(bottom_shape),
             shape((n_a, rows_a * 16, cols_a * 2)),
             shape((n_b, rows_b * 16, cols_b * 2)),
         ],
-        7 * slots + 64,
-        1,
-        "collect",
-        history,
-        small,
-        large,
-    )
-
-
-def send_hist(array, dx, dz=0):
-    pairs = [(h, (h // 2 + dx) % 4 * 2 + (h % 2 + dz) % 2) for h in range(8)]
-    return lax.ppermute(array, "hist", pairs)
-
-
-def send_tok(array, dzh=0, dy=0, dc=0):
-    pairs = [
-        (t, (t // 8 + dzh) % 2 * 8 + (t // 2 % 4 + dy) % 4 * 2 + (t % 2 + dc) % 2) for t in range(16)
-    ]
-    return lax.ppermute(array, "tok", pairs)
+        in_specs=[ANY, ANY, ANY, VMEM, VMEM],
+        out_specs=[VMEM, ANY, ANY, ANY, ANY],
+        scratch_shapes=[
+            vmem(top_shape, BF16),
+            vmem(bottom_shape, BF16),
+            vmem(piece, jnp.float32),
+            vmem((3,) + piece, BF16),
+            vmem((3,) + piece, BF16),
+            vmem(piece, BF16),
+            vmem(piece, BF16),
+            sem((64,)),
+            sem((64,)),
+            sem((14,)),
+            sem((14,)),
+            sem((8,)),
+            sem((6,)),
+        ],
+        compiler_params=pltpu.CompilerParams(
+            collective_id=1, has_side_effects=True, vmem_limit_bytes=48 * 2**20
+        ),
+        name="collect",
+    )(history, small, up, top_weights, bottom_weights)
 
 
 def dot_nt(left, right):
@@ -546,16 +538,16 @@
     return jnp.mean(value, axis=1, keepdims=True)
 
 
-def middle(heads, small, large, stream, gains, da_in, da_out, da_bias, out_grad, mix_cot_in):
+def middle(heads, small, up, down, stream, gains, da_in, da_out, da_bias, out_grad, mix_cot_in):
     rows_all, head_cols = heads.shape
-    width, hidden = large.shape[1:]
+    width, hidden = up.shape[1:]
     step = 16
     half = BLOCK // 2
     tile = 2 * BLOCK
     tiles = width // tile
 
     def kernel(
-        heads, small, large, stream, gains, da_in, da_out, da_bias, out_grad, mix_cot_in,
+        heads, small, up, down, stream, gains, da_in, da_out, da_bias, out_grad, mix_cot_in,
         block_out, mix_next, residual_grad, heads_cot, gain_grads, side_sum, other, out_proj_grad, up_sum, down_sum,
         w_out, w_up, w_down, mid_all, active, slope, cot_all, up_cot, attn_cot,
         part, got1, got3, own, residual, unit, total, flat, aux, inv, grad_stage, sums,
@@ -572,8 +564,8 @@
         right, left, far = places[1], places[3], places[2]
         loads = [
             pltpu.make_async_copy(small.at[3], w_out, load.at[0]),
-            pltpu.make_async_copy(large.at[0], w_up, load.at[1]),
-            pltpu.make_async_copy(large.at[1], w_down, load.at[2]),
+            pltpu.make_async_copy(up.at[0], w_up, load.at[1]),
+            pltpu.make_async_copy(down.at[0], w_down, load.at[2]),
         ]
         for copy in loads:
             copy.start()
@@ -958,7 +950,7 @@
             shape((tiles * BLOCK, hidden)),
             shape((tiles * BLOCK, hidden)),
         ],
-        in_specs=[VMEM, ANY, ANY] + [VMEM] * 7,
+        in_specs=[VMEM, ANY, ANY, ANY] + [VMEM] * 7,
         out_specs=[VMEM] * 6 + [ANY] * 4,
         scratch_shapes=[
             vmem((width, head_cols), BF16),
@@ -1003,7 +995,141 @@
             collective_id=4, has_side_effects=True, vmem_limit_bytes=62 * 2**20
         ),
         name="middle",
-    )(heads, small, large, stream, gains, da_in, da_out, da_bias, out_grad, mix_cot_in)
+    )(heads, small, up, down, stream, gains, da_in, da_out, da_bias, out_grad, mix_cot_in)
+
+
+def project(streams, gains, small, tables, down):
+    width = streams.shape[2]
+    cols = small.shape[2]
+    rows_all = 4 * BLOCK
+    step = 16
+    half = BLOCK // 2
+    order = (1, 2, 0)
+
+    def kernel(
+        streams, gains, small, tables, down,
+        queries, keys, values, other_keys, other_values, normed_out, full_down,
+        weights, normed, load, send, recv, zsend, zrecv, local, wsend, wrecv,
+    ):
+        x, zl, zh, y, c = coords()
+        partner = device(x, 1 - zl, zh, y, c)
+        places = {k: (x + k) % 4 for k in (1, 2, 3)}
+        right, left, far = places[1], places[3], places[2]
+        peers = {k: device(places[k], zl, zh, y, c) for k in (1, 3)}
+        loads = [pltpu.make_async_copy(small.at[i], weights.at[i], load.at[i]) for i in range(3)]
+        for i in order:
+            loads[i].start()
+        greeted, start, relay_z, relay_y, finish = weight_gather(
+            (down,), (full_down,), (x, zl, zh, y, c), wsend, wrecv, 0
+        )
+        greet(greeted + [peers[1], peers[3]])
+        kept = start(local, 3)
+
+        def block(place):
+            return pl.ds(pl.multiple_of(place * BLOCK, BLOCK), BLOCK)
+
+        def piece(i, place, top):
+            begin = pl.multiple_of(place * BLOCK + (0 if top else half), half)
+            return normed.at[i, pl.ds(begin, half)]
+
+        copies = {}
+
+        def push(i, number, place, top, peer):
+            part = piece(i, place, top)
+            j = i * 6 + number
+            copies[i, number] = remote(part, part, send.at[j], recv.at[j], peer)
+            copies[i, number].start()
+
+        for i in order:
+
+            def norm(r, carry, i=i):
+                at = pl.ds(pl.multiple_of(r * step, step), step)
+                there = pl.ds(pl.multiple_of(x * BLOCK + r * step, step), step)
+                value = streams[i, at, :]
+                centered = value - row_mean(value)
+                scale = lax.rsqrt(row_mean(centered * centered) + EPSILON)
+                normed[i, there, :] = (centered * scale * gains[i : i + 1, :]).astype(BF16)
+                return carry
+
+            lax.fori_loop(0, BLOCK // step, norm, 0)
+            push(i, 0, x, True, peers[1])
+            push(i, 2, x, False, peers[3])
+            push(i, 1, x, False, peers[1])
+            push(i, 3, x, True, peers[3])
+
+        given = []
+
+        def work(i, place):
+            result = dot_nn(normed[i, block(place), :], weights[i])
+            out = (queries, keys, values)[i]
+            if i == 2:
+                out[block(place), :] = result.astype(BF16)
+            else:
+                at = block(place)
+                for h in range(cols // HD):
+                    part = result[:, h * HD : (h + 1) * HD]
+                    ahead, behind = pltpu.roll(part, HD - ROT // 2, 1), pltpu.roll(part, ROT // 2, 1)
+                    turned = part * tables[0, at, :] + ahead * tables[1, at, :] + behind * tables[2, at, :]
+                    out[at, h * HD : (h + 1) * HD] = turned.astype(BF16)
+            if i > 0:
+                j = len(given)
+                other = (None, other_keys, other_values)[i]
+                given.append(remote(out.at[block(place)], other.at[block(place)], zsend.at[j], zrecv.at[j], partner))
+                given[-1].start()
+
+        for i in order:
+            loads[i].wait()
+            work(i, x)
+        relay_z()
+        for i in order:
+            copies[i, 0].wait_recv()
+            push(i, 4, left, True, peers[1])
+            copies[i, 2].wait_recv()
+            push(i, 5, right, False, peers[3])
+            copies[i, 1].wait_recv()
+            work(i, left)
+            copies[i, 3].wait_recv()
+            work(i, right)
+            relay_y((1, 2, 0).index(i))
+        stores = []
+        for i in order:
+            copies[i, 4].wait_recv()
+            copies[i, 5].wait_recv()
+            stores.append(pltpu.make_async_copy(normed.at[i], normed_out.at[i], local.at[i]))
+            stores[-1].start()
+            work(i, far)
+        relay_y(3)
+        finish()
+        for copy in given + stores + kept:
+            copy.wait()
+        for copy in copies.values():
+            copy.wait_send()
+
+    vmem = pltpu.VMEM
+    sem = pltpu.SemaphoreType.DMA
+    return pl.pallas_call(
+        kernel,
+        out_shape=[shape((rows_all, cols))] * 5
+        + [shape((3, rows_all, width)), shape((1, down.shape[1] * 16, down.shape[2] * 2))],
+        in_specs=[VMEM, VMEM, ANY, VMEM, ANY],
+        out_specs=[VMEM] * 5 + [ANY, ANY],
+        scratch_shapes=[
+            vmem((3, width, cols), BF16),
+            vmem((3, rows_all, width), BF16),
+            sem((3,)),
+            sem((18,)),
+            sem((18,)),
+            sem((8,)),
+            sem((8,)),
+            sem((4,)),
+            sem((32,)),
+            sem((32,)),
+        ],
+        compiler_params=pltpu.CompilerParams(
+            collective_id=2, has_side_effects=True, vmem_limit_bytes=40 * 2**20
+        ),
+        name="project",
+    )(streams, gains, small, tables, down)
 
 
 def inward(grads, gives, small, normed, out_proj_grad, streams, residual_grad, gains, late_gains, tables, down):
@@ -1014,27 +1140,30 @@
     tile = 2 * BLOCK
     tiles = width // tile
     hidden = down.shape[3]
+    thin = hidden // 2
 
     def kernel(
         dq, dk, dv, give_k, give_v, small, normed, out_proj_grad, streams, residual_grad, gains, late, tables,
         down,
-        stream_cot, gain_grads, small_sum, down_sum,
-        weights, inputs, cots, got_k, got_v, far_part, near, hop, got, own, grad, swapped, sums, down_y,
+        stream_cot, gain_grads, small_sum, down_out,
+        weights, inputs, cots, got_k, got_v, far_part, near, hop, got, own, grad, swapped, sums, down_y, down_part, down_z, stream,
         load, send, recv, ssend, srecv, gsend, grecv, local,
     ):
         x, zl, zh, y, c = coords()
         z = zh * 2 + zl
-        along_y = y_peers(x, zl, zh, y, c)
+        z = zh * 2 + zl
+        along_z, along_y = z_peers(x, zl, zh, y, c), y_peers(x, zl, zh, y, c)
         partner = device(x, 1 - zl, zh, y, c)
         sibling = device(x, zl, zh, y, 1 - c)
         places = {k: (x + k) % 4 for k in (1, 2, 3)}
         peers = {k: device(places[k], zl, zh, y, c) for k in (1, 3)}
         loads = [pltpu.make_async_copy(small.at[i], weights.at[i], load.at[i]) for i in range(3)]
         loads += [pltpu.make_async_copy(normed.at[i], inputs.at[i], load.at[3 + i]) for i in range(3)]
-        loads.append(pltpu.make_async_copy(out_proj_grad, grad.at[3], load.at[6]))
+        loads.append(pltpu.make_async_copy(out_proj_grad, grad.at[0], load.at[6]))
+        loads.append(pltpu.make_async_copy(streams.at[pl.ds(0, 3)], stream, load.at[7]))
         for copy in loads:
             copy.start()
-        greet([peers[1], peers[3], partner, sibling] + [peer for _, peer in along_y])
+        greet([peers[1], peers[3], sibling] + [peer for _, peer in along_z + along_y])
         sides = []
 
         def side(src, dst, peer):
@@ -1106,12 +1235,13 @@
         swaps = []
 
         def weight_grad(i):
+            slot = (1, 0, 1, 0)[i]
             if i < 3:
                 loads[3 + i].wait()
 
                 def one(m, carry):
                     at = pl.ds(pl.multiple_of(m * tile, tile), tile)
-                    grad[i, at, :] = dot_tn(inputs[i, :, at], cots[i]).astype(BF16)
+                    grad[slot, at, :] = dot_tn(inputs[i, :, at], cots[i]).astype(BF16)
                     return carry
 
                 lax.fori_loop(0, tiles, one, 0)
@@ -1121,7 +1251,7 @@
                 begin = pl.multiple_of(m * tile + (1 - c) * BLOCK, BLOCK)
                 j = i * tiles + m
                 swaps.append(
-                    remote(grad.at[i, pl.ds(begin, BLOCK)], swapped.at[i, m], gsend.at[j], grecv.at[j], sibling)
+                    remote(grad.at[slot, pl.ds(begin, BLOCK)], swapped.at[i, m], gsend.at[j], grecv.at[j], sibling)
                 )
                 swaps[-1].start()
 
@@ -1133,7 +1263,7 @@
                 m, part = r // (BLOCK // step), lax.rem(r, BLOCK // step)
                 at = pl.ds(pl.multiple_of(m * tile + c * BLOCK + part * step, step), step)
                 there = pl.ds(pl.multiple_of(part * step, step), step)
-                value = grad[i, at, :].astype(jnp.float32) + swapped[i, m, there, :].astype(jnp.float32)
+                value = grad[(1, 0, 1, 0)[i], at, :].astype(jnp.float32) + swapped[i, m, there, :].astype(jnp.float32)
                 swapped[i, m, there, :] = value.astype(BF16)
                 return carry
 
@@ -1162,12 +1292,37 @@
         far_sums(2)
         near_sums(1)
         near_sums(2)
+        add_cores(3)
+        add_cores(0)
         grads_of(1)
         grads_of(2)
         own_sums(1)
         own_sums(2)
-        for i in (3, 0, 1, 2):
-            add_cores(i)
+        for copy in sides[2:] + locals_[:1]:
+            copy.wait()
+
+        def add_four(parts, places, dst):
+            def one(r, carry):
+                at = pl.ds(pl.multiple_of(r * step, step), step)
+                value = parts[(0,) + places + (at,)].astype(jnp.float32)
+                for src in range(1, 4):
+                    value = value + parts[(src,) + places + (at,)].astype(jnp.float32)
+                dst[places + (at,)] = value.astype(dst.dtype)
+                return carry
+
+            lax.fori_loop(0, BLOCK // step, one, 0)
+
+        def down_piece(high, low):
+            return down_part.at[high, :, pl.ds(pl.multiple_of(low * thin, thin), thin)]
+
+        for high in range(2):
+            add_four(down_y, (high,), down_part)
+        for pz, peer in along_z:
+            side(down_piece(pz // 2, pz % 2), down_z.at[z], peer)
+        down_z[z] = down_part[zh, :, pl.ds(pl.multiple_of(zl * thin, thin), thin)]
+        add_cores(1)
+        add_cores(2)
+        loads[7].wait()
         sums[...] = jnp.zeros_like(sums)
         for i in range(3):
             for side_of in range(2):
@@ -1176,7 +1331,7 @@
 
             def back(r, carry, i=i):
                 at = pl.ds(pl.multiple_of(r * step, step), step)
-                value = streams[i, at, :]
+                value = stream[i, at, :]
                 centered = value - row_mean(value)
                 scale = lax.rsqrt(row_mean(centered * centered) + EPSILON)
                 unit = centered * scale
@@ -1195,19 +1350,9 @@
             gain_grads[i : i + 1, :] = jnp.sum(sums[i], axis=0, keepdims=True)
         gain_grads[3:4, :] = late[1:2, :]
         gain_grads[4:5, :] = late[0:1, :]
-        for copy in sides[2:] + locals_[:1]:
+        for copy in sides[5:]:
             copy.wait()
-        for high in range(2):
-
-            def add_y(r, carry, high=high):
-                at = pl.ds(pl.multiple_of(r * step, step), step)
-                value = down_y[0, high, at, :].astype(jnp.float32)
-                for src in range(1, 4):
-                    value = value + down_y[src, high, at, :].astype(jnp.float32)
-                down_sum[high, at, :] = value.astype(BF16)
-                return carry
-
-            lax.fori_loop(0, BLOCK // step, add_y, 0)
+        add_four(down_z, (), down_out)
         for copy in started + sides[:2]:
             copy.wait_send()
         for copy in locals_[1:]:
@@ -1222,9 +1367,9 @@
             shape((4, BLOCK, width)),
             shape((8, width), f32),
             shape((tiles, 4, BLOCK, cols)),
-            shape((2, BLOCK, hidden)),
+            shape((BLOCK, thin), f32),
         ],
-        in_specs=[VMEM] * 5 + [ANY] * 3 + [VMEM] * 5 + [ANY],
+        in_specs=[VMEM] * 5 + [ANY] * 4 + [VMEM] * 4 + [ANY],
         out_specs=[VMEM, VMEM, ANY, VMEM],
         scratch_shapes=[
             vmem((3, width, cols), BF16),
@@ -1237,11 +1382,14 @@
             vmem((3, 2, half, width), BF16),
             vmem((3, 2, BLOCK, width), BF16),
             vmem((3, BLOCK, width), f32),
-            vmem((4, width, cols), BF16),
+            vmem((2, width, cols), BF16),
             vmem((4, tiles, BLOCK, cols), BF16),
             vmem((3, 8, width), f32),
             vmem((4, 2, BLOCK, hidden), BF16),
-            sem((7,)),
+            vmem((2, BLOCK, hidden), BF16),
+            vmem((4, BLOCK, thin), BF16),
+            vmem((3, BLOCK, width), f32),
+            sem((8,)),
             sem((12,)),
             sem((12,)),
             sem((8,)),
@@ -1259,8 +1407,8 @@
     )
 
 
-def hand_out(own_hist, weights, stream_cot, gains, small, up, down):
-    groups, n, rows, width = own_hist.shape
+def hand_out(top_hist, bottom_hist, top_weights, bottom_weights, stream_cot, gains, small, up):
+    _, _, n, half, width = top_hist.shape
     cols = small.shape[3]
     thin = cols // 2
     hidden = up.shape[2] // 2
@@ -1268,31 +1416,25 @@
     lanes = 128
 
     def kernel(
-        hist, w, cot, gains, small, up, down,
-        out, omg, gains_out, small_out, up_out, down_out,
-        held, stage, mixes, turned, x_slots, z_slots, y_slots, c_part, c_slot,
-        small_y, small_part, small_z, up_y, up_part, up_z, down_z,
-        load, send, recv, msend, mrecv, local, sends, recvs, ssend, srecv,
+        top_hist, bottom_hist, tw, bw, cot, gains, small, up,
+        out, top_mix, bottom_mix, gains_out, small_out, up_out,
+        top, bottom, top_stage, bottom_stage, cot_z, cot_x, mixes, turned,
+        x_slots, z_slots, y_slots, c_part, c_slot,
+        small_y, small_part, small_z, up_y, up_part, up_z,
+        load, csend, crecv, send, recv, msend, mrecv, local, sends, recvs, ssend, srecv,
     ):
         x, zl, zh, y, c = coords()
         z = zh * 2 + zl
-        place = x * 2 + zl
-        others = hist_peers(x, zl)
-        peers = [device(px, pz, zh, y, c) for px, pz in others]
-        holders = [px * 2 + pz for px, pz in others] + [place]
-        loads = []
-        for k, holder in enumerate(holders):
-            for j in range(n):
-                i = k * n + j
-                loads.append(pltpu.make_async_copy(hist.at[holder, j], held.at[k, j], load.at[i]))
-        for j in range(n):
-            for copy in loads[j::n]:
-                copy.start()
+        partner = device(x, 1 - zl, zh, y, c)
+        peers = {k: device((x + k) % 4, zl, zh, y, c) for k in (1, 2, 3)}
+        loads = [pltpu.make_async_copy(top_hist.at[o], top.at[o], load.at[o]) for o in range(2)]
+        loads += [pltpu.make_async_copy(bottom_hist.at[k], bottom.at[k], load.at[2 + k]) for k in range(4)]
+        for i in (0, 2, 1, 3, 5, 4):
+            loads[i].start()
         along_x, along_z = x_peers(x, zl, zh, y, c), z_peers(x, zl, zh, y, c)
         along_y = y_peers(x, zl, zh, y, c)
         sibling = device(x, zl, zh, y, 1 - c)
-        others_z = [device(x, 1 - zl, 1 - zh, y, c), device(x, zl, 1 - zh, y, c)]
-        greet(peers + others_z + [peer for _, peer in along_y] + [sibling])
+        greet([peer for _, peer in along_x + along_z + along_y] + [sibling])
         sides = []
 
         def side(src, dst, peer):
@@ -1302,79 +1444,132 @@
 
         first = exchange(gains, x_slots, x, along_x, sends, recvs, 0)
         x_slots[x] = gains[...]
+        copies = []
+
+        def push(src, dst, send, recv, i, peer):
+            copies.append(remote(src, dst, send.at[i], recv.at[i], peer))
+            copies[-1].start()
+
+        push(cot.at[:, pl.ds(0, half)], cot_z, csend, crecv, 0, partner)
+        for k in (1, 3, 2):
+            push(cot.at[:, pl.ds(half, half)], cot_x.at[3 - k], csend, crecv, 1 + 3 - k, peers[k])
         for py, peer in along_y:
             for high in range(2):
                 side(small.at[high * 4 + py], small_y.at[y, high], peer)
         for py, peer in along_y:
             for high in range(2):
                 side(up.at[high * 4 + py], up_y.at[y, high], peer)
-        for pz, peer in along_z:
-            high, low = pz // 2, pz % 2
-            side(down.at[high, :, pl.ds(pl.multiple_of(low * hidden, hidden), hidden)], down_z.at[z], peer)
-        own_rows = pl.ds(pl.multiple_of(place * rows, rows), rows)
         locals_ = [
             pltpu.make_async_copy(small.at[y], small_y.at[y, 0], local.at[0]),
             pltpu.make_async_copy(small.at[4 + y], small_y.at[y, 1], local.at[1]),
-            pltpu.make_async_copy(
-                down.at[zh, :, pl.ds(pl.multiple_of(zl * hidden, hidden), hidden)], down_z.at[z], local.at[2]
-            ),
-            pltpu.make_async_copy(up.at[y], up_y.at[y, 0], local.at[3]),
-            pltpu.make_async_copy(up.at[4 + y], up_y.at[y, 1], local.at[4]),
+            pltpu.make_async_copy(up.at[y], up_y.at[y, 0], local.at[2]),
+            pltpu.make_async_copy(up.at[4 + y], up_y.at[y, 1], local.at[3]),
         ]
         for copy in locals_:
             copy.start()
-        copies = []
+
         lane = lax.broadcasted_iota(jnp.int32, (step, lanes), 1)
 
-        def entry_grads(k, j):
-            holder = holders[k]
-            loads[k * n + j].wait()
-
-            def some_rows(r, carry):
-                at = pl.ds(pl.multiple_of(r * step, step), step)
-                factors = w[holder, j, at, :]
-                factors = [jnp.broadcast_to(factors[:, s : s + 1], (step, lanes)) for s in range(4)]
-                totals = [jnp.zeros((step, lanes), jnp.float32) for _ in range(4)]
-                for block in range(width // lanes):
-                    part = pl.ds(block * lanes, lanes)
-                    entry = held[k, j, at, part].astype(jnp.float32)
-                    mixed = jnp.zeros((step, lanes), jnp.float32)
+        def grads_of(entry_of, factors_of, cot_of, stage, slot):
+            for j in range(n):
+
+                def some_rows(r, carry, j=j):
+                    at = pl.ds(pl.multiple_of(r * step, step), step)
+                    factors = factors_of(j, at)
+                    factors = [jnp.broadcast_to(factors[:, s : s + 1], (step, lanes)) for s in range(4)]
+                    totals = [jnp.zeros((step, lanes), jnp.float32) for _ in range(4)]
+                    for block in range(width // lanes):
+                        part = pl.ds(block * lanes, lanes)
+                        entry = entry_of(j)[at, part].astype(jnp.float32)
+                        mixed = jnp.zeros((step, lanes), jnp.float32)
+                        for s in range(4):
+                            piece = cot_of(s)[at, part].astype(jnp.float32)
+                            mixed = mixed + factors[s] * piece
+                            totals[s] = totals[s] + entry * piece
+                        stage[j, at, part] = mixed.astype(BF16)
+                    packed = jnp.zeros((step, lanes), jnp.float32) if j == 0 else mixes[at, :]
                     for s in range(4):
-                        piece = cot[s, at, part].astype(jnp.float32)
-                        mixed = mixed + factors[s] * piece
-                        totals[s] = totals[s] + entry * piece
-                    stage[k, j, at, part] = mixed.astype(BF16)
-                packed = jnp.zeros((step, lanes), jnp.float32)
-                for s in range(4):
-                    packed = jnp.where(lane == s, jnp.sum(totals[s], axis=1, keepdims=True), packed)
-                mixes[at, :] = packed
-                return carry
-
-            lax.fori_loop(0, rows // step, some_rows, 0)
-            turned[k, j] = jnp.transpose(mixes[...])[:8]
-            if k < 7:
-                i = k * n + j
-                copies.append(remote(stage.at[k, j], out.at[j, own_rows], send.at[i], recv.at[i], peers[k]))
-                copies[-1].start()
-                if j == n - 1:
-                    copies.append(remote(turned.at[k], omg.at[place], msend.at[k], mrecv.at[k], peers[k]))
-                    copies[-1].start()
-
-        for k in range(7):
-            entry_grads(k, 0)
+                        total = jnp.sum(totals[s], axis=1, keepdims=True)
+                        packed = jnp.where(lane == j * 4 + s, total, packed)
+                    mixes[at, :] = packed
+                    return carry
+
+                lax.fori_loop(0, half // step, some_rows, 0)
+            turned[slot] = jnp.transpose(mixes[...])[:16]
+
+        def out_rows(k, other, low):
+            begin = ((x + k) % 4 * 2 + (1 - zl if other else zl)) * BLOCK + low * half
+            return out.at[:, pl.ds(pl.multiple_of(begin, half), half)]
+
+        def owner(k, other):
+            return (x + k) % 4 * 2 + (1 - zl if other else zl)
+
+        def keep(src, dst):
+            locals_.append(pltpu.make_async_copy(src, dst, local.at[len(locals_)]))
+            locals_[-1].start()
+
+        def do_top(other, k):
+            slot = other * 4 + k
+            source = cot_z if other else cot
+            cot_of = (lambda s: source.at[s]) if other else (lambda s: source.at[s, pl.ds(0, half)])
+            grads_of(
+                lambda j: top.at[other, k, j],
+                lambda j, at: tw[other, k * 3 + j, at, :],
+                cot_of,
+                top_stage.at[other, k],
+                slot,
+            )
+            if k == 0:
+                keep(top_stage.at[other, 0], out_rows(0, other, 0))
+                keep(turned.at[slot], top_mix.at[owner(0, other)])
+            else:
+                i = other * 3 + k - 1
+                push(top_stage.at[other, k], out_rows(0, other, 0), send, recv, i, peers[k])
+                push(turned.at[slot], top_mix.at[owner(0, other)], msend, mrecv, i, peers[k])
+
+        def do_bottom(k, other):
+            slot = 8 + k * 2 + other
+            cot_of = (lambda s: cot_x.at[k - 1, s]) if k else (lambda s: cot.at[s, pl.ds(half, half)])
+            grads_of(
+                lambda j: bottom.at[k, other, j],
+                lambda j, at: bw[k, other * 3 + j, at, :],
+                cot_of,
+                bottom_stage.at[k, other],
+                slot,
+            )
+            if other:
+                push(bottom_stage.at[k, 1], out_rows(k, 0, 1), send, recv, 6 + k, partner)
+                push(turned.at[slot], bottom_mix.at[owner(k, 0)], msend, mrecv, 6 + k, partner)
+            else:
+                keep(bottom_stage.at[k, 0], out_rows(k, 0, 1))
+                keep(turned.at[slot], bottom_mix.at[owner(k, 0)])
+
+        def cot_came(ref, i):
+            remote(ref, ref, csend.at[i], crecv.at[i], partner).wait_recv()
+
+        mixes[...] = jnp.zeros_like(mixes)
+        loads[0].wait()
+        do_top(0, 1)
+        do_top(0, 3)
+        loads[2].wait()
+        do_bottom(0, 1)
+        do_top(0, 2)
         for copy in first:
             copy.wait()
         z_slots[z] = x_slots[0] + x_slots[1] + x_slots[2] + x_slots[3]
         second = exchange(z_slots.at[z], z_slots, z, along_z, sends, recvs, 3)
-        for j in range(1, n):
-            for k in range(7):
-                entry_grads(k, j)
-        for j in range(n):
-            entry_grads(7, j)
-            locals_.append(pltpu.make_async_copy(stage.at[7, j], out.at[j, own_rows], local.at[5 + j]))
-            locals_[-1].start()
-        locals_.append(pltpu.make_async_copy(turned.at[7], omg.at[place], local.at[5 + n]))
-        locals_[-1].start()
+        cot_came(cot_z, 0)
+        loads[1].wait()
+        for k in (1, 3, 2):
+            do_top(1, k)
+        for k in (1, 3, 2):
+            cot_came(cot_x.at[k - 1], k)
+            loads[2 + k].wait()
+            do_bottom(k, 1)
+        do_top(0, 0)
+        do_top(1, 0)
+        for k in range(4):
+            do_bottom(k, 0)
         for copy in second:
             copy.wait()
         y_slots[y] = z_slots[0] + z_slots[1] + z_slots[2] + z_slots[3]
@@ -1396,67 +1591,75 @@
                 dst[places + (at,)] = value.astype(dst.dtype)
                 return carry
 
-            lax.fori_loop(0, rows // step, one, 0)
-
-        def to_z(parts, slots, wide, first_sem):
-            cut = [slice(None)] * (len(parts.shape) - 2)
-
-            def piece(high, low):
-                return parts.at[tuple([high] + cut + [pl.ds(pl.multiple_of(low * wide, wide), wide)])]
-
-            out_copies = []
-            for k, (pz, peer) in enumerate(along_z):
-                i = first_sem + k
-                out_copies.append(remote(piece(pz // 2, pz % 2), slots.at[z], ssend.at[i], srecv.at[i], peer))
-            out_copies.append(pltpu.make_async_copy(piece(zh, zl), slots.at[z], local.at[6 + n + first_sem // 18]))
-            for copy in out_copies:
-                copy.start()
-            return out_copies
+            lax.fori_loop(0, BLOCK // step, one, 0)
+
+        def small_piece(high, low):
+            return small_part.at[high, :, :, pl.ds(pl.multiple_of(low * thin, thin), thin)]
 
         for copy in sides[:6] + locals_[:2]:
             copy.wait()
         for high in range(2):
             for i in range(4):
                 add_four(small_y, (high, i), small_part)
-        small_last = to_z(small_part, small_z, thin, 15)
-        for copy in sides[6:12] + locals_[3:5]:
+        small_last = []
+        for k, (pz, peer) in enumerate(along_z):
+            small_last.append(
+                remote(small_piece(pz // 2, pz % 2), small_z.at[z], ssend.at[12 + k], srecv.at[12 + k], peer)
+            )
+            small_last[-1].start()
+        keep(small_piece(zh, zl), small_z.at[z])
+        for copy in sides[6:] + locals_[2:4]:
             copy.wait()
         for high in range(2):
             add_four(up_y, (high,), up_part)
-        up_last = to_z(up_part, up_z, hidden, 18)
-        for copy in sides[12:] + locals_[2:3]:
-            copy.wait()
-        add_four(down_z, (), down_out)
-        for copy in small_last:
+
+        def up_piece(high, low):
+            return up_part.at[high, :, pl.ds(pl.multiple_of(low * hidden, hidden), hidden)]
+
+        up_last = []
+        for k, (pz, peer) in enumerate(along_z):
+            up_last.append(
+                remote(up_piece(pz // 2, pz % 2), up_z.at[z], ssend.at[15 + k], srecv.at[15 + k], peer)
+            )
+            up_last[-1].start()
+        keep(up_piece(zh, zl), up_z.at[z])
+        for copy in small_last + locals_[4:]:
             copy.wait()
         for i in range(4):
             add_four(small_z, (i,), small_out)
         for copy in up_last:
             copy.wait()
         add_four(up_z, (), up_out)
-        for copy in copies + locals_[5:]:
+        for copy in copies[:4]:
+            copy.wait_send()
+        for copy in copies[4:]:
             copy.wait()
 
     f32 = jnp.float32
     vmem = pltpu.VMEM
     sem = pltpu.SemaphoreType.DMA
+    piece = (4, half, width)
     return pl.pallas_call(
         kernel,
         out_shape=[
-            shape((n, groups * rows, width)),
-            shape((groups, n, 8, lanes), f32),
+            shape((n, 8 * BLOCK, width)),
+            shape((8, 16, lanes), f32),
+            shape((8, 16, lanes), f32),
             shape(gains.shape, f32),
             shape((4, BLOCK, thin), f32),
             shape((BLOCK, hidden), f32),
-            shape((BLOCK, hidden), f32),
         ],
-        in_specs=[ANY, VMEM, VMEM, VMEM, ANY, ANY, ANY],
-        out_specs=[ANY, ANY, VMEM, VMEM, VMEM, VMEM],
+        in_specs=[ANY, ANY, VMEM, VMEM, VMEM, VMEM, ANY, ANY],
+        out_specs=[ANY, ANY, ANY, VMEM, VMEM, VMEM],
         scratch_shapes=[
-            vmem((groups, n, rows, width), BF16),
-            vmem((groups, n, rows, width), BF16),
-            vmem((rows, lanes), f32),
-            vmem((groups, n, 8, lanes), f32),
+            vmem(top_hist.shape, BF16),
+            vmem(bottom_hist.shape, BF16),
+            vmem(top_hist.shape, BF16),
+            vmem(bottom_hist.shape, BF16),
+            vmem(piece, BF16),
+            vmem((3,) + piece, BF16),
+            vmem((BLOCK, lanes), f32),
+            vmem((16, 16, lanes), f32),
             vmem((4,) + gains.shape, f32),
             vmem((4,) + gains.shape, f32),
             vmem((4,) + gains.shape, f32),
@@ -1468,23 +1671,24 @@
             vmem((4, 2, BLOCK, 2 * hidden), BF16),
             vmem((2, BLOCK, 2 * hidden), BF16),
             vmem((4, BLOCK, hidden), BF16),
-            vmem((4, BLOCK, hidden), BF16),
-            sem((groups * n,)),
-            sem((7 * n,)),
-            sem((7 * n,)),
-            sem((7,)),
-            sem((7,)),
-            sem((n + 8,)),
+            sem((6,)),
+            sem((4,)),
+            sem((4,)),
             sem((10,)),
             sem((10,)),
-            sem((21,)),
-            sem((21,)),
+            sem((10,)),
+            sem((10,)),
+            sem((18,)),
+            sem((10,)),
+            sem((10,)),
+            sem((18,)),
+            sem((18,)),
         ],
         compiler_params=pltpu.CompilerParams(
             collective_id=6, has_side_effects=True, vmem_limit_bytes=56 * 2**20
         ),
         name="hand_out",
-    )(own_hist, weights, stream_cot, gains, small, up, down)
+    )(top_hist, bottom_hist, top_weights, bottom_weights, stream_cot, gains, small, up)
 
 
 def body(
@@ -1504,51 +1708,52 @@
     mix_grad_in,
 ):
     place = lax.axis_index("hist")
-    low_z = place % 2
+    along_x, low_z = place // 2, place % 2
     slots, seq_len, width = history.shape
     small = jnp.concatenate([jnp.transpose(w_qkv, (1, 0, 2)), w_out[None]], axis=0)
-    large = jnp.stack([w_up, w_down], axis=0)
-    own_hist, full_small, full_large = collect(history, small, large)
-    w_q, w_k, w_v, full_out = (full_small[i] for i in range(4))
-    full_up, full_down = full_large[0], full_large[1]
-    flat_hist = own_hist.reshape(8 * slots, BLOCK, width)
-
-    own_mix = lax.dynamic_slice_in_dim(mix_weights, place * BLOCK, BLOCK, 2)
-    pick = (layer_ids[:, None] == jnp.arange(own_mix.shape[1], dtype=jnp.int32)[None, :]).astype(jnp.float32)
-    slot_weights = jnp.einsum("jl,slt->sjt", pick, own_mix, precision=HIGHEST)
-    owned = jnp.zeros((4, BLOCK, width), jnp.float32)
-    for j in range(8 * slots):
-        owned = owned + slot_weights[:, j, :, None] * flat_hist[j][None].astype(jnp.float32)
-
-    norm_unit, inv_std = norm_rows(owned[:3])
-    normed = (norm_unit * gains[:3, None, :]).astype(BF16)
-    gathered = gather_x(normed, 2, "gather_normed").reshape(3, 4 * BLOCK, width)
+
+    def ring(values, axis):
+        return lax.dynamic_slice_in_dim(jnp.concatenate([values, values], axis=axis), along_x, 4, axis)
+
+    def own_first(values, axis):
+        return jnp.where(low_z == 0, values, jnp.flip(values, axis=axis))
+
+    def picked(ids):
+        return (ids.reshape(-1, 1) == jnp.arange(layers, dtype=jnp.int32)[None, :]).astype(jnp.float32)
+
+    layers = mix_weights.shape[1]
+    ids = layer_ids.reshape(4, 2, slots)
+    tokens = mix_weights.reshape(4, layers, 4, 2, 2, BLOCK // 2)
+    top_ids = ring(lax.dynamic_index_in_dim(ids, low_z, 1, False), 0)
+    bottom_ids = own_first(lax.dynamic_index_in_dim(ids, along_x, 0, False), 0)
+    top_tokens = own_first(lax.dynamic_index_in_dim(tokens[:, :, :, :, 0], along_x, 2, False), 2)
+    bottom_tokens = ring(lax.dynamic_index_in_dim(tokens[:, :, :, :, 1], low_z, 3, False), 2)
+    top_weights = jnp.einsum("rl,slot->orts", picked(top_ids), top_tokens, precision=HIGHEST)
+    bottom_weights = jnp.einsum("rl,slkt->krts", picked(bottom_ids), bottom_tokens, precision=HIGHEST)
+    owned, top_hist, bottom_hist, full_small, full_up = collect(
+        history, small, w_up[None], top_weights, bottom_weights
+    )
     rows_here = 4 * BLOCK
-    heads_cols = full_out.shape[1]
     cosine, sine_table = rotary_tables(seq_len, ROT)
 
     def here(table, side=low_z):
         return lax.dynamic_index_in_dim(table.reshape(4, 2, BLOCK, -1), side, 1, False).reshape(rows_here, -1)
 
-    cos_here, sin_here = here(cosine), here(sine_table)
-    nothing = jnp.zeros_like(sin_here)
-    rest = jnp.zeros((rows_here, HD - ROT), jnp.float32)
-    tables = [
-        jnp.tile(jnp.concatenate(parts, axis=1), (1, heads_cols // HD))
-        for parts in ((cos_here, cos_here, rest + 1.0), (-sin_here, nothing, rest), (nothing, sin_here, rest))
-    ]
-
-    def turn(values, direction):
-        ahead, behind = jnp.roll(values, -ROT // 2, axis=1), jnp.roll(values, ROT // 2, axis=1)
-        return values * tables[0] + direction * (ahead * tables[1] + behind * tables[2])
-
-    def project(which, weight):
-        return jnp.dot(gathered[which], weight, preferred_element_type=jnp.float32)
-
-    keys = turn(project(1, w_k), 1.0).astype(BF16)
-    values = project(2, w_v).astype(BF16)
-    other_keys, other_values = send_hist(keys, 0, 1), send_hist(values, 0, 1)
-    queries = turn(project(0, w_q), 1.0).astype(BF16)
+    nothing = jnp.zeros_like(sine_table)
+    rest = jnp.zeros((seq_len, HD - ROT), jnp.float32)
+    tables = jnp.stack(
+        [
+            here(jnp.concatenate(parts, axis=1))
+            for parts in (
+                (cosine, cosine, rest + 1.0),
+                (-sine_table, nothing, rest),
+                (nothing, sine_table, rest),
+            )
+        ]
+    )
+    queries, keys, values, other_keys, other_values, gathered, full_down = project(
+        owned, gains, full_small, tables, w_down[None]
+    )
     places = jnp.stack([jnp.arange(seq_len, dtype=jnp.int32), doc_ids], axis=1)
     query_at, other_at = here(places), here(places, 1 - low_z)
     key_at = jnp.concatenate([query_at.T, other_at.T], axis=0)
@@ -1571,7 +1776,8 @@
     ) = middle(
         heads_flat,
         full_small,
-        full_large,
+        full_up,
+        full_down,
         owned,
         gains,
         jnp.pad(da_in, ((0, 0), (0, spare))),
@@ -1594,14 +1800,22 @@
         residual_grad,
         gains,
         late_gains,
-        jnp.stack([table[:, :HD] for table in tables]),
+        tables,
         down_sum.reshape(2, 4, BLOCK, -1),
     )
-    columns = jnp.transpose(slot_weights.reshape(4, 8, slots, BLOCK), (1, 2, 3, 0))
-    history_grad, mix_out, gains_sum, small_sum, up_sum, down_sum = hand_out(
-        own_hist, columns, stream_cot, gains_local, small_sum, up_sum.reshape(8, BLOCK, -1), down_sum
+    history_grad, top_mix, bottom_mix, gains_sum, small_sum, up_sum = hand_out(
+        top_hist,
+        bottom_hist,
+        top_weights,
+        bottom_weights,
+        stream_cot,
+        gains_local,
+        small_sum,
+        up_sum.reshape(8, BLOCK, -1),
     )
-    mix_grad = jnp.transpose(mix_out[:, :, :4], (2, 1, 0, 3)).reshape(4, slots, seq_len)
+    half = BLOCK // 2
+    mix_out = jnp.concatenate([top_mix[:, : 4 * slots, :half], bottom_mix[:, : 4 * slots, :half]], axis=2)
+    mix_grad = jnp.transpose(mix_out.reshape(8, slots, 4, BLOCK), (2, 1, 0, 3)).reshape(4, slots, seq_len)
     return (
         block_out,
         mix_next[:, :mixers],

time: 783 us -> 630 us (0.80)
  Pallas kernels: 675 us -> 566 us
  other arithmetic: 24.6 us -> 5.05 us
  matrix products: 11 us -> 0.46 us
  local copies, waits for them, and re-layouts: 61.5 us -> 51.6 us
    pallas_call x3, Pallas kernels: 422 us -> 318 us  [the longest x1 131 us: hand_out(): pl.pallas_call(kernel, out_shape=[shape((n, 8 * BLOCK, width)), shape((8,...]
    dot_general x4 -> x2, matrix products: 11 us -> 0.46 us  [the longest x1 0.24 us: body(): jnp.einsum('rl,slkt->krts', picked(bottom_ids), bottom_tokens, precision=...]
    unnamed x86 -> x60, local copies, waits for them, and re-layouts: 36.9 us -> 35.3 us
  transfers between devices with their start and end apart: 2 -> 0, of which waited for: 0 -> 0; matrix products, arithmetic and copies ran while one was open for 4% -> 0% of each run, Pallas kernels for 0% -> 0%
where the time goes in v3:
time: 630 us; the launch traced here: 624 us
  Pallas kernels  566 us (90%)
  local copies, waits for them, and re-layouts  51.6 us (8%)
    pallas_call x1, Pallas kernels, middle(): pl.pallas_call(kernel, out_shape=[shape((BLOCK, width)), shape((BLOCK, BL...  166 us
    pallas_call x1, Pallas kernels, hand_out(): pl.pallas_call(kernel, out_shape=[shape((n, 8 * BLOCK, width)), shape((8,...  131 us
    pallas_call x1, Pallas kernels, collect(): pl.pallas_call(kernel, out_shape=[shape((4, BLOCK, width), jnp.float32),...  124 us
    pallas_call x1, Pallas kernels, inward(): pl.pallas_call(kernel, out_shape=[shape((4, BLOCK, width)), shape((8, wid...  64.7 us
    pallas_call x1, Pallas kernels, project(): pl.pallas_call(kernel, out_shape=[shape((rows_all, cols))] * 5 + [shape((...  63.1 us
    unnamed x60, local copies, waits for them, and re-layouts  35.3 us

profile of v3, /device:TPU:1, one launch (start us, length us, event | category | flops | bytes accessed | tf_op | source)
XLA Modules:
  0.0 624.2 jit_solution(11045326004747193148)
XLA Ops:
  0.7 1.2 pad_bitcast_fusion.da_bias
  3.9 1.4 pad.17.da_out
  7.9 1.3 copy.42
  10.1 1.6 reshape.149
  13.8 1.9 multiply_cosine_fusion
  16.1 124.1 %collect.1 = (f32[4,128,2048]{2,1,0:T(8,128)}, bf16[2,4,3,64,2048]{4,3,2,1,0:T(8,128)(2,1)}, bf16[4,2,3,64,2048]{4,3,2,1,0:T(8,128)(2,1)}, bf16[4,2048,512]{2,1,0:T(8,128)(2,1)}, bf16[1,2048,2048]{2,1,0:T(8,128)(2,1)}) custom-call(bf16[3,1024,2048]{2,1,0:T(8,128)(2,1)} %hist.1, bf16[4,128,256]{2,1,0:T(8,128)(2,1)S(1)} %pad_maximum_fusion.1.wa, ...), custom_call_target="tpu_custom_call" | custom-call | tf_op jit(solution)/shard_map/collect/pallas_call | solution.py:374
  140.3 2.2 copy-done
  142.4 63.1 %project.1 = (bf16[512,512]{1,0:T(8,128)(2,1)S(1)}, bf16[512,512]{1,0:T(8,128)(2,1)S(1)}, bf16[512,512]{1,0:T(8,128)(2,1)S(1)}, bf16[512,512]{1,0:T(8,128)(2,1)S...) custom-call(f32[4,128,2048]{2,1,0:T(8,128)S(1)} %copy-done, ...), custom_call_target="tpu_custom_call" | custom-call | tf_op jit(solution)/shard_map/project/pallas_call | solution.py:1110
  205.6 2.7 copy-done.4
  208.3 6.7 %attend.1 = (bf16[512,512]{1,0:T(8,128)(2,1)S(1)}, f32[4,512,1]{2,1,0:T(8,128)S(1)}) custom-call(bf16[512,512]{1,0:T(8,128)(2,1)S(1)} %get-tuple-element.52.q, bf16[512,512]{1,0:T(8,128)(2,1)S(1)} %get-tuple-element.53.k, bf16[512,512]{1,0:T(8,128)(2,1)S(1)} %get-tuple-element.54.v, bf16[512,512]{1,0:T(8,128)(2,1)S(1)} %get-tuple-element.55.ok, ...), custom_call_target="tpu_custom_call" | custom-call | tf_op jit(solution)/shard_map/attend/pallas_call | solution.py:447
  217.6 165.7 %middle.1 = (bf16[128,2048]{1,0:T(8,128)(2,1)}, f32[128,128]{1,0:T(8,128)}, f32[128,2048]{1,0:T(8,128)}, bf16[512,512]{1,0:T(8,128)(2,1)}, f32[2,2048]{1,0:T(2,1...) custom-call(bf16[512,512]{1,0:T(8,128)(2,1)} %copy-done.17, ...), custom_call_target="tpu_custom_call" | custom-call | tf_op jit(solution)/shard_map/middle/pallas_call | solution.py:939
  383.3 1.6 copy.46
  384.8 1.2 slice_bitcast_fusion.2
  386.0 1.4 slice.51
  387.5 1.3 slice.50
  388.8 1.3 copy.47
  391.1 1.0 copy-done.8
  392.1 1.2 copy-done.10
  394.4 10.5 %attend_back.1 = (f32[512,512]{1,0:T(8,128)S(1)}, f32[512,512]{1,0:T(8,128)S(1)}, f32[512,512]{1,0:T(8,128)S(1)}, bf16[512,512]{1,0:T(8,128)(2,1)S(1)}, bf16[512,512]{1,0:T(8,128)(2,1)S(1)}) custom-call(bf16[512,512]{1,0:T(8,128)(2,1)S(1)} %get-tuple-element.52.q, bf16[512,512]{1,0:T(8,128)(2,1)S(1)} %get-tuple-element.53.k, ...), custom_call_target="tpu_custom_call" | custom-call | tf_op jit(solution)/shard_map/attend_back/pallas_call | solution.py:498
  409.4 64.7 %inward.1 = (bf16[4,128,2048]{2,1,0:T(8,128)(2,1)}, f32[8,2048]{1,0:T(8,128)}, bf16[8,4,128,512]{3,2,1,0:T(8,128)(2,1)}, f32[128,1024]{1,0:T(8,128)}) custom-call(f32[512,512]{1,0:T(8,128)} %copy-done.11, f32[512,512]{1,0:T(8,128)} %copy-done.12, f32[512,512]{1,0:T(8,128)} %copy-done.13, bf16[512,512]{1,0:T(8,128)(2,1)} %copy-done.15, ...), custom_call_target="tpu_custom_call" | custom-call | tf_op jit(solution)/shard_map/inward/pallas_call | solution.py:1364
  474.2 130.7 %hand_out.1 = (bf16[3,1024,2048]{2,1,0:T(8,128)(2,1)}, f32[8,16,128]{2,1,0:T(8,128)}, f32[8,16,128]{2,1,0:T(8,128)}, f32[8,2048]{1,0:T(8,128)}, f32[4,128,256]{2,1,0:T(8,128)}, /*index=5*/f32[128,1024]{1,0:T(8,128)}) custom-call(bf16[2,4,3,64,2048]{4,3,2,1,0:T(8,128)(2,1)} %get-tuple-element.62.top_hist, ...), custom_call_target="tpu_custom_call" | custom-call | tf_op jit(solution)/shard_map/hand_out/pallas_call | solution.py:1642
  606.5 1.6 slice_bitcast_fusion.1
  608.1 1.8 slice_bitcast_fusion
  610.7 10.8 %copy.68 = bf16[3,1024,2048]{2,1,0:T(8,128)(2,1)} copy(bf16[3,1024,2048]{2,1,0:T(8,128)(2,1)} %get-tuple-element.139) | data formatting | bytes 25165824
  (90 shorter events, 21.8 us)
Async XLA Ops:
  10.1 5.9 copy-start.19
  13.4 126.8 %copy-start.1 = (f32[4,2,64,12]{0,2,3,1:T(8,128)}, f32[4,2,64,12]{0,2,3,1:T(8,128)S(1)}, u32[]{:S(2)}) copy-start(f32[4,2,64,12]{0,2,3,1:T(8,128)S(1)} %copy.38) | copy-start | bytes 73732
  13.7 126.5 %copy-start.2 = (f32[4,4,64,6]{0,2,3,1:T(8,128)}, f32[4,4,64,6]{0,2,3,1:T(8,128)S(1)}, u32[]{:S(2)}) copy-start(f32[4,4,64,6]{0,2,3,1:T(8,128)S(1)} %copy.40) | copy-start | bytes 73732
  16.1 124.2 %copy-start.3 = (f32[3,512,128]{2,1,0:T(8,128)}, f32[3,512,128]{2,1,0:T(8,128)S(1)}, u32[]{:S(2)}) copy-start(f32[3,512,128]{2,1,0:T(8,128)S(1)} %pad_maximum_fusion.tables) | copy-start | bytes 2359300
  16.1 124.2 %copy-start.14 = (f32[5,2048]{1,0:T(8,128)S(1)}, f32[5,2048]{1,0:T(8,128)}, u32[]{:S(2)}) copy-start(f32[5,2048]{1,0:T(8,128)} %gains.5) | copy-start | bytes 122884
  16.1 124.2 %copy-start.20 = (bf16[128,1024]{1,0:T(8,128)(2,1)S(1)}, bf16[128,1024]{1,0:T(8,128)(2,1)}, u32[]{:S(2)}) copy-start(bf16[128,1024]{1,0:T(8,128)(2,1)} %param.22) | copy-start | bytes 786436
  140.3 2.2 copy-start
  205.6 2.7 copy-start.4
  208.3 6.7 %copy-start.7 = (bf16[512,512]{1,0:T(8,128)(2,1)}, bf16[512,512]{1,0:T(8,128)(2,1)S(1)}, u32[]{:S(2)}) copy-start(bf16[512,512]{1,0:T(8,128)(2,1)S(1)} %get-tuple-element.56.ov) | copy-start | bytes 1572868
  215.0 0.8 copy-start.5
  215.8 1.0 copy-start.9
  390.0 1.0 copy-start.6
  391.1 1.0 copy-start.8
  392.1 1.2 copy-start.10
  393.3 1.0 copy-start.18
  404.9 1.0 copy-start.11
  405.8 1.0 copy-start.12
  406.8 1.0 copy-start.13
  407.9 0.8 copy-start.15
  408.6 0.8 copy-start.16
  474.2 135.7 %copy-start.21 = (bf16[128,2048]{1,0:T(8,128)(2,1)S(1)}, bf16[128,2048]{1,0:T(8,128)(2,1)}, u32[]{:S(2)}) copy-start(bf16[128,2048]{1,0:T(8,128)(2,1)} %get-tuple-element.137) | copy-start | bytes 1572868
  610.7 10.8 %copy-start.24 = (f32[8,2048]{1,0:T(8,128)S(1)}, f32[8,2048]{1,0:T(8,128)}, u32[]{:S(2)}) copy-start(f32[8,2048]{1,0:T(8,128)} %get-tuple-element.83) | copy-start | bytes 196612
  610.7 11.5 %copy-start.23 = (f32[128,1024]{1,0:T(8,128)S(1)}, f32[128,1024]{1,0:T(8,128)}, u32[]{:S(2)}) copy-start(f32[128,1024]{1,0:T(8,128)} %get-tuple-element.144) | copy-start | bytes 1572868
  610.7 12.3 %copy-start.22 = (f32[128,1024]{1,0:T(8,128)S(1)}, f32[128,1024]{1,0:T(8,128)}, u32[]{:S(2)}) copy-start(f32[128,1024]{1,0:T(8,128)} %get-tuple-element.145) | copy-start | bytes 1572868
  (1 other events, 0.8 us)

commit v4 on v3

--- a/solution.py
+++ b/solution.py
@@ -1,5 +1,6 @@
 import jax
 import jax.numpy as jnp
+import numpy as np
 from jax import lax
 from jax.experimental import pallas as pl
 from jax.experimental.pallas import tpu as pltpu
@@ -70,8 +71,10 @@
 
 MESH = pl.DeviceIdType.MESH
 ANY = pl.BlockSpec(memory_space=pl.ANY)
+HBM = pl.BlockSpec(memory_space=pltpu.HBM)
 BF16 = jnp.bfloat16
 BLOCK = 128
+VMEM_LIMIT = 62 * 2**20
 
 
 def coords():
@@ -136,7 +139,8 @@
 
 
 VMEM = pl.BlockSpec(memory_space=pltpu.VMEM)
-SIDE_ROWS = 136
+SIDE_ROWS = 112
+MIXERS = 104
 
 
 def exchange(src, slots, mine, peers, send, recv, first):
@@ -228,15 +232,16 @@
     return greeted, start, relay_z, relay_y, finish
 
 
-def collect(history, small, up, top_weights, bottom_weights):
+def collect(history, small, up, layer_ids, mix_weights):
     slots, _, width = history.shape
+    layers = mix_weights.shape[1]
     half = BLOCK // 2
     step = 16
     lanes = 128
 
     def kernel(
-        hist, wa, wb, tw, bw, streams, top_out, bottom_out, full_a, full_b,
-        top, bottom, acc, part_x, got_x, part_z, got_z,
+        hist, wa, wb, ids, given, streams, top_out, bottom_out, full_a, full_b, tw, bw,
+        top, bottom, acc, far_part, hop, part_x, got_x, part_z, got_z,
         wsend, wrecv, send, recv, local, store,
     ):
         here = coords()
@@ -273,14 +278,43 @@
             for k in (1, 3, 2):
                 push(rows(k, other, 0), top.at[other, 4 - k], 4 + 3 * other + 3 - k, peers[k])
 
+        def columns_of(slots_here, owner, low, into):
+            cols = pl.ds(pl.multiple_of(owner * BLOCK, BLOCK), BLOCK)
+            column = lax.broadcasted_iota(jnp.int32, (lanes, layers), 0)
+            layer = lax.broadcasted_iota(jnp.int32, (lanes, layers), 1)
+            wanted = jnp.full((lanes, layers), -1, jnp.int32)
+            for i, slot in enumerate(slots_here):
+                wanted = jnp.where(column // 4 == i, ids[slot], wanted)
+            total = jnp.zeros((lanes, BLOCK), jnp.float32)
+            for s in range(4):
+                pick = jnp.where((layer == wanted) & (column % 4 == s), 1.0, 0.0)
+                total = total + lax.dot_general(
+                    pick,
+                    given[s, :, cols],
+                    (((1,), (0,)), ((), ())),
+                    precision=HIGHEST,
+                    preferred_element_type=jnp.float32,
+                )
+            into[...] = jnp.transpose(total)[low * half : (low + 1) * half]
+
+        for other in range(2):
+            owner = x * 2 + (1 - zl if other else zl)
+            columns_of([(x + k) % 4 * 6 + zl * 3 + j for k in range(4) for j in range(3)], owner, 0, tw.at[other])
+        for k in range(4):
+            wanted_slots = [x * 6 + (1 - zl if r else zl) * 3 + j for r in range(2) for j in range(3)]
+            columns_of(wanted_slots, (x + k) % 4 * 2 + zl, 1, bw.at[k])
+
         def mix(entries, factors_of, groups, into, offset):
             def some_rows(r, carry):
                 at = pl.ds(pl.multiple_of(r * step, step), step)
                 there = pl.ds(pl.multiple_of(offset + r * step, step), step)
                 for g in range(groups):
                     factors = [
-                        [jnp.broadcast_to(factors_of(g * 3 + e, at)[:, s : s + 1], (step, lanes)) for s in range(4)]
-                        for e in range(3)
+                        [
+                            jnp.broadcast_to(factors_of(at)[:, i * 4 + s : i * 4 + s + 1], (step, lanes))
+                            for s in range(4)
+                        ]
+                        for i in range(g * 3, g * 3 + 3)
                     ]
 
                     def some_cols(b, inner, g=g, factors=factors):
@@ -297,10 +331,10 @@
             lax.fori_loop(0, half // step, some_rows, 0)
 
         def mix_top(other, into, offset):
-            mix(lambda g, e: top.at[other, g, e], lambda i, at: tw[other, i, at, :], 4, into, offset)
+            mix(lambda g, e: top.at[other, g, e], lambda at: tw[other, at, :], 4, into, offset)
 
         def mix_bottom(k, into, offset):
-            mix(lambda g, e: bottom.at[k, g, e], lambda i, at: bw[k, i, at, :], 2, into, offset)
+            mix(lambda g, e: bottom.at[k, g, e], lambda at: bw[k, at, :], 2, into, offset)
 
         stores = []
 
@@ -316,8 +350,18 @@
                 mix_bottom(0, streams, half)
                 return
             mix_bottom(k, acc, 0)
-            part_x[k - 1] = acc[...].astype(BF16)
-            push(part_x.at[k - 1], got_x.at[3 - k], 10 + 3 - k, peers[k])
+            if k == 2:
+                far_part[...] = acc[...].astype(BF16)
+                push(far_part.at[:, pl.ds(0, half // 2)], hop.at[0], 14, peers[1])
+                push(far_part.at[:, pl.ds(half // 2, half // 2)], hop.at[1], 15, peers[3])
+                return
+            side = 0 if k == 1 else 1
+            came(hop.at[side], 14 + side)
+            merged = pl.ds(side * (half // 2), half // 2)
+            for s in range(4):
+                acc[s, merged] = acc[s, merged] + hop[side, s].astype(jnp.float32)
+            part_x[side] = acc[...].astype(BF16)
+            push(part_x.at[side], got_x.at[side], 10 + side, peers[k])
 
         relay_z()
         bottom_sums(2)
@@ -356,9 +400,9 @@
             lax.fori_loop(0, half // step, lambda r, carry: add(r, carry, offset, parts), 0)
 
         add_all(0, [lambda s, at: got_z[s, at, :].astype(jnp.float32)])
-        for k in (1, 2, 3):
-            came(got_x.at[k - 1], 10 + k - 1)
-        add_all(half, [lambda s, at, k=k: got_x[k, s, at, :].astype(jnp.float32) for k in range(3)])
+        for side in range(2):
+            came(got_x.at[side], 10 + side)
+        add_all(half, [lambda s, at, k=k: got_x[k, s, at, :].astype(jnp.float32) for k in range(2)])
         finish()
         for copy in kept + stores:
             copy.wait()
@@ -379,29 +423,33 @@
             shape(bottom_shape),
             shape((n_a, rows_a * 16, cols_a * 2)),
             shape((n_b, rows_b * 16, cols_b * 2)),
+            shape((2, half, lanes), jnp.float32),
+            shape((4, half, lanes), jnp.float32),
         ],
-        in_specs=[ANY, ANY, ANY, VMEM, VMEM],
-        out_specs=[VMEM, ANY, ANY, ANY, ANY],
+        in_specs=[ANY, ANY, ANY, pl.BlockSpec(memory_space=pltpu.SMEM), VMEM],
+        out_specs=[VMEM, HBM, HBM, HBM, HBM, VMEM, VMEM],
         scratch_shapes=[
             vmem(top_shape, BF16),
             vmem(bottom_shape, BF16),
             vmem(piece, jnp.float32),
-            vmem((3,) + piece, BF16),
-            vmem((3,) + piece, BF16),
+            vmem(piece, BF16),
+            vmem((2, 4, half // 2, width), BF16),
+            vmem((2,) + piece, BF16),
+            vmem((2,) + piece, BF16),
             vmem(piece, BF16),
             vmem(piece, BF16),
             sem((64,)),
             sem((64,)),
-            sem((14,)),
-            sem((14,)),
+            sem((16,)),
+            sem((16,)),
             sem((8,)),
             sem((6,)),
         ],
         compiler_params=pltpu.CompilerParams(
-            collective_id=1, has_side_effects=True, vmem_limit_bytes=48 * 2**20
+            collective_id=1, has_side_effects=True, vmem_limit_bytes=VMEM_LIMIT
         ),
         name="collect",
-    )(history, small, up, top_weights, bottom_weights)
+    )(history, small, up, layer_ids, mix_weights)
 
 
 def dot_nt(left, right):
@@ -416,97 +464,111 @@
     return lax.dot_general(left, right, (((0,), (0,)), ((), ())), preferred_element_type=jnp.float32)
 
 
-def attend(queries, keys, values, other_keys, other_values, query_at, key_at):
-    rows, cols = queries.shape
-    heads = cols // HD
+def token_places(docs, zl):
+    rows = docs[...].astype(jnp.float32)
+    cols = jnp.transpose(rows)
+    first = zl == 0
+    queries = [[], []]
+    keys = [[], [], [], []]
+    down = lax.broadcasted_iota(jnp.int32, (BLOCK, 1), 0)
+    along = lax.broadcasted_iota(jnp.int32, (1, BLOCK), 1)
+    for p in range(4):
+        even, odd = cols[:, 2 * p : 2 * p + 1], cols[:, 2 * p + 1 : 2 * p + 2]
+        queries[0].append((down + (2 * p + zl) * BLOCK).astype(jnp.float32))
+        queries[1].append(jnp.where(first, even, odd))
+        even, odd = rows[2 * p : 2 * p + 1], rows[2 * p + 1 : 2 * p + 2]
+        for side, low in ((0, zl), (1, 1 - zl)):
+            keys[2 * side].append((along + (2 * p + low) * BLOCK).astype(jnp.float32))
+        keys[1].append(jnp.where(first, even, odd))
+        keys[3].append(jnp.where(first, odd, even))
+    return (
+        [jnp.concatenate(part, axis=0) for part in queries],
+        [jnp.concatenate(part, axis=1) for part in keys],
+    )
+
+
+def allowed_keys(query_pos, query_doc, keys, side):
+    return (keys[2 * side] <= query_pos) & (keys[2 * side + 1] == query_doc)
+
+
+def attend(q, k, v, ok, ov, places, keys, out, lse):
+    rows, cols = q.shape
     scale = HD ** (-0.5)
     tall = 256
 
-    def kernel(q, k, v, ok, ov, qa, ka, out, lse):
+    def one_head(h, carry):
+        head = pl.ds(pl.multiple_of(h * HD, HD), HD)
         for r in range(rows // tall):
             at = pl.ds(r * tall, tall)
-            query_pos, query_doc = qa[at, 0:1], qa[at, 1:2]
+            query_pos, query_doc = places[at, 0:1], places[at, 1:2]
             scores = []
-            for half, key in enumerate((k, ok)):
-                allowed = (ka[2 * half : 2 * half + 1, :] <= query_pos) & (
-                    ka[2 * half + 1 : 2 * half + 2, :] == query_doc
-                )
-                scores.append(jnp.where(allowed, dot_nt(q[at, :], key[...]) * scale, NEGATIVE))
+            for side, key in enumerate((k, ok)):
+                allowed = allowed_keys(query_pos, query_doc, keys, side)
+                scores.append(jnp.where(allowed, dot_nt(q[at, head], key[:, head]) * scale, NEGATIVE))
             top = jnp.maximum(
                 jnp.max(scores[0], axis=1, keepdims=True), jnp.max(scores[1], axis=1, keepdims=True)
             )
             shifted = [jnp.exp(part - top) for part in scores]
             total = jnp.sum(shifted[0], axis=1, keepdims=True) + jnp.sum(shifted[1], axis=1, keepdims=True)
             share = 1.0 / total
-            result = dot_nn((shifted[0] * share).astype(BF16), v[...])
-            result = result + dot_nn((shifted[1] * share).astype(BF16), ov[...])
-            out[at, :] = result.astype(BF16)
-            lse[0, at, :] = top + jnp.log(total)
-
-    head = pl.BlockSpec((rows, HD), lambda h: (0, h))
-    return pl.pallas_call(
-        kernel,
-        grid=(heads,),
-        out_shape=[shape((rows, cols)), shape((heads, rows, 1), jnp.float32)],
-        in_specs=[head] * 5
-        + [pl.BlockSpec(query_at.shape, lambda h: (0, 0)), pl.BlockSpec(key_at.shape, lambda h: (0, 0))],
-        out_specs=[head, pl.BlockSpec((1, rows, 1), lambda h: (h, 0, 0))],
-        compiler_params=pltpu.CompilerParams(vmem_limit_bytes=40 * 2**20),
-        name="attend",
-    )(queries, keys, values, other_keys, other_values, query_at, key_at)
-
-
-def attend_back(queries, keys, values, other_keys, other_values, query_at, key_at, log_totals, out_cot):
-    rows, cols = queries.shape
-    heads = cols // HD
+            result = dot_nn((shifted[0] * share).astype(BF16), v[:, head])
+            result = result + dot_nn((shifted[1] * share).astype(BF16), ov[:, head])
+            out[at, head] = result.astype(BF16)
+            lane = lax.broadcasted_iota(jnp.int32, (tall, HD), 1)
+            lse[at, :] = jnp.where(lane == h, top + jnp.log(total), lse[at, :])
+        return carry
+
+    lax.fori_loop(0, cols // HD, one_head, 0)
+
+
+def attend_back(q, k, v, ok, ov, places, keys, lse, cot, dq, dk, dv, dok, dov, key_sum, value_sum, finish):
+    rows, cols = q.shape
     scale = HD ** (-0.5)
     tall = 256
 
-    def kernel(q, k, v, ok, ov, qa, ka, lse, cot, dq, dk, dv, dok, dov, key_sum, value_sum):
+    def one_head(h, carry):
+        head = pl.ds(pl.multiple_of(h * HD, HD), HD)
         for r in range(rows // tall):
             at = pl.ds(r * tall, tall)
-            query_pos, query_doc = qa[at, 0:1], qa[at, 1:2]
+            query_pos, query_doc = places[at, 0:1], places[at, 1:2]
+            lane = lax.broadcasted_iota(jnp.int32, (tall, HD), 1)
+            log_total = jnp.sum(jnp.where(lane == h, lse[at, :], 0.0), axis=1, keepdims=True)
             probs, prob_grads = [], []
-            for half, (key, value) in enumerate(((k, v), (ok, ov))):
-                allowed = (ka[2 * half : 2 * half + 1, :] <= query_pos) & (
-                    ka[2 * half + 1 : 2 * half + 2, :] == query_doc
-                )
-                scores = jnp.where(allowed, dot_nt(q[at, :], key[...]) * scale, NEGATIVE)
-                probs.append(jnp.exp(scores - lse[0, at, :]))
-                prob_grads.append(dot_nt(cot[at, :], value[...]))
+            for side, (key, value) in enumerate(((k, v), (ok, ov))):
+                allowed = allowed_keys(query_pos, query_doc, keys, side)
+                scores = jnp.where(allowed, dot_nt(q[at, head], key[:, head]) * scale, NEGATIVE)
+                probs.append(jnp.exp(scores - log_total))
+                prob_grads.append(dot_nt(cot[at, head], value[:, head]))
             row_dot = sum(jnp.sum(p * g, axis=1, keepdims=True) for p, g in zip(probs, prob_grads))
             query_grad = jnp.zeros((tall, HD), jnp.float32)
-            for half, (p, g) in enumerate(zip(probs, prob_grads)):
+            for side, (p, g) in enumerate(zip(probs, prob_grads)):
                 score_cot = (p * (g - row_dot)).astype(BF16)
-                key = (k, ok)[half]
-                query_grad = query_grad + dot_nn(score_cot, key[...])
-                key_part = dot_tn(score_cot, q[at, :])
-                value_part = dot_tn(p.astype(BF16), cot[at, :])
+                key = (k, ok)[side]
+                query_grad = query_grad + dot_nn(score_cot, key[:, head])
+                key_part = dot_tn(score_cot, q[at, head])
+                value_part = dot_tn(p.astype(BF16), cot[at, head])
                 if r == 0:
-                    key_sum[half] = key_part
-                    value_sum[half] = value_part
+                    key_sum[side] = key_part
+                    value_sum[side] = value_part
                 else:
-                    key_sum[half] += key_part
-                    value_sum[half] += value_part
-            dq[at, :] = query_grad * scale
-        dk[...] = key_sum[0] * scale
-        dv[...] = value_sum[0]
-        dok[...] = (key_sum[1] * scale).astype(BF16)
-        dov[...] = value_sum[1].astype(BF16)
-
-    head = pl.BlockSpec((rows, HD), lambda h: (0, h))
-    return pl.pallas_call(
-        kernel,
-        grid=(heads,),
-        out_shape=[shape((rows, cols), jnp.float32)] * 3 + [shape((rows, cols))] * 2,
-        in_specs=[head] * 5
-        + [pl.BlockSpec(query_at.shape, lambda h: (0, 0)), pl.BlockSpec(key_at.shape, lambda h: (0, 0))]
-        + [pl.BlockSpec((1, rows, 1), lambda h: (h, 0, 0)), head],
-        out_specs=[head] * 5,
-        scratch_shapes=[pltpu.VMEM((2, rows, HD), jnp.float32)] * 2,
-        compiler_params=pltpu.CompilerParams(vmem_limit_bytes=40 * 2**20),
-        name="attend_back",
-    )(queries, keys, values, other_keys, other_values, query_at, key_at, log_totals, out_cot)
+                    key_sum[side] += key_part
+                    value_sum[side] += value_part
+            dq[at, head] = query_grad * scale
+        dk[:, head] = key_sum[0] * scale
+        dv[:, head] = value_sum[0]
+        dok[:, head] = (key_sum[1] * scale).astype(BF16)
+        dov[:, head] = value_sum[1].astype(BF16)
+        finish(h)
+        return carry
+
+    lax.fori_loop(0, cols // HD, one_head, 0)
+
+
+def set_places(docs, zl, places):
+    queries, keys = token_places(docs, zl)
+    lane = lax.broadcasted_iota(jnp.int32, places.shape, 1)
+    places[...] = jnp.where(lane == 0, queries[0], jnp.where(lane == 1, queries[1], 0.0))
+    return keys
 
 
 def erf(value):
@@ -545,14 +607,16 @@
     half = BLOCK // 2
     tile = 2 * BLOCK
     tiles = width // tile
+    mixers = da_out.shape[0]
 
     def kernel(
-        heads, small, up, down, stream, gains, da_in, da_out, da_bias, out_grad, mix_cot_in,
-        block_out, mix_next, residual_grad, heads_cot, gain_grads, side_sum, other, out_proj_grad, up_sum, down_sum,
+        heads, small, up, down, stream_in, gains, in_given, net_given, bias_given, out_grad, mix_given,
+        block_out, mix_next, residual_grad, heads_cot, gain_grads, other, out_proj_grad, up_sum, down_sum,
+        in_grad, net_grad, bias_grad,
         w_out, w_up, w_down, mid_all, active, slope, cot_all, up_cot, attn_cot,
         part, got1, got3, own, residual, unit, total, flat, aux, inv, grad_stage, sums,
-        y_slots, z_part, z_slots, c_part, c_slot, x_slots, result,
-        load, send, recv, gsend, grecv, gkeep, sends, recvs, dload,
+        y_slots, z_part, z_slots, c_part, c_slot, x_slots, result, side_sum,
+        stream, da_in, padded, load, send, recv, gsend, grecv, gkeep, sends, recvs, dload,
     ):
         x, zl, zh, y, c = coords()
         z = zh * 2 + zl
@@ -566,6 +630,7 @@
             pltpu.make_async_copy(small.at[3], w_out, load.at[0]),
             pltpu.make_async_copy(up.at[0], w_up, load.at[1]),
             pltpu.make_async_copy(down.at[0], w_down, load.at[2]),
+            pltpu.make_async_copy(stream_in.at[3], stream, load.at[3]),
         ]
         for copy in loads:
             copy.start()
@@ -646,10 +711,19 @@
         for k in (2, 1, 3, 0):
             place = x if k == 0 else places[k]
             give_part(0, k, got1, dot_nt(heads[block(place), :], w_out[...]))
+        aux[...] = jnp.zeros_like(aux)
+        aux[:mixers, :] = in_given[...].astype(jnp.float32)
+        da_in[...] = aux[...].astype(BF16)
+        padded[...] = jnp.zeros_like(padded)
+        padded[0, :mixers, :mixers] = net_given[...].astype(jnp.float32)
+        padded[1, :1, :mixers] = bias_given[...]
+        padded[2, :mixers, :] = mix_given[...]
+        padded[2] = jnp.transpose(padded[2])
+        loads[3].wait()
         arrived(0, got1)
 
         def to_mid(at, there):
-            value = stream[3, at, :] + own[at, :]
+            value = stream[at, :] + own[at, :]
             for k in range(3):
                 value = value + got1[k, at, :].astype(jnp.float32)
             residual[at, :] = value
@@ -670,9 +744,9 @@
             total[...] = dot_nn(mid_all[block(place), :], w_up[...])
 
             def bend(at, there):
-                value, change = gelu_both(total[at, :])
-                active[there, :] = value.astype(BF16)
-                slope[there, :] = change.astype(slope.dtype)
+                value = total[at, :]
+                active[there, :] = (0.5 * value * (1.0 + erf(value * 0.7071067811865476))).astype(BF16)
+                slope[there, :] = value
 
             chunks(bend, place)
             if not waited:
@@ -681,6 +755,13 @@
             give_part(1, k, got3, dot_nt(active[block(place), :], w_down[...]))
 
         gathered(mid_all, 9, feed)
+
+        def bend_more(r, carry):
+            at = pl.ds(pl.multiple_of(r * step, step), step)
+            slope[at, :] = gelu_both(slope[at, :])[1]
+            return carry
+
+        lax.fori_loop(0, rows_all // step, bend_more, 0)
         arrived(1, got3)
 
         def to_out(at, _):
@@ -694,12 +775,13 @@
             flat[at, :] = (value * scale * gains[4:5, :]).astype(BF16)
 
         chunks(to_out)
-        inner_act, inner_slope = gelu_both(dot_nn(flat[...], da_in[...]))
+        da_out = padded[0].astype(BF16)
+        inner_act, inner_slope = gelu_both(dot_nt(flat[...], da_in[...]))
         inner_act = inner_act.astype(BF16)
-        mix_next[...] = dot_nn(inner_act, da_out[...]) + da_bias[...]
-        mix_cot = mix_cot_in[...].astype(BF16)
-        inner_cot = (dot_nt(mix_cot, da_out[...]) * inner_slope).astype(BF16)
-        aux[...] = dot_nt(inner_cot, da_in[...])
+        mix_next[...] = jnp.transpose(dot_nn(inner_act, da_out) + padded[1, :1, :])[:mixers]
+        mix_cot = padded[2].astype(BF16)
+        inner_cot = (dot_nt(mix_cot, da_out) * inner_slope).astype(BF16)
+        aux[...] = dot_nn(inner_cot, da_in[...])
         sums[...] = jnp.zeros_like(sums)
 
         def to_cot(at, there):
@@ -718,21 +800,18 @@
         chunks(to_cot, x)
 
         def small_grads():
-            grad = dot_tn(flat[...], inner_cot)
-            c_rows = SIDE_ROWS
-            bias = jnp.sum(mix_cot_in[...], axis=0, keepdims=True)
-            tail = jnp.concatenate(
-                [
-                    dot_tn(inner_act, mix_cot)[:104],
-                    jnp.where(lax.broadcasted_iota(jnp.int32, (24, BLOCK), 0) == 0, bias, 0.0),
-                ],
-                axis=0,
-            )
-            whole = jnp.concatenate([grad, tail], axis=0)
-            for py in range(4):
-                for pz in range(4):
-                    begin = (py * 4 + pz) * c_rows
-                    result[py, pz] = whole[begin : begin + c_rows]
+            aux[...] = dot_tn(inner_cot, flat[...])
+            net = dot_tn(inner_act, mix_cot)
+            bias = jnp.sum(padded[2], axis=0, keepdims=True)
+            row = lax.broadcasted_iota(jnp.int32, (8, BLOCK), 0)
+            for i in range(16):
+                place = (i // 4, i % 4)
+                result[place + (slice(0, MIXERS),)] = aux[:MIXERS, i * BLOCK : (i + 1) * BLOCK]
+                if i < MIXERS // 8:
+                    tail = net[i * 8 : (i + 1) * 8]
+                else:
+                    tail = jnp.where(row == 0, bias, 0.0)
+                result[place + (slice(MIXERS, SIDE_ROWS),)] = tail
 
         side = {}
 
@@ -926,6 +1005,13 @@
         out_grad_copy(tiles - 1).wait()
         for copy in side[5]:
             copy.wait()
+        for i in range(16):
+            chunk = side_sum[i // 4, i % 4]
+            in_grad[:, i * BLOCK : (i + 1) * BLOCK] = chunk[:mixers]
+            if i < MIXERS // 8:
+                count = min(8, mixers - i * 8)
+                net_grad[i * 8 : i * 8 + count, :] = chunk[MIXERS : MIXERS + count, :mixers]
+        bias_grad[...] = side_sum[3, 3, MIXERS : MIXERS + 1, :mixers]
         up_done = add_cores(0)
         down_done.wait()
         up_done.wait()
@@ -940,18 +1026,20 @@
         kernel,
         out_shape=[
             shape((BLOCK, width)),
-            shape((BLOCK, BLOCK), f32),
+            shape((mixers, BLOCK), f32),
             shape((BLOCK, width), f32),
             shape(heads.shape),
             shape((2, width), f32),
-            shape((4, 4) + piece, f32),
             shape((2, tiles, BLOCK, hidden)),
             shape((width, head_cols)),
             shape((tiles * BLOCK, hidden)),
             shape((tiles * BLOCK, hidden)),
+            shape((mixers, width), f32),
+            shape((mixers, mixers), f32),
+            shape((1, mixers), f32),
         ],
-        in_specs=[VMEM, ANY, ANY, ANY] + [VMEM] * 7,
-        out_specs=[VMEM] * 6 + [ANY] * 4,
+        in_specs=[VMEM, HBM, HBM, HBM, HBM] + [VMEM] * 6,
+        out_specs=[VMEM] * 5 + [HBM] * 4 + [VMEM] * 3,
         scratch_shapes=[
             vmem((width, head_cols), BF16),
             vmem((width, hidden), BF16),
@@ -981,7 +1069,11 @@
             vmem(piece, f32),
             vmem((4,) + piece, f32),
             vmem((4, 4) + piece, f32),
-            pltpu.SemaphoreType.DMA((3,)),
+            vmem((4, 4) + piece, f32),
+            vmem((BLOCK, width), f32),
+            vmem((BLOCK, width), BF16),
+            vmem((3, BLOCK, BLOCK), f32),
+            pltpu.SemaphoreType.DMA((4,)),
             pltpu.SemaphoreType.DMA((27,)),
             pltpu.SemaphoreType.DMA((27,)),
             pltpu.SemaphoreType.DMA((2 * tiles,)),
@@ -992,13 +1084,13 @@
             pltpu.SemaphoreType.DMA((2 * tiles,)),
         ],
         compiler_params=pltpu.CompilerParams(
-            collective_id=4, has_side_effects=True, vmem_limit_bytes=62 * 2**20
+            collective_id=4, has_side_effects=True, vmem_limit_bytes=VMEM_LIMIT
         ),
         name="middle",
     )(heads, small, up, down, stream, gains, da_in, da_out, da_bias, out_grad, mix_cot_in)
 
 
-def project(streams, gains, small, tables, down):
+def project(streams, gains, small, tables, down, docs):
     width = streams.shape[2]
     cols = small.shape[2]
     rows_all = 4 * BLOCK
@@ -1007,9 +1099,9 @@
     order = (1, 2, 0)
 
     def kernel(
-        streams, gains, small, tables, down,
-        queries, keys, values, other_keys, other_values, normed_out, full_down,
-        weights, normed, load, send, recv, zsend, zrecv, local, wsend, wrecv,
+        streams_in, gains, small, tables_in, down, docs,
+        queries_out, keys_out, values_out, other_keys_out, other_values_out, heads, lse_out, normed_out, full_down,
+        queries, keys, values, other_keys, other_values, lse, streams, tables, places_in, weights, normed, load, send, recv, zsend, zrecv, local, wsend, wrecv,
     ):
         x, zl, zh, y, c = coords()
         partner = device(x, 1 - zl, zh, y, c)
@@ -1017,7 +1109,9 @@
         right, left, far = places[1], places[3], places[2]
         peers = {k: device(places[k], zl, zh, y, c) for k in (1, 3)}
         loads = [pltpu.make_async_copy(small.at[i], weights.at[i], load.at[i]) for i in range(3)]
-        for i in order:
+        loads += [pltpu.make_async_copy(streams_in.at[i], streams.at[i], load.at[3 + i]) for i in range(3)]
+        loads.append(pltpu.make_async_copy(tables_in.at[:, :, zl], tables, load.at[6]))
+        for i in (4, 5, 3, 6, 1, 2, 0):
             loads[i].start()
         greeted, start, relay_z, relay_y, finish = weight_gather(
             (down,), (full_down,), (x, zl, zh, y, c), wsend, wrecv, 0
@@ -1051,6 +1145,7 @@
                 normed[i, there, :] = (centered * scale * gains[i : i + 1, :]).astype(BF16)
                 return carry
 
+            loads[3 + i].wait()
             lax.fori_loop(0, BLOCK // step, norm, 0)
             push(i, 0, x, True, peers[1])
             push(i, 2, x, False, peers[3])
@@ -1069,7 +1164,7 @@
                 for h in range(cols // HD):
                     part = result[:, h * HD : (h + 1) * HD]
                     ahead, behind = pltpu.roll(part, HD - ROT // 2, 1), pltpu.roll(part, ROT // 2, 1)
-                    turned = part * tables[0, at, :] + ahead * tables[1, at, :] + behind * tables[2, at, :]
+                    turned = part * tables[0, place] + ahead * tables[1, place] + behind * tables[2, place]
                     out[at, h * HD : (h + 1) * HD] = turned.astype(BF16)
             if i > 0:
                 j = len(given)
@@ -1077,10 +1172,13 @@
                 given.append(remote(out.at[block(place)], other.at[block(place)], zsend.at[j], zrecv.at[j], partner))
                 given[-1].start()
 
+        loads[6].wait()
         for i in order:
             loads[i].wait()
             work(i, x)
         relay_z()
+        key_places = set_places(docs, zl, places_in)
+        lse[...] = jnp.zeros_like(lse)
         for i in order:
             copies[i, 0].wait_recv()
             push(i, 4, left, True, peers[1])
@@ -1099,8 +1197,18 @@
             stores[-1].start()
             work(i, far)
         relay_y(3)
+        for copy in given:
+            copy.wait()
+        kept_here = (queries, keys, values, other_keys, other_values)
+        outs = (queries_out, keys_out, values_out, other_keys_out, other_values_out)
+        for i, (src, dst) in enumerate(zip(kept_here, outs)):
+            stores.append(pltpu.make_async_copy(src, dst, local.at[4 + i]))
+            stores[-1].start()
+        attend(queries, keys, values, other_keys, other_values, places_in, key_places, heads, lse)
+        stores.append(pltpu.make_async_copy(lse, lse_out, local.at[9]))
+        stores[-1].start()
         finish()
-        for copy in given + stores + kept:
+        for copy in stores + kept:
             copy.wait()
         for copy in copies.values():
             copy.wait_send()
@@ -1109,31 +1217,40 @@
     sem = pltpu.SemaphoreType.DMA
     return pl.pallas_call(
         kernel,
-        out_shape=[shape((rows_all, cols))] * 5
-        + [shape((3, rows_all, width)), shape((1, down.shape[1] * 16, down.shape[2] * 2))],
-        in_specs=[VMEM, VMEM, ANY, VMEM, ANY],
-        out_specs=[VMEM] * 5 + [ANY, ANY],
-        scratch_shapes=[
+        out_shape=[shape((rows_all, cols))] * 6
+        + [
+            shape((rows_all, HD), jnp.float32),
+            shape((3, rows_all, width)),
+            shape((1, down.shape[1] * 16, down.shape[2] * 2)),
+        ],
+        in_specs=[HBM, VMEM, HBM, HBM, ANY, VMEM],
+        out_specs=[HBM] * 5 + [VMEM] + [HBM] * 3,
+        scratch_shapes=[vmem((rows_all, cols), BF16)] * 5
+        + [
+            vmem((rows_all, HD), jnp.float32),
+            vmem((3, BLOCK, width), jnp.float32),
+            vmem((3, 4, BLOCK, HD), jnp.float32),
+            vmem((rows_all, HD), jnp.float32),
             vmem((3, width, cols), BF16),
             vmem((3, rows_all, width), BF16),
-            sem((3,)),
+            sem((7,)),
             sem((18,)),
             sem((18,)),
             sem((8,)),
             sem((8,)),
-            sem((4,)),
+            sem((10,)),
             sem((32,)),
             sem((32,)),
         ],
         compiler_params=pltpu.CompilerParams(
-            collective_id=2, has_side_effects=True, vmem_limit_bytes=40 * 2**20
+            collective_id=2, has_side_effects=True, vmem_limit_bytes=VMEM_LIMIT
         ),
         name="project",
-    )(streams, gains, small, tables, down)
-
-
-def inward(grads, gives, small, normed, out_proj_grad, streams, residual_grad, gains, late_gains, tables, down):
-    rows_all, cols = grads[0].shape
+    )(streams, gains, small, tables, down, docs)
+
+
+def inward(attention, lse, heads_cot, docs, small, normed, out_proj_grad, streams, residual_grad, gains, late_gains, tables, down):
+    rows_all, cols = heads_cot.shape
     width = streams.shape[2]
     step = 16
     half = BLOCK // 2
@@ -1143,11 +1260,13 @@
     thin = hidden // 2
 
     def kernel(
-        dq, dk, dv, give_k, give_v, small, normed, out_proj_grad, streams, residual_grad, gains, late, tables,
-        down,
+        q_in, k_in, v_in, ok_in, ov_in, lse_in, cot, docs, small, normed, out_proj_grad, streams, residual_grad,
+        gains, late,
+        tables_in, down,
         stream_cot, gain_grads, small_sum, down_out,
         weights, inputs, cots, got_k, got_v, far_part, near, hop, got, own, grad, swapped, sums, down_y, down_part, down_z, stream,
-        load, send, recv, ssend, srecv, gsend, grecv, local,
+        tables, places_in, dq, dk, dv, give_k, give_v, key_sum, value_sum, q, k, v, ok, ov, lse,
+        ksend, krecv, load, send, recv, ssend, srecv, gsend, grecv, local,
     ):
         x, zl, zh, y, c = coords()
         z = zh * 2 + zl
@@ -1157,10 +1276,19 @@
         sibling = device(x, zl, zh, y, 1 - c)
         places = {k: (x + k) % 4 for k in (1, 2, 3)}
         peers = {k: device(places[k], zl, zh, y, c) for k in (1, 3)}
+        early = [
+            pltpu.make_async_copy(src, dst, load.at[9 + i])
+            for i, (src, dst) in enumerate(
+                ((q_in, q), (k_in, k), (v_in, v), (ok_in, ok), (ov_in, ov), (lse_in, lse))
+            )
+        ]
+        for copy in early:
+            copy.start()
         loads = [pltpu.make_async_copy(small.at[i], weights.at[i], load.at[i]) for i in range(3)]
         loads += [pltpu.make_async_copy(normed.at[i], inputs.at[i], load.at[3 + i]) for i in range(3)]
         loads.append(pltpu.make_async_copy(out_proj_grad, grad.at[0], load.at[6]))
         loads.append(pltpu.make_async_copy(streams.at[pl.ds(0, 3)], stream, load.at[7]))
+        loads.append(pltpu.make_async_copy(tables_in.at[:, :, zl], tables, load.at[8]))
         for copy in loads:
             copy.start()
         greet([peers[1], peers[3], sibling] + [peer for _, peer in along_z + along_y])
@@ -1171,8 +1299,6 @@
             sides.append(remote(src, dst, ssend.at[i], srecv.at[i], peer))
             sides[-1].start()
 
-        side(give_k, got_k, partner)
-        side(give_v, got_v, partner)
         for py, peer in along_y:
             side(down.at[:, py], down_y.at[y], peer)
         locals_ = [pltpu.make_async_copy(down.at[:, y], down_y.at[y], local.at[0])]
@@ -1182,26 +1308,29 @@
         def block(place):
             return pl.ds(pl.multiple_of(place * BLOCK, BLOCK), BLOCK)
 
-        def turn_back(value):
+        def turn_back(value, place, there):
             def one(at):
                 part = value(at)
                 ahead, behind = pltpu.roll(part, HD - ROT // 2, 1), pltpu.roll(part, ROT // 2, 1)
-                return part * tables[0, at, :] - ahead * tables[1, at, :] - behind * tables[2, at, :]
+                table = [tables[t, place, there, :] for t in range(3)]
+                return part * table[0] - ahead * table[1] - behind * table[2]
 
             return one
 
         def to_cots(i, value):
             def one(r, carry):
                 at = pl.ds(pl.multiple_of(r * step, step), step)
+                per = BLOCK // step
+                there = pl.ds(pl.multiple_of(lax.rem(r, per) * step, step), step)
                 for h in range(cols // HD):
                     head = slice(h * HD, (h + 1) * HD)
-                    cots[i, at, head] = value(at, head).astype(BF16)
+                    cots[i, at, head] = value(at, head, lax.div(r, per), there).astype(BF16)
                 return carry
 
             lax.fori_loop(0, rows_all // step, one, 0)
 
         def turned(value):
-            return lambda at, head: turn_back(lambda at: value(at, head))(at)
+            return lambda at, head, place, there: turn_back(lambda at: value(at, head), place, there)(at)
 
         started = []
 
@@ -1278,17 +1407,37 @@
             weight_grad(i)
             swaps_of[i] = swaps[begin:]
 
+        key_places = set_places(docs, zl, places_in)
+        for copy in early:
+            copy.wait()
+
+        def swap(which, h):
+            head = pl.ds(pl.multiple_of(h * HD, HD), HD)
+            src, dst = (give_k, give_v)[which], (got_k, got_v)[which]
+            j = h * 2 + which
+            return remote(src.at[:, head], dst.at[:, head], ksend.at[j], krecv.at[j], partner)
+
+        def give_head(h):
+            swap(0, h).start()
+            swap(1, h).start()
+
+        attend_back(
+            q, k, v, ok, ov, places_in, key_places, lse, cot, dq, dk, dv, give_k, give_v, key_sum, value_sum, give_head
+        )
+        loads[8].wait()
         to_cots(0, turned(lambda at, head: dq[at, head]))
         far_sums(0)
         near_sums(0)
         grads_of(3)
         grads_of(0)
         own_sums(0)
-        sides[0].wait_recv()
+        for h in range(cols // HD):
+            swap(0, h).wait()
         to_cots(1, turned(lambda at, head: dk[at, head] + got_k[at, head].astype(jnp.float32)))
         far_sums(1)
-        sides[1].wait_recv()
-        to_cots(2, lambda at, head: dv[at, head] + got_v[at, head].astype(jnp.float32))
+        for h in range(cols // HD):
+            swap(1, h).wait()
+        to_cots(2, lambda at, head, place, there: dv[at, head] + got_v[at, head].astype(jnp.float32))
         far_sums(2)
         near_sums(1)
         near_sums(2)
@@ -1298,7 +1447,7 @@
         grads_of(2)
         own_sums(1)
         own_sums(2)
-        for copy in sides[2:] + locals_[:1]:
+        for copy in sides + locals_[:1]:
             copy.wait()
 
         def add_four(parts, places, dst):
@@ -1350,10 +1499,10 @@
             gain_grads[i : i + 1, :] = jnp.sum(sums[i], axis=0, keepdims=True)
         gain_grads[3:4, :] = late[1:2, :]
         gain_grads[4:5, :] = late[0:1, :]
-        for copy in sides[5:]:
+        for copy in sides[3:]:
             copy.wait()
         add_four(down_z, (), down_out)
-        for copy in started + sides[:2]:
+        for copy in started:
             copy.wait_send()
         for copy in locals_[1:]:
             copy.wait()
@@ -1369,8 +1518,8 @@
             shape((tiles, 4, BLOCK, cols)),
             shape((BLOCK, thin), f32),
         ],
-        in_specs=[VMEM] * 5 + [ANY] * 4 + [VMEM] * 4 + [ANY],
-        out_specs=[VMEM, VMEM, ANY, VMEM],
+        in_specs=[HBM] * 6 + [VMEM] * 2 + [HBM] * 4 + [VMEM] * 3 + [HBM] * 2,
+        out_specs=[VMEM, VMEM, HBM, VMEM],
         scratch_shapes=[
             vmem((3, width, cols), BF16),
             vmem((3, rows_all, width), BF16),
@@ -1389,7 +1538,22 @@
             vmem((2, BLOCK, hidden), BF16),
             vmem((4, BLOCK, thin), BF16),
             vmem((3, BLOCK, width), f32),
+            vmem((3, 4, BLOCK, HD), f32),
+            vmem((rows_all, HD), f32),
+            vmem((rows_all, cols), f32),
+            vmem((rows_all, cols), f32),
+            vmem((rows_all, cols), f32),
+            vmem((rows_all, cols), BF16),
+            vmem((rows_all, cols), BF16),
+            vmem((2, rows_all, HD), f32),
+            vmem((2, rows_all, HD), f32),
+        ]
+        + [vmem((rows_all, cols), BF16)] * 5
+        + [
+            vmem((rows_all, HD), f32),
             sem((8,)),
+            sem((8,)),
+            sem((15,)),
             sem((12,)),
             sem((12,)),
             sem((8,)),
@@ -1399,11 +1563,12 @@
             sem((5,)),
         ],
         compiler_params=pltpu.CompilerParams(
-            collective_id=5, has_side_effects=True, vmem_limit_bytes=60 * 2**20
+            collective_id=5, has_side_effects=True, vmem_limit_bytes=VMEM_LIMIT
         ),
         name="inward",
     )(
-        *grads, *gives, small, normed, out_proj_grad, streams, residual_grad, gains, late_gains, tables, down
+        *attention, lse, heads_cot, docs, small, normed, out_proj_grad, streams, residual_grad, gains, late_gains,
+        tables, down
     )
 
 
@@ -1417,8 +1582,8 @@
 
     def kernel(
         top_hist, bottom_hist, tw, bw, cot, gains, small, up,
-        out, top_mix, bottom_mix, gains_out, small_out, up_out,
-        top, bottom, top_stage, bottom_stage, cot_z, cot_x, mixes, turned,
+        out, mix_out, gains_out, three_out, last_out, up_out,
+        top, bottom, top_mix, bottom_mix, top_stage, bottom_stage, cot_z, cot_x, mixes, turned,
         x_slots, z_slots, y_slots, c_part, c_slot,
         small_y, small_part, small_z, up_y, up_part, up_z,
         load, csend, crecv, send, recv, msend, mrecv, local, sends, recvs, ssend, srecv,
@@ -1470,13 +1635,16 @@
 
         lane = lax.broadcasted_iota(jnp.int32, (step, lanes), 1)
 
-        def grads_of(entry_of, factors_of, cot_of, stage, slot):
+        def grads_of(entry_of, factors_of, begin, cot_of, stage, slot):
             for j in range(n):
 
                 def some_rows(r, carry, j=j):
                     at = pl.ds(pl.multiple_of(r * step, step), step)
-                    factors = factors_of(j, at)
-                    factors = [jnp.broadcast_to(factors[:, s : s + 1], (step, lanes)) for s in range(4)]
+                    factors = factors_of(at)
+                    factors = [
+                        jnp.broadcast_to(factors[:, begin + j * 4 + s : begin + j * 4 + s + 1], (step, lanes))
+                        for s in range(4)
+                    ]
                     totals = [jnp.zeros((step, lanes), jnp.float32) for _ in range(4)]
                     for block in range(width // lanes):
                         part = pl.ds(block * lanes, lanes)
@@ -1514,7 +1682,8 @@
             cot_of = (lambda s: source.at[s]) if other else (lambda s: source.at[s, pl.ds(0, half)])
             grads_of(
                 lambda j: top.at[other, k, j],
-                lambda j, at: tw[other, k * 3 + j, at, :],
+                lambda at: tw[other, at, :],
+                k * 12,
                 cot_of,
                 top_stage.at[other, k],
                 slot,
@@ -1532,7 +1701,8 @@
             cot_of = (lambda s: cot_x.at[k - 1, s]) if k else (lambda s: cot.at[s, pl.ds(half, half)])
             grads_of(
                 lambda j: bottom.at[k, other, j],
-                lambda j, at: bw[k, other * 3 + j, at, :],
+                lambda at: bw[k, at, :],
+                other * 12,
                 cot_of,
                 bottom_stage.at[k, other],
                 slot,
@@ -1580,15 +1750,20 @@
         fourth = remote(c_part, c_slot, sends.at[9], recvs.at[9], sibling)
         fourth.start()
         fourth.wait()
-        gains_out[...] = c_part[...] + c_slot[...]
-
-        def add_four(parts, places, dst):
+        gains_out[...] = (c_part[...] + c_slot[...])[: gains_out.shape[0]]
+
+        def add_four(parts, places, dst, column=None):
             def one(r, carry):
                 at = pl.ds(pl.multiple_of(r * step, step), step)
                 value = parts[(0,) + places + (at,)].astype(jnp.float32)
                 for src in range(1, 4):
                     value = value + parts[(src,) + places + (at,)].astype(jnp.float32)
-                dst[places + (at,)] = value.astype(dst.dtype)
+                if column is None:
+                    dst[places + (at,)] = value.astype(dst.dtype)
+                elif column < 3:
+                    dst[column, at, :] = value
+                else:
+                    dst[at, :] = value
                 return carry
 
             lax.fori_loop(0, BLOCK // step, one, 0)
@@ -1626,14 +1801,20 @@
         for copy in small_last + locals_[4:]:
             copy.wait()
         for i in range(4):
-            add_four(small_z, (i,), small_out)
+            add_four(small_z, (i,), three_out if i < 3 else last_out, i)
         for copy in up_last:
             copy.wait()
-        add_four(up_z, (), up_out)
+        add_four(up_z, (), up_out, 3)
         for copy in copies[:4]:
             copy.wait_send()
         for copy in copies[4:]:
             copy.wait()
+        for place in range(8):
+            both = jnp.concatenate([top_mix[place][:, :half], bottom_mix[place][:, :half]], axis=1)
+            for s in range(4):
+                for j in range(n):
+                    row = j * 4 + s
+                    mix_out[j, s : s + 1, place * BLOCK : (place + 1) * BLOCK] = both[row : row + 1]
 
     f32 = jnp.float32
     vmem = pltpu.VMEM
@@ -1643,17 +1824,19 @@
         kernel,
         out_shape=[
             shape((n, 8 * BLOCK, width)),
-            shape((8, 16, lanes), f32),
-            shape((8, 16, lanes), f32),
-            shape(gains.shape, f32),
-            shape((4, BLOCK, thin), f32),
+            shape((n, 4, 8 * BLOCK), f32),
+            shape((5, gains.shape[1]), f32),
+            shape((3, BLOCK, thin), f32),
+            shape((BLOCK, thin), f32),
             shape((BLOCK, hidden), f32),
         ],
-        in_specs=[ANY, ANY, VMEM, VMEM, VMEM, VMEM, ANY, ANY],
-        out_specs=[ANY, ANY, ANY, VMEM, VMEM, VMEM],
+        in_specs=[HBM, HBM, VMEM, VMEM, VMEM, VMEM, HBM, HBM],
+        out_specs=[HBM, VMEM, VMEM, VMEM, VMEM, VMEM],
         scratch_shapes=[
             vmem(top_hist.shape, BF16),
             vmem(bottom_hist.shape, BF16),
+            vmem((8, 16, lanes), f32),
+            vmem((8, 16, lanes), f32),
             vmem(top_hist.shape, BF16),
             vmem(bottom_hist.shape, BF16),
             vmem(piece, BF16),
@@ -1685,10 +1868,60 @@
             sem((18,)),
         ],
         compiler_params=pltpu.CompilerParams(
-            collective_id=6, has_side_effects=True, vmem_limit_bytes=56 * 2**20
+            collective_id=6, has_side_effects=True, vmem_limit_bytes=VMEM_LIMIT
         ),
         name="hand_out",
     )(top_hist, bottom_hist, top_weights, bottom_weights, stream_cot, gains, small, up)
+
+
+def rotary_columns(length):
+    half_rot = ROT // 2
+    frequency = 10000.0 ** (-2.0 * np.arange(half_rot, dtype=np.float32) / ROT).astype(np.float32)
+    angles = np.arange(length, dtype=np.float32)[:, None] * frequency.astype(np.float32)[None, :]
+    cosine, sine = np.cos(angles), np.sin(angles)
+    table = np.zeros((3, length, HD), np.float32)
+    table[0] = 1.0
+    table[0, :, :half_rot] = cosine
+    table[0, :, half_rot:ROT] = cosine
+    table[1, :, :half_rot] = -sine
+    table[2, :, half_rot:ROT] = sine
+    return table.reshape(3, 4, 2, BLOCK, HD)
+
+
+def place_outputs(arrays, cuts):
+    def kernel(*refs):
+        many = len(arrays)
+        srcs, dsts, held, loads, stores = refs[:many], refs[many : 2 * many], refs[2 * many : -2], refs[-2], refs[-1]
+        pieces = []
+        for src, dst, kept, cut in zip(srcs, dsts, held, cuts):
+            count = src.shape[0] // cut
+            for i in range(cut):
+                rows = pl.ds(i * count, count)
+                j = len(pieces)
+                pieces.append(
+                    (
+                        pltpu.make_async_copy(src.at[rows], kept.at[rows], loads.at[j]),
+                        pltpu.make_async_copy(kept.at[rows], dst.at[rows], stores.at[j]),
+                    )
+                )
+        for load, _ in pieces:
+            load.start()
+        for load, store in pieces:
+            load.wait()
+            store.start()
+        for _, store in pieces:
+            store.wait()
+
+    return pl.pallas_call(
+        kernel,
+        out_shape=[shape(a.shape, a.dtype) for a in arrays],
+        in_specs=[HBM] * len(arrays),
+        out_specs=[HBM] * len(arrays),
+        scratch_shapes=[pltpu.VMEM(a.shape, a.dtype) for a in arrays]
+        + [pltpu.SemaphoreType.DMA((sum(cuts),))] * 2,
+        compiler_params=pltpu.CompilerParams(vmem_limit_bytes=VMEM_LIMIT),
+        name="place_outputs",
+    )(*arrays)
 
 
 def body(
@@ -1707,72 +1940,30 @@
     out_grad,
     mix_grad_in,
 ):
-    place = lax.axis_index("hist")
-    along_x, low_z = place // 2, place % 2
     slots, seq_len, width = history.shape
     small = jnp.concatenate([jnp.transpose(w_qkv, (1, 0, 2)), w_out[None]], axis=0)
 
-    def ring(values, axis):
-        return lax.dynamic_slice_in_dim(jnp.concatenate([values, values], axis=axis), along_x, 4, axis)
-
-    def own_first(values, axis):
-        return jnp.where(low_z == 0, values, jnp.flip(values, axis=axis))
-
-    def picked(ids):
-        return (ids.reshape(-1, 1) == jnp.arange(layers, dtype=jnp.int32)[None, :]).astype(jnp.float32)
-
-    layers = mix_weights.shape[1]
-    ids = layer_ids.reshape(4, 2, slots)
-    tokens = mix_weights.reshape(4, layers, 4, 2, 2, BLOCK // 2)
-    top_ids = ring(lax.dynamic_index_in_dim(ids, low_z, 1, False), 0)
-    bottom_ids = own_first(lax.dynamic_index_in_dim(ids, along_x, 0, False), 0)
-    top_tokens = own_first(lax.dynamic_index_in_dim(tokens[:, :, :, :, 0], along_x, 2, False), 2)
-    bottom_tokens = ring(lax.dynamic_index_in_dim(tokens[:, :, :, :, 1], low_z, 3, False), 2)
-    top_weights = jnp.einsum("rl,slot->orts", picked(top_ids), top_tokens, precision=HIGHEST)
-    bottom_weights = jnp.einsum("rl,slkt->krts", picked(bottom_ids), bottom_tokens, precision=HIGHEST)
-    owned, top_hist, bottom_hist, full_small, full_up = collect(
-        history, small, w_up[None], top_weights, bottom_weights
+    owned, top_hist, bottom_hist, full_small, full_up, top_weights, bottom_weights = collect(
+        history, small, w_up[None], layer_ids, mix_weights
     )
-    rows_here = 4 * BLOCK
-    cosine, sine_table = rotary_tables(seq_len, ROT)
-
-    def here(table, side=low_z):
-        return lax.dynamic_index_in_dim(table.reshape(4, 2, BLOCK, -1), side, 1, False).reshape(rows_here, -1)
-
-    nothing = jnp.zeros_like(sine_table)
-    rest = jnp.zeros((seq_len, HD - ROT), jnp.float32)
-    tables = jnp.stack(
-        [
-            here(jnp.concatenate(parts, axis=1))
-            for parts in (
-                (cosine, cosine, rest + 1.0),
-                (-sine_table, nothing, rest),
-                (nothing, sine_table, rest),
-            )
-        ]
+    tables = jnp.asarray(rotary_columns(seq_len))
+    docs = doc_ids.reshape(8, BLOCK)
+    *attention, heads_flat, log_totals, gathered, full_down = project(
+        owned, gains, full_small, tables, w_down[None], docs
     )
-    queries, keys, values, other_keys, other_values, gathered, full_down = project(
-        owned, gains, full_small, tables, w_down[None]
-    )
-    places = jnp.stack([jnp.arange(seq_len, dtype=jnp.int32), doc_ids], axis=1)
-    query_at, other_at = here(places), here(places, 1 - low_z)
-    key_at = jnp.concatenate([query_at.T, other_at.T], axis=0)
-    attention = (queries, keys, values, other_keys, other_values, query_at, key_at)
-    heads_flat, log_totals = attend(*attention)
-
-    mixers = da_out.shape[0]
-    spare = BLOCK - mixers
     (
         block_out,
         mix_next,
         residual_grad,
         heads_cot,
         late_gains,
-        side,
         _,
         out_proj_grad,
         up_sum,
         down_sum,
+        da_in_sum,
+        da_out_sum,
+        bias_sum,
     ) = middle(
         heads_flat,
         full_small,
@@ -1780,19 +1971,17 @@
         full_down,
         owned,
         gains,
-        jnp.pad(da_in, ((0, 0), (0, spare))),
-        jnp.pad(da_out, ((0, spare), (0, spare))),
-        jnp.pad(da_bias, (0, spare))[None],
+        da_in.T,
+        da_out,
+        da_bias[None],
         out_grad,
-        jnp.pad(mix_grad_in, ((0, 0), (0, spare))),
+        mix_grad_in.T,
     )
-    side = side.reshape(16 * SIDE_ROWS, BLOCK)[:, :mixers]
-    da_in_sum, da_out_sum, bias_sum = side[:width], side[width : width + mixers], side[width + 104]
-
-    *grads, key_give, value_give = attend_back(*attention, log_totals, heads_cot)
     stream_cot, gains_local, small_sum, down_sum = inward(
-        grads,
-        (key_give, value_give),
+        attention,
+        log_totals,
+        heads_cot,
+        docs,
         full_small,
         gathered,
         out_proj_grad,
@@ -1803,7 +1992,7 @@
         tables,
         down_sum.reshape(2, 4, BLOCK, -1),
     )
-    history_grad, top_mix, bottom_mix, gains_sum, small_sum, up_sum = hand_out(
+    history_grad, mix_grad, gains_sum, qkv_sum, out_sum, up_sum = hand_out(
         top_hist,
         bottom_hist,
         top_weights,
@@ -1813,22 +2002,39 @@
         small_sum,
         up_sum.reshape(8, BLOCK, -1),
     )
-    half = BLOCK // 2
-    mix_out = jnp.concatenate([top_mix[:, : 4 * slots, :half], bottom_mix[:, : 4 * slots, :half]], axis=2)
-    mix_grad = jnp.transpose(mix_out.reshape(8, slots, 4, BLOCK), (2, 1, 0, 3)).reshape(4, slots, seq_len)
+    big = history_grad.reshape(-1, width)
+    big, block_out, mix_next, mix_grad, gains_sum, qkv_sum, out_sum, up_sum, down_sum, in_sum, net_sum, bias_sum = (
+        place_outputs(
+            (
+                big,
+                block_out,
+                mix_next,
+                mix_grad,
+                gains_sum,
+                qkv_sum,
+                out_sum,
+                up_sum,
+                down_sum,
+                da_in_sum,
+                da_out_sum,
+                bias_sum,
+            ),
+            (12,) + (1,) * 11,
+        )
+    )
     return (
         block_out,
-        mix_next[:, :mixers],
-        history_grad,
-        mix_grad,
-        gains_sum[: gains.shape[0]],
-        jnp.transpose(small_sum[:3], (1, 0, 2)),
-        small_sum[3],
+        mix_next.T,
+        big.reshape(history_grad.shape),
+        jnp.transpose(mix_grad, (1, 0, 2)),
+        gains_sum,
+        jnp.transpose(qkv_sum, (1, 0, 2)),
+        out_sum,
         up_sum,
         down_sum,
-        da_in_sum,
-        da_out_sum,
-        bias_sum,
+        in_sum.T,
+        net_sum,
+        bias_sum[0],
     )
 
 

time: 630 us -> 573 us (0.910)
  local copies, waits for them, and re-layouts: 51.6 us -> 0 us
    unnamed x60 -> x0, local copies, waits for them, and re-layouts: 35.3 us -> none
    pallas_call x1, Pallas kernels: 124 us -> 115 us  [collect(): pl.pallas_call(kernel, out_shape=[shape((4, BLOCK, width), jnp.float32),...]
    pallas_call x1, Pallas kernels: 64.7 us -> 73.3 us  [inward(): pl.pallas_call(kernel, out_shape=[shape((4, BLOCK, width)), shape((8, wid...]
    pallas_call x5 -> x4, Pallas kernels: 377 us -> 373 us  [the longest x1 162 us: middle(): pl.pallas_call(kernel, out_shape=[shape((BLOCK, width)), shape((mixers, B...]
where the time goes in v4:
time: 573 us; the launch traced here: 564 us
  Pallas kernels  561 us (98%)
    pallas_call x1, Pallas kernels, middle(): pl.pallas_call(kernel, out_shape=[shape((BLOCK, width)), shape((mixers, B...  162 us
    pallas_call x1, Pallas kernels, hand_out(): pl.pallas_call(kernel, out_shape=[shape((n, 8 * BLOCK, width)), shape((n,...  131 us
    pallas_call x1, Pallas kernels, collect(): pl.pallas_call(kernel, out_shape=[shape((4, BLOCK, width), jnp.float32),...  115 us
    pallas_call x1, Pallas kernels, inward(): pl.pallas_call(kernel, out_shape=[shape((4, BLOCK, width)), shape((8, wid...  73.3 us
    pallas_call x1, Pallas kernels, project(): pl.pallas_call(kernel, out_shape=[shape((rows_all, cols))] * 6 + [shape((...  67.6 us
    pallas_call x1, Pallas kernels, place_outputs(): pl.pallas_call(kernel, out_shape=[shape(a.shape, a.dtype) for a in arrays...  11.9 us

profile of v4, /device:TPU:1, one launch (start us, length us, event | category | flops | bytes accessed | tf_op | source)
XLA Modules:
  0.0 564.3 jit_solution(11178755303701281102)
XLA Ops:
  0.6 1.7 pad_maximum_fusion.wa
  2.3 115.1 %collect.1 = (f32[4,128,2048]{2,1,0:T(8,128)}, bf16[2,4,3,64,2048]{4,3,2,1,0:T(8,128)(2,1)}, bf16[4,2,3,64,2048]{4,3,2,1,0:T(8,128)(2,1)}, bf16[4,2048,512]{2,1,...) custom-call(bf16[3,1024,2048]{2,1,0:T(8,128)(2,1)} %hist.1, ...), custom_call_target="tpu_custom_call" | custom-call | tf_op jit(solution)/shard_map/collect/pallas_call | solution.py:418
  117.4 67.6 %project.1 = (bf16[512,512]{1,0:T(8,128)(2,1)}, bf16[512,512]{1,0:T(8,128)(2,1)}, bf16[512,512]{1,0:T(8,128)(2,1)}, bf16[512,512]{1,0:T(8,128)(2,1)}, bf16[512,5...) custom-call(f32[4,128,2048]{2,1,0:T(8,128)} %get-tuple-element.65.st, ...), custom_call_target="tpu_custom_call" | custom-call | tf_op jit(solution)/shard_map/project/pallas_call | solution.py:1218
  185.0 162.5 %middle.1 = (bf16[128,2048]{1,0:T(8,128)(2,1)}, f32[100,128]{1,0:T(8,128)}, f32[128,2048]{1,0:T(8,128)}, bf16[512,512]{1,0:T(8,128)(2,1)}, f32[2,2048]{1,0:T(2,1...) custom-call(bf16[512,512]{1,0:T(8,128)(2,1)} %get-tuple-element.73.h, ...), custom_call_target="tpu_custom_call" | custom-call | tf_op jit(solution)/shard_map/middle/pallas_call | solution.py:1025
  347.5 73.3 %inward.1 = (bf16[4,128,2048]{2,1,0:T(8,128)(2,1)}, f32[8,2048]{1,0:T(8,128)}, bf16[8,4,128,512]{3,2,1,0:T(8,128)(2,1)}, f32[128,1024]{1,0:T(8,128)}) custom-call(bf16[512,512]{1,0:T(8,128)(2,1)} %get-tuple-element.67.q_in, bf16[512,512]{1,0:T(8,128)(2,1)} %get-tuple-element.68.k_in, bf16[512,512]{1,0:T(8,128)(2,1)} %get-tuple-element.69.v_in, ...), custom_call_target="tpu_custom_call" | custom-call | tf_op jit(solution)/shard_map/inward/pallas_call | solution.py:1513
  420.8 131.1 %hand_out.1 = (bf16[3,1024,2048]{2,1,0:T(8,128)(2,1)}, f32[3,4,1024]{2,1,0:T(4,128)}, f32[5,2048]{1,0:T(8,128)}, f32[3,128,256]{2,1,0:T(8,128)}, f32[128,256]{1,0:T(8,128)}, /*index=5*/f32[128,1024]{1,0:T(8,128)}) custom-call(bf16[2,4,3,64,2048]{4,3,2,1,0:T(8,128)(2,1)} %get-tuple-element.61.top_hist, ...), custom_call_target="tpu_custom_call" | custom-call | tf_op jit(solution)/shard_map/hand_out/pallas_call | solution.py:1823
  551.9 11.9 %place_outputs.1 = (bf16[3072,2048]{1,0:T(8,128)(2,1)}, bf16[128,2048]{1,0:T(8,128)(2,1)}, f32[100,128]{1,0:T(8,128)}, f32[3,4,1024]{2,1,0:T(4,128)}, f32[5,2048...) custom-call(bf16[3072,2048]{1,0:T(8,128)(2,1)} %bitcast.17, ...), custom_call_target="tpu_custom_call" | custom-call | tf_op jit(solution)/shard_map/place_outputs/pallas_call | solution.py:1915

commit v5 on v4

--- a/solution.py
+++ b/solution.py
@@ -232,7 +232,7 @@
     return greeted, start, relay_z, relay_y, finish
 
 
-def collect(history, small, up, layer_ids, mix_weights):
+def collect(history, three, last, up, layer_ids, mix_weights):
     slots, _, width = history.shape
     layers = mix_weights.shape[1]
     half = BLOCK // 2
@@ -240,7 +240,7 @@
     lanes = 128
 
     def kernel(
-        hist, wa, wb, ids, given, streams, top_out, bottom_out, full_a, full_b, tw, bw,
+        hist, wa, wb, wc, ids, given, streams, top_out, bottom_out, full_a, full_b, full_c, tw, bw,
         top, bottom, acc, far_part, hop, part_x, got_x, part_z, got_z,
         wsend, wrecv, send, recv, local, store,
     ):
@@ -248,7 +248,9 @@
         x, zl, zh, y, c = here
         partner = device(x, 1 - zl, zh, y, c)
         peers = {k: device((x + k) % 4, zl, zh, y, c) for k in (1, 2, 3)}
-        greeted, start, relay_z, relay_y, finish = weight_gather((wa, wb), (full_a, full_b), here, wsend, wrecv, 0)
+        greeted, start, relay_z, relay_y, finish = weight_gather(
+            (wa, wb, wc), (full_a, full_b, full_c), here, wsend, wrecv, 0
+        )
         greet(greeted + [peers[1], peers[2], peers[3]])
 
         def rows(k, other, low):
@@ -409,8 +411,9 @@
         for copy in copies:
             copy.wait_send()
 
-    n_a, rows_a, cols_a = small.shape
-    n_b, rows_b, cols_b = up.shape
+    def whole(block):
+        return shape((block.shape[0], block.shape[1] * 16, block.shape[2] * 2))
+
     vmem = pltpu.VMEM
     sem = pltpu.SemaphoreType.DMA
     top_shape, bottom_shape = (2, 4, slots, half, width), (4, 2, slots, half, width)
@@ -421,13 +424,14 @@
             shape((4, BLOCK, width), jnp.float32),
             shape(top_shape),
             shape(bottom_shape),
-            shape((n_a, rows_a * 16, cols_a * 2)),
-            shape((n_b, rows_b * 16, cols_b * 2)),
+            whole(three),
+            whole(last),
+            whole(up),
             shape((2, half, lanes), jnp.float32),
             shape((4, half, lanes), jnp.float32),
         ],
-        in_specs=[ANY, ANY, ANY, pl.BlockSpec(memory_space=pltpu.SMEM), VMEM],
-        out_specs=[VMEM, HBM, HBM, HBM, HBM, VMEM, VMEM],
+        in_specs=[ANY, ANY, ANY, ANY, pl.BlockSpec(memory_space=pltpu.SMEM), VMEM],
+        out_specs=[VMEM, HBM, HBM, HBM, HBM, HBM, VMEM, VMEM],
         scratch_shapes=[
             vmem(top_shape, BF16),
             vmem(bottom_shape, BF16),
@@ -438,18 +442,18 @@
             vmem((2,) + piece, BF16),
             vmem(piece, BF16),
             vmem(piece, BF16),
-            sem((64,)),
-            sem((64,)),
+            sem((96,)),
+            sem((96,)),
             sem((16,)),
             sem((16,)),
-            sem((8,)),
+            sem((9,)),
             sem((6,)),
         ],
         compiler_params=pltpu.CompilerParams(
             collective_id=1, has_side_effects=True, vmem_limit_bytes=VMEM_LIMIT
         ),
         name="collect",
-    )(history, small, up, layer_ids, mix_weights)
+    )(history, three, last, up, layer_ids, mix_weights)
 
 
 def dot_nt(left, right):
@@ -491,74 +495,60 @@
     return (keys[2 * side] <= query_pos) & (keys[2 * side + 1] == query_doc)
 
 
-def attend(q, k, v, ok, ov, places, keys, out, lse):
-    rows, cols = q.shape
+def attend(q, k, v, ok, ov, places, keys, out, lse, at):
+    cols = q.shape[1]
     scale = HD ** (-0.5)
-    tall = 256
 
     def one_head(h, carry):
         head = pl.ds(pl.multiple_of(h * HD, HD), HD)
-        for r in range(rows // tall):
-            at = pl.ds(r * tall, tall)
-            query_pos, query_doc = places[at, 0:1], places[at, 1:2]
-            scores = []
-            for side, key in enumerate((k, ok)):
-                allowed = allowed_keys(query_pos, query_doc, keys, side)
-                scores.append(jnp.where(allowed, dot_nt(q[at, head], key[:, head]) * scale, NEGATIVE))
-            top = jnp.maximum(
-                jnp.max(scores[0], axis=1, keepdims=True), jnp.max(scores[1], axis=1, keepdims=True)
-            )
-            shifted = [jnp.exp(part - top) for part in scores]
-            total = jnp.sum(shifted[0], axis=1, keepdims=True) + jnp.sum(shifted[1], axis=1, keepdims=True)
-            share = 1.0 / total
-            result = dot_nn((shifted[0] * share).astype(BF16), v[:, head])
-            result = result + dot_nn((shifted[1] * share).astype(BF16), ov[:, head])
-            out[at, head] = result.astype(BF16)
-            lane = lax.broadcasted_iota(jnp.int32, (tall, HD), 1)
-            lse[at, :] = jnp.where(lane == h, top + jnp.log(total), lse[at, :])
+        query_pos, query_doc = places[at, 0:1], places[at, 1:2]
+        scores = []
+        for side, key in enumerate((k, ok)):
+            allowed = allowed_keys(query_pos, query_doc, keys, side)
+            scores.append(jnp.where(allowed, dot_nt(q[at, head], key[:, head]) * scale, NEGATIVE))
+        top = jnp.maximum(jnp.max(scores[0], axis=1, keepdims=True), jnp.max(scores[1], axis=1, keepdims=True))
+        shifted = [jnp.exp(part - top) for part in scores]
+        total = jnp.sum(shifted[0], axis=1, keepdims=True) + jnp.sum(shifted[1], axis=1, keepdims=True)
+        share = 1.0 / total
+        result = dot_nn((shifted[0] * share).astype(BF16), v[:, head])
+        result = result + dot_nn((shifted[1] * share).astype(BF16), ov[:, head])
+        out[at, head] = result.astype(BF16)
+        lane = lax.broadcasted_iota(jnp.int32, (BLOCK, HD), 1)
+        lse[at, :] = jnp.where(lane == h, top + jnp.log(total), lse[at, :])
         return carry
 
     lax.fori_loop(0, cols // HD, one_head, 0)
 
 
-def attend_back(q, k, v, ok, ov, places, keys, lse, cot, dq, dk, dv, dok, dov, key_sum, value_sum, finish):
-    rows, cols = q.shape
+def attend_back(q, k, v, ok, ov, places, keys, lse, cot, dq, dk, dv, dok, dov, at, begin):
+    cols = q.shape[1]
     scale = HD ** (-0.5)
-    tall = 256
+
+    def add(into, head, value):
+        if begin:
+            into[:, head] = value
+        else:
+            into[:, head] = into[:, head] + value
 
     def one_head(h, carry):
         head = pl.ds(pl.multiple_of(h * HD, HD), HD)
-        for r in range(rows // tall):
-            at = pl.ds(r * tall, tall)
-            query_pos, query_doc = places[at, 0:1], places[at, 1:2]
-            lane = lax.broadcasted_iota(jnp.int32, (tall, HD), 1)
-            log_total = jnp.sum(jnp.where(lane == h, lse[at, :], 0.0), axis=1, keepdims=True)
-            probs, prob_grads = [], []
-            for side, (key, value) in enumerate(((k, v), (ok, ov))):
-                allowed = allowed_keys(query_pos, query_doc, keys, side)
-                scores = jnp.where(allowed, dot_nt(q[at, head], key[:, head]) * scale, NEGATIVE)
-                probs.append(jnp.exp(scores - log_total))
-                prob_grads.append(dot_nt(cot[at, head], value[:, head]))
-            row_dot = sum(jnp.sum(p * g, axis=1, keepdims=True) for p, g in zip(probs, prob_grads))
-            query_grad = jnp.zeros((tall, HD), jnp.float32)
-            for side, (p, g) in enumerate(zip(probs, prob_grads)):
-                score_cot = (p * (g - row_dot)).astype(BF16)
-                key = (k, ok)[side]
-                query_grad = query_grad + dot_nn(score_cot, key[:, head])
-                key_part = dot_tn(score_cot, q[at, head])
-                value_part = dot_tn(p.astype(BF16), cot[at, head])
-                if r == 0:
-                    key_sum[side] = key_part
-                    value_sum[side] = value_part
-                else:
-                    key_sum[side] += key_part
-                    value_sum[side] += value_part
-            dq[at, head] = query_grad * scale
-        dk[:, head] = key_sum[0] * scale
-        dv[:, head] = value_sum[0]
-        dok[:, head] = (key_sum[1] * scale).astype(BF16)
-        dov[:, head] = value_sum[1].astype(BF16)
-        finish(h)
+        query_pos, query_doc = places[at, 0:1], places[at, 1:2]
+        lane = lax.broadcasted_iota(jnp.int32, (BLOCK, HD), 1)
+        log_total = jnp.sum(jnp.where(lane == h, lse[at, :], 0.0), axis=1, keepdims=True)
+        probs, prob_grads = [], []
+        for side, (key, value) in enumerate(((k, v), (ok, ov))):
+            allowed = allowed_keys(query_pos, query_doc, keys, side)
+            scores = jnp.where(allowed, dot_nt(q[at, head], key[:, head]) * scale, NEGATIVE)
+            probs.append(jnp.exp(scores - log_total))
+            prob_grads.append(dot_nt(cot[at, head], value[:, head]))
+        row_dot = sum(jnp.sum(p * g, axis=1, keepdims=True) for p, g in zip(probs, prob_grads))
+        query_grad = jnp.zeros((BLOCK, HD), jnp.float32)
+        for key, key_grad, value_grad, p, g in zip((k, ok), (dk, dok), (dv, dov), probs, prob_grads):
+            score_cot = (p * (g - row_dot)).astype(BF16)
+            query_grad = query_grad + dot_nn(score_cot, key[:, head])
+            add(key_grad, head, dot_tn(score_cot, q[at, head]) * scale)
+            add(value_grad, head, dot_tn(p.astype(BF16), cot[at, head]))
+        dq[at, head] = query_grad * scale
         return carry
 
     lax.fori_loop(0, cols // HD, one_head, 0)
@@ -600,8 +590,8 @@
     return jnp.mean(value, axis=1, keepdims=True)
 
 
-def middle(heads, small, up, down, stream, gains, da_in, da_out, da_bias, out_grad, mix_cot_in):
-    rows_all, head_cols = heads.shape
+def middle(attention, docs, last, up, down, stream, gains, da_in, da_out, da_bias, out_grad, mix_cot_in):
+    rows_all, head_cols = attention[0].shape
     width, hidden = up.shape[1:]
     step = 16
     half = BLOCK // 2
@@ -610,13 +600,15 @@
     mixers = da_out.shape[0]
 
     def kernel(
-        heads, small, up, down, stream_in, gains, in_given, net_given, bias_given, out_grad, mix_given,
-        block_out, mix_next, residual_grad, heads_cot, gain_grads, other, out_proj_grad, up_sum, down_sum,
-        in_grad, net_grad, bias_grad,
+        q_in, k_in, v_in, ok_in, ov_in, docs, last, up, down, stream_in, gains, in_given, net_given, bias_given,
+        out_grad, mix_given,
+        block_out, mix_next, residual_grad, gain_grads, other, up_sum, down_sum, in_grad, net_grad, bias_grad,
+        dq_out, dk_out, dv_out, dok_out, dov_out, heads_out, attn_cot_out,
+        heads, heads_cot, lse, places_in, key_rows, other_values_grad,
         w_out, w_up, w_down, mid_all, active, slope, cot_all, up_cot, attn_cot,
         part, got1, got3, own, residual, unit, total, flat, aux, inv, grad_stage, sums,
         y_slots, z_part, z_slots, c_part, c_slot, x_slots, result, side_sum,
-        stream, da_in, padded, load, send, recv, gsend, grecv, gkeep, sends, recvs, dload,
+        stream, da_in, padded, aload, astore, load, send, recv, gsend, grecv, gkeep, sends, recvs, dload,
     ):
         x, zl, zh, y, c = coords()
         z = zh * 2 + zl
@@ -627,34 +619,46 @@
         peers = {k: device(places[k], zl, zh, y, c) for k in steps}
         right, left, far = places[1], places[3], places[2]
         loads = [
-            pltpu.make_async_copy(small.at[3], w_out, load.at[0]),
+            pltpu.make_async_copy(last.at[0], w_out, load.at[0]),
             pltpu.make_async_copy(up.at[0], w_up, load.at[1]),
             pltpu.make_async_copy(down.at[0], w_down, load.at[2]),
             pltpu.make_async_copy(stream_in.at[3], stream, load.at[3]),
         ]
-        for copy in loads:
+
+        def cols_of(ref, i):
+            return ref.at[:, pl.ds(i * head_cols, head_cols)]
+
+        attention_refs = [cols_of(cot_all, i) for i in range(4)] + [cols_of(active, 0)]
+
+        def load_attention(first):
+            return [
+                pltpu.make_async_copy(src, dst, aload.at[first + i])
+                for i, (src, dst) in enumerate(zip((q_in, k_in, v_in, ok_in, ov_in), attention_refs))
+            ]
+
+        early = load_attention(0)
+        for copy in early + loads:
             copy.start()
         greet([peers[k] for k in steps] + [peer for _, peer in along_z + along_y] + [sibling])
 
         def block(place):
             return pl.ds(pl.multiple_of(place * BLOCK, BLOCK), BLOCK)
 
-        def chunks(work, place=0):
+        def chunks(work, place=0, begin=0, count=BLOCK // step):
             def one(r, carry):
-                begin = r * step
                 work(
-                    pl.ds(pl.multiple_of(begin, step), step),
-                    pl.ds(pl.multiple_of(place * BLOCK + begin, step), step),
+                    pl.ds(pl.multiple_of(r * step, step), step),
+                    pl.ds(pl.multiple_of(place * BLOCK + r * step, step), step),
                 )
                 return carry
 
-            lax.fori_loop(0, BLOCK // step, one, 0)
+            lax.fori_loop(begin, begin + count, one, 0)
 
         sent = []
         given = ({}, {}, {})
 
         def arrived(stage, got):
-            for k in steps:
+            for k in steps if stage else (1, 3):
                 i = stage * 3 + k - 1
                 remote(got.at[k - 1], got.at[k - 1], send.at[i], recv.at[i], sibling).wait_recv()
 
@@ -670,21 +674,23 @@
                 return
             slot = stage % 2
             if stage == 2:
-                given[0][k].wait_send()
+                for copy in hops if k == 2 else (given[0][k],):
+                    copy.wait_send()
             part[slot, k - 1] = product.astype(BF16)
             given[stage][k] = push(part.at[slot, k - 1], got.at[k - 1], stage * 3 + k - 1, peers[k])
 
-        def spread(buf, base):
+        def spread(buf, base, fill):
             def piece(place, top):
                 begin = pl.multiple_of(place * BLOCK + (0 if top else half), half)
                 return buf.at[pl.ds(begin, half)]
 
-            first = [
-                push(piece(x, True), piece(x, True), base, peers[1]),
-                push(piece(x, False), piece(x, False), base + 2, peers[3]),
-                push(piece(x, False), piece(x, False), base + 1, peers[1]),
-                push(piece(x, True), piece(x, True), base + 3, peers[3]),
-            ]
+            first = [None] * 4
+            chunks(fill, x, 0, half // step)
+            first[0] = push(piece(x, True), piece(x, True), base, peers[1])
+            first[3] = push(piece(x, True), piece(x, True), base + 3, peers[3])
+            chunks(fill, x, half // step, half // step)
+            first[1] = push(piece(x, False), piece(x, False), base + 2, peers[3])
+            first[2] = push(piece(x, False), piece(x, False), base + 1, peers[1])
 
             def forward():
                 first[0].wait_recv()
@@ -695,8 +701,8 @@
 
             return first, forward
 
-        def gathered(buf, base, work):
-            first, forward = spread(buf, base)
+        def gathered(buf, base, fill, work):
+            first, forward = spread(buf, base, fill)
             work(0, x)
             one, two = forward()
             first[2].wait_recv()
@@ -708,9 +714,38 @@
             work(2, far)
 
         loads[0].wait()
-        for k in (2, 1, 3, 0):
-            place = x if k == 0 else places[k]
-            give_part(0, k, got1, dot_nt(heads[block(place), :], w_out[...]))
+        for i, row in enumerate(set_places(docs, zl, places_in)):
+            key_rows[i : i + 1, :] = row
+        key_places = [key_rows.at[pl.ds(i, 1)] for i in range(4)]
+        lse[...] = jnp.zeros_like(lse)
+        for copy in early:
+            copy.wait()
+
+        def attend_rows(place):
+            keys = [row[...] for row in key_places]
+            attend(*attention_refs, places_in, keys, heads, lse, block(place))
+
+        attend_rows(far)
+        part[0, 1] = dot_nt(heads[block(far), :], w_out[...]).astype(BF16)
+        tops, bottoms = pl.ds(0, half), pl.ds(half, half)
+        hops = (
+            push(part.at[0, 1, tops], got1.at[1, tops], 1, peers[1]),
+            push(part.at[0, 1, bottoms], got1.at[1, bottoms], 27, peers[3]),
+        )
+        attend_rows(right)
+        total[...] = dot_nt(heads[block(right), :], w_out[...])
+        attend_rows(left)
+        aux[...] = dot_nt(heads[block(left), :], w_out[...])
+        attend_rows(x)
+        own[...] = dot_nt(heads[block(x), :], w_out[...])
+        heads_kept = pltpu.make_async_copy(heads, heads_out, astore.at[0])
+        heads_kept.start()
+        hops[0].wait_recv()
+        total[tops, :] = total[tops, :] + got1[1, tops, :].astype(jnp.float32)
+        give_part(0, 1, got1, total[...])
+        hops[1].wait_recv()
+        aux[bottoms, :] = aux[bottoms, :] + got1[1, bottoms, :].astype(jnp.float32)
+        give_part(0, 3, got1, aux[...])
         aux[...] = jnp.zeros_like(aux)
         aux[:mixers, :] = in_given[...].astype(jnp.float32)
         da_in[...] = aux[...].astype(BF16)
@@ -724,7 +759,7 @@
 
         def to_mid(at, there):
             value = stream[at, :] + own[at, :]
-            for k in range(3):
+            for k in (0, 2):
                 value = value + got1[k, at, :].astype(jnp.float32)
             residual[at, :] = value
             centered = value - row_mean(value)
@@ -734,7 +769,6 @@
             unit[at, :] = normed
             mid_all[there, :] = (normed * gains[3:4, :]).astype(BF16)
 
-        chunks(to_mid, x)
 
         waited = []
 
@@ -754,7 +788,7 @@
                 waited.append(True)
             give_part(1, k, got3, dot_nt(active[block(place), :], w_down[...]))
 
-        gathered(mid_all, 9, feed)
+        gathered(mid_all, 9, to_mid, feed)
 
         def bend_more(r, carry):
             at = pl.ds(pl.multiple_of(r * step, step), step)
@@ -797,7 +831,6 @@
             residual[at, :] = value
             cot_all[there, :] = value.astype(BF16)
 
-        chunks(to_cot, x)
 
         def small_grads():
             aux[...] = dot_tn(inner_cot, flat[...])
@@ -860,7 +893,7 @@
             chunks(bend, place)
             give_part(2, k, got1, dot_nt(up_cot[block(place), :], w_up[...]))
 
-        first, forward = spread(cot_all, 15)
+        first, forward = spread(cot_all, 15, to_cot)
         side_start()
         feed_back(0, x)
         one, two = forward()
@@ -943,6 +976,13 @@
 
         weight_grad(1, cot_all, active)
         side_x()
+        ended = [*first, one, two]
+        for copy in ended:
+            copy.wait_send()
+        late = load_attention(5)
+        for copy in late:
+            copy.start()
+        weight_grad(0, mid_all, up_cot)
         arrived(2, got1)
 
         def to_residual(at, there):
@@ -960,20 +1000,26 @@
             residual_grad[at, :] = value
             attn_cot[there, :] = value.astype(BF16)
 
-        chunks(to_residual, x)
-        first, forward = spread(attn_cot, 21)
-
-        def head_back(place):
+        first, forward = spread(attn_cot, 21, to_residual)
+
+        grads = [cols_of(slope, i) for i in range(4)] + [other_values_grad]
+
+        def head_back(place, begin=False):
             heads_cot[block(place), :] = dot_nn(attn_cot[block(place), :], w_out[...]).astype(BF16)
+            keys = [row[...] for row in key_places]
+            attend_back(
+                *attention_refs, places_in, keys, lse, heads_cot, *grads, block(place), begin
+            )
 
         side_up_z()
-        head_back(x)
+        for copy in late:
+            copy.wait()
+        head_back(x, True)
         one, two = forward()
         fetch_other(1)
-        weight_grad(0, mid_all, up_cot)
+        fetch_other(0)
         side_up_y()
         down_done = add_cores(1)
-        fetch_other(0)
         gain_grads[...] = jnp.sum(sums[...], axis=1)
         first[2].wait_recv()
         head_back(left)
@@ -982,27 +1028,21 @@
         one.wait_recv()
         two.wait_recv()
         head_back(far)
-
-        def out_grad_copy(m):
-            rows = pl.ds(pl.multiple_of(m * tile, tile), tile)
-            slot = lax.rem(m, 2)
-            return pltpu.make_async_copy(
-                grad_stage.at[slot, :, pl.ds(0, head_cols)], out_proj_grad.at[rows], gkeep.at[slot]
+        cols_of(active, 1)[...] = grads[3][...].astype(BF16)
+        cols_of(active, 2)[...] = grads[4][...].astype(BF16)
+        stored = [heads_kept]
+        for i, (src, dst) in enumerate(
+            (
+                (cols_of(active, 1), dok_out),
+                (cols_of(active, 2), dov_out),
+                (grads[0], dq_out),
+                (grads[1], dk_out),
+                (grads[2], dv_out),
+                (attn_cot, attn_cot_out),
             )
-
-        def out_grad_tile(m, carry):
-            @pl.when(m >= 2)
-            def _():
-                out_grad_copy(m - 2).wait()
-
-            cols = pl.ds(pl.multiple_of(m * tile, tile), tile)
-            grad_stage[lax.rem(m, 2), :, :head_cols] = dot_tn(attn_cot[:, cols], heads[...]).astype(BF16)
-            out_grad_copy(m).start()
-            return carry
-
-        lax.fori_loop(0, tiles, out_grad_tile, 0)
-        out_grad_copy(tiles - 2).wait()
-        out_grad_copy(tiles - 1).wait()
+        ):
+            stored.append(pltpu.make_async_copy(src, dst, astore.at[1 + i]))
+            stored[-1].start()
         for copy in side[5]:
             copy.wait()
         for i in range(16):
@@ -1015,8 +1055,10 @@
         up_done = add_cores(0)
         down_done.wait()
         up_done.wait()
+        for copy in stored:
+            copy.wait()
         for i, copy in enumerate(sent):
-            if all(copy is not first for first in given[0].values()):
+            if all(copy is not other_copy for other_copy in (*given[0].values(), *hops, *ended)):
                 copy.wait_send()
 
     f32 = jnp.float32
@@ -1028,19 +1070,26 @@
             shape((BLOCK, width)),
             shape((mixers, BLOCK), f32),
             shape((BLOCK, width), f32),
-            shape(heads.shape),
             shape((2, width), f32),
             shape((2, tiles, BLOCK, hidden)),
-            shape((width, head_cols)),
             shape((tiles * BLOCK, hidden)),
             shape((tiles * BLOCK, hidden)),
             shape((mixers, width), f32),
             shape((mixers, mixers), f32),
             shape((1, mixers), f32),
-        ],
-        in_specs=[VMEM, HBM, HBM, HBM, HBM] + [VMEM] * 6,
-        out_specs=[VMEM] * 5 + [HBM] * 4 + [VMEM] * 3,
+        ]
+        + [shape((rows_all, head_cols), f32)] * 3
+        + [shape((rows_all, head_cols))] * 3
+        + [shape((rows_all, width))],
+        in_specs=[HBM] * 5 + [VMEM] + [HBM] * 4 + [VMEM] * 6,
+        out_specs=[VMEM] * 4 + [HBM] * 3 + [VMEM] * 3 + [HBM] * 7,
         scratch_shapes=[
+            vmem((rows_all, head_cols), BF16),
+            vmem((rows_all, head_cols), BF16),
+            vmem((rows_all, HD), f32),
+            vmem((rows_all, HD), f32),
+            vmem((8, rows_all), f32),
+            vmem((rows_all, head_cols), f32),
             vmem((width, head_cols), BF16),
             vmem((width, hidden), BF16),
             vmem((width, hidden), BF16),
@@ -1073,9 +1122,11 @@
             vmem((BLOCK, width), f32),
             vmem((BLOCK, width), BF16),
             vmem((3, BLOCK, BLOCK), f32),
+            pltpu.SemaphoreType.DMA((10,)),
+            pltpu.SemaphoreType.DMA((7,)),
             pltpu.SemaphoreType.DMA((4,)),
-            pltpu.SemaphoreType.DMA((27,)),
-            pltpu.SemaphoreType.DMA((27,)),
+            pltpu.SemaphoreType.DMA((28,)),
+            pltpu.SemaphoreType.DMA((28,)),
             pltpu.SemaphoreType.DMA((2 * tiles,)),
             pltpu.SemaphoreType.DMA((2 * tiles,)),
             pltpu.SemaphoreType.DMA((4,)),
@@ -1087,10 +1138,10 @@
             collective_id=4, has_side_effects=True, vmem_limit_bytes=VMEM_LIMIT
         ),
         name="middle",
-    )(heads, small, up, down, stream, gains, da_in, da_out, da_bias, out_grad, mix_cot_in)
-
-
-def project(streams, gains, small, tables, down, docs):
+    )(*attention, docs, last, up, down, stream, gains, da_in, da_out, da_bias, out_grad, mix_cot_in)
+
+
+def project(streams, gains, small, tables, down):
     width = streams.shape[2]
     cols = small.shape[2]
     rows_all = 4 * BLOCK
@@ -1099,9 +1150,9 @@
     order = (1, 2, 0)
 
     def kernel(
-        streams_in, gains, small, tables_in, down, docs,
-        queries_out, keys_out, values_out, other_keys_out, other_values_out, heads, lse_out, normed_out, full_down,
-        queries, keys, values, other_keys, other_values, lse, streams, tables, places_in, weights, normed, load, send, recv, zsend, zrecv, local, wsend, wrecv,
+        streams_in, gains, small, tables_in, down,
+        queries_out, keys_out, values_out, other_keys_out, other_values_out, normed_out, full_down,
+        queries, keys, values, other_keys, other_values, streams, tables, weights, normed, load, send, recv, zsend, zrecv, local, wsend, wrecv,
     ):
         x, zl, zh, y, c = coords()
         partner = device(x, 1 - zl, zh, y, c)
@@ -1177,8 +1228,6 @@
             loads[i].wait()
             work(i, x)
         relay_z()
-        key_places = set_places(docs, zl, places_in)
-        lse[...] = jnp.zeros_like(lse)
         for i in order:
             copies[i, 0].wait_recv()
             push(i, 4, left, True, peers[1])
@@ -1204,9 +1253,6 @@
         for i, (src, dst) in enumerate(zip(kept_here, outs)):
             stores.append(pltpu.make_async_copy(src, dst, local.at[4 + i]))
             stores[-1].start()
-        attend(queries, keys, values, other_keys, other_values, places_in, key_places, heads, lse)
-        stores.append(pltpu.make_async_copy(lse, lse_out, local.at[9]))
-        stores[-1].start()
         finish()
         for copy in stores + kept:
             copy.wait()
@@ -1217,20 +1263,17 @@
     sem = pltpu.SemaphoreType.DMA
     return pl.pallas_call(
         kernel,
-        out_shape=[shape((rows_all, cols))] * 6
+        out_shape=[shape((rows_all, cols))] * 5
         + [
-            shape((rows_all, HD), jnp.float32),
             shape((3, rows_all, width)),
             shape((1, down.shape[1] * 16, down.shape[2] * 2)),
         ],
-        in_specs=[HBM, VMEM, HBM, HBM, ANY, VMEM],
-        out_specs=[HBM] * 5 + [VMEM] + [HBM] * 3,
+        in_specs=[HBM, VMEM, HBM, HBM, ANY],
+        out_specs=[HBM] * 7,
         scratch_shapes=[vmem((rows_all, cols), BF16)] * 5
         + [
-            vmem((rows_all, HD), jnp.float32),
             vmem((3, BLOCK, width), jnp.float32),
             vmem((3, 4, BLOCK, HD), jnp.float32),
-            vmem((rows_all, HD), jnp.float32),
             vmem((3, width, cols), BF16),
             vmem((3, rows_all, width), BF16),
             sem((7,)),
@@ -1238,7 +1281,7 @@
             sem((18,)),
             sem((8,)),
             sem((8,)),
-            sem((10,)),
+            sem((9,)),
             sem((32,)),
             sem((32,)),
         ],
@@ -1246,11 +1289,11 @@
             collective_id=2, has_side_effects=True, vmem_limit_bytes=VMEM_LIMIT
         ),
         name="project",
-    )(streams, gains, small, tables, down, docs)
-
-
-def inward(attention, lse, heads_cot, docs, small, normed, out_proj_grad, streams, residual_grad, gains, late_gains, tables, down):
-    rows_all, cols = heads_cot.shape
+    )(streams, gains, small, tables, down)
+
+
+def inward(grads, gives, heads, attn_cot, small, normed, streams, residual_grad, gains, late_gains, tables, down):
+    rows_all, cols = heads.shape
     width = streams.shape[2]
     step = 16
     half = BLOCK // 2
@@ -1260,12 +1303,11 @@
     thin = hidden // 2
 
     def kernel(
-        q_in, k_in, v_in, ok_in, ov_in, lse_in, cot, docs, small, normed, out_proj_grad, streams, residual_grad,
-        gains, late,
+        dq_in, dk_in, dv_in, give_k, give_v, heads_in, cot_in, small, normed, streams, residual_grad, gains, late,
         tables_in, down,
         stream_cot, gain_grads, small_sum, down_out,
         weights, inputs, cots, got_k, got_v, far_part, near, hop, got, own, grad, swapped, sums, down_y, down_part, down_z, stream,
-        tables, places_in, dq, dk, dv, give_k, give_v, key_sum, value_sum, q, k, v, ok, ov, lse,
+        tables, dq, dk, dv, heads, attn_cot,
         ksend, krecv, load, send, recv, ssend, srecv, gsend, grecv, local,
     ):
         x, zl, zh, y, c = coords()
@@ -1279,16 +1321,15 @@
         early = [
             pltpu.make_async_copy(src, dst, load.at[9 + i])
             for i, (src, dst) in enumerate(
-                ((q_in, q), (k_in, k), (v_in, v), (ok_in, ok), (ov_in, ov), (lse_in, lse))
+                ((dq_in, dq), (dk_in, dk), (dv_in, dv), (heads_in, heads), (cot_in, attn_cot))
             )
         ]
         for copy in early:
             copy.start()
         loads = [pltpu.make_async_copy(small.at[i], weights.at[i], load.at[i]) for i in range(3)]
         loads += [pltpu.make_async_copy(normed.at[i], inputs.at[i], load.at[3 + i]) for i in range(3)]
-        loads.append(pltpu.make_async_copy(out_proj_grad, grad.at[0], load.at[6]))
+        loads.append(pltpu.make_async_copy(tables_in.at[:, :, zl], tables, load.at[8]))
         loads.append(pltpu.make_async_copy(streams.at[pl.ds(0, 3)], stream, load.at[7]))
-        loads.append(pltpu.make_async_copy(tables_in.at[:, :, zl], tables, load.at[8]))
         for copy in loads:
             copy.start()
         greet([peers[1], peers[3], sibling] + [peer for _, peer in along_z + along_y])
@@ -1299,6 +1340,11 @@
             sides.append(remote(src, dst, ssend.at[i], srecv.at[i], peer))
             sides[-1].start()
 
+        swaps_z = [
+            remote(src, dst, ksend.at[i], krecv.at[i], partner)
+            for i, (src, dst) in enumerate(((give_k, got_k), (give_v, got_v)))
+        ]
+        swaps_z[0].start()
         for py, peer in along_y:
             side(down.at[:, py], down_y.at[y], peer)
         locals_ = [pltpu.make_async_copy(down.at[:, y], down_y.at[y], local.at[0])]
@@ -1367,15 +1413,18 @@
             slot = (1, 0, 1, 0)[i]
             if i < 3:
                 loads[3 + i].wait()
-
-                def one(m, carry):
-                    at = pl.ds(pl.multiple_of(m * tile, tile), tile)
-                    grad[slot, at, :] = dot_tn(inputs[i, :, at], cots[i]).astype(BF16)
-                    return carry
-
-                lax.fori_loop(0, tiles, one, 0)
+                left_side, right_side = inputs.at[i], cots.at[i]
             else:
-                loads[6].wait()
+                early[3].wait()
+                early[4].wait()
+                left_side, right_side = attn_cot, heads
+
+            def one(m, carry):
+                at = pl.ds(pl.multiple_of(m * tile, tile), tile)
+                grad[slot, at, :] = dot_tn(left_side[:, at], right_side[...]).astype(BF16)
+                return carry
+
+            lax.fori_loop(0, tiles, one, 0)
             for m in range(tiles):
                 begin = pl.multiple_of(m * tile + (1 - c) * BLOCK, BLOCK)
                 j = i * tiles + m
@@ -1407,36 +1456,21 @@
             weight_grad(i)
             swaps_of[i] = swaps[begin:]
 
-        key_places = set_places(docs, zl, places_in)
-        for copy in early:
+        for copy in early[:3]:
             copy.wait()
-
-        def swap(which, h):
-            head = pl.ds(pl.multiple_of(h * HD, HD), HD)
-            src, dst = (give_k, give_v)[which], (got_k, got_v)[which]
-            j = h * 2 + which
-            return remote(src.at[:, head], dst.at[:, head], ksend.at[j], krecv.at[j], partner)
-
-        def give_head(h):
-            swap(0, h).start()
-            swap(1, h).start()
-
-        attend_back(
-            q, k, v, ok, ov, places_in, key_places, lse, cot, dq, dk, dv, give_k, give_v, key_sum, value_sum, give_head
-        )
-        loads[8].wait()
+        loads[6].wait()
         to_cots(0, turned(lambda at, head: dq[at, head]))
         far_sums(0)
         near_sums(0)
+        swaps_z[0].wait_send()
+        swaps_z[1].start()
         grads_of(3)
         grads_of(0)
         own_sums(0)
-        for h in range(cols // HD):
-            swap(0, h).wait()
+        swaps_z[0].wait_recv()
         to_cots(1, turned(lambda at, head: dk[at, head] + got_k[at, head].astype(jnp.float32)))
         far_sums(1)
-        for h in range(cols // HD):
-            swap(1, h).wait()
+        swaps_z[1].wait()
         to_cots(2, lambda at, head, place, there: dv[at, head] + got_v[at, head].astype(jnp.float32))
         far_sums(2)
         near_sums(1)
@@ -1518,7 +1552,7 @@
             shape((tiles, 4, BLOCK, cols)),
             shape((BLOCK, thin), f32),
         ],
-        in_specs=[HBM] * 6 + [VMEM] * 2 + [HBM] * 4 + [VMEM] * 3 + [HBM] * 2,
+        in_specs=[HBM] * 10 + [VMEM] * 3 + [HBM] * 2,
         out_specs=[VMEM, VMEM, HBM, VMEM],
         scratch_shapes=[
             vmem((3, width, cols), BF16),
@@ -1539,20 +1573,13 @@
             vmem((4, BLOCK, thin), BF16),
             vmem((3, BLOCK, width), f32),
             vmem((3, 4, BLOCK, HD), f32),
-            vmem((rows_all, HD), f32),
             vmem((rows_all, cols), f32),
             vmem((rows_all, cols), f32),
             vmem((rows_all, cols), f32),
             vmem((rows_all, cols), BF16),
-            vmem((rows_all, cols), BF16),
-            vmem((2, rows_all, HD), f32),
-            vmem((2, rows_all, HD), f32),
-        ]
-        + [vmem((rows_all, cols), BF16)] * 5
-        + [
-            vmem((rows_all, HD), f32),
-            sem((8,)),
-            sem((8,)),
+            vmem((rows_all, width), BF16),
+            sem((2,)),
+            sem((2,)),
             sem((15,)),
             sem((12,)),
             sem((12,)),
@@ -1567,8 +1594,7 @@
         ),
         name="inward",
     )(
-        *attention, lse, heads_cot, docs, small, normed, out_proj_grad, streams, residual_grad, gains, late_gains,
-        tables, down
+        *grads, *gives, heads, attn_cot, small, normed, streams, residual_grad, gains, late_gains, tables, down
     )
 
 
@@ -1941,32 +1967,35 @@
     mix_grad_in,
 ):
     slots, seq_len, width = history.shape
-    small = jnp.concatenate([jnp.transpose(w_qkv, (1, 0, 2)), w_out[None]], axis=0)
-
-    owned, top_hist, bottom_hist, full_small, full_up, top_weights, bottom_weights = collect(
-        history, small, w_up[None], layer_ids, mix_weights
+
+    owned, top_hist, bottom_hist, full_three, full_last, full_up, top_weights, bottom_weights = collect(
+        history, jnp.transpose(w_qkv, (1, 0, 2)), w_out[None], w_up[None], layer_ids, mix_weights
     )
     tables = jnp.asarray(rotary_columns(seq_len))
     docs = doc_ids.reshape(8, BLOCK)
-    *attention, heads_flat, log_totals, gathered, full_down = project(
-        owned, gains, full_small, tables, w_down[None], docs
-    )
+    *attention, gathered, full_down = project(owned, gains, full_three, tables, w_down[None])
     (
         block_out,
         mix_next,
         residual_grad,
-        heads_cot,
         late_gains,
         _,
-        out_proj_grad,
         up_sum,
         down_sum,
         da_in_sum,
         da_out_sum,
         bias_sum,
+        query_grad,
+        key_grad,
+        value_grad,
+        key_give,
+        value_give,
+        heads,
+        attn_cot,
     ) = middle(
-        heads_flat,
-        full_small,
+        attention,
+        docs,
+        full_last,
         full_up,
         full_down,
         owned,
@@ -1978,13 +2007,12 @@
         mix_grad_in.T,
     )
     stream_cot, gains_local, small_sum, down_sum = inward(
-        attention,
-        log_totals,
-        heads_cot,
-        docs,
-        full_small,
+        (query_grad, key_grad, value_grad),
+        (key_give, value_give),
+        heads,
+        attn_cot,
+        full_three,
         gathered,
-        out_proj_grad,
         owned,
         residual_grad,
         gains,
@@ -2019,7 +2047,7 @@
                 da_out_sum,
                 bias_sum,
             ),
-            (12,) + (1,) * 11,
+            (24,) + (1,) * 11,
         )
     )
     return (

time: 573 us -> 571 us (level)
  no operation moved by 1% of the time
where the time goes in v5:
time: 571 us; the launch traced here: 561 us
  Pallas kernels  560 us (98%)
    pallas_call x1, Pallas kernels, middle(): pl.pallas_call(kernel, out_shape=[shape((BLOCK, width)), shape((mixers, B...  162 us
    pallas_call x1, Pallas kernels, hand_out(): pl.pallas_call(kernel, out_shape=[shape((n, 8 * BLOCK, width)), shape((n,...  129 us
    pallas_call x1, Pallas kernels, collect(): pl.pallas_call(kernel, out_shape=[shape((4, BLOCK, width), jnp.float32),...  116 us
    pallas_call x1, Pallas kernels, inward(): pl.pallas_call(kernel, out_shape=[shape((4, BLOCK, width)), shape((8, wid...  76.3 us
    pallas_call x1, Pallas kernels, project(): pl.pallas_call(kernel, out_shape=[shape((rows_all, cols))] * 5 + [shape((...  65.3 us
    pallas_call x1, Pallas kernels, place_outputs(): pl.pallas_call(kernel, out_shape=[shape(a.shape, a.dtype) for a in arrays...  11.7 us

profile of v5, /device:TPU:1, one launch (start us, length us, event | category | flops | bytes accessed | tf_op | source)
XLA Modules:
  0.0 561.1 jit_solution(11726122577883386513)
XLA Ops:
  0.6 116.0 %collect.1 = (f32[4,128,2048]{2,1,0:T(8,128)}, bf16[2,4,3,64,2048]{4,3,2,1,0:T(8,128)(2,1)}, bf16[4,2,3,64,2048]{4,3,2,1,0:T(8,128)(2,1)}, bf16[3,2048,512]{2,1,...) custom-call(bf16[3,1024,2048]{2,1,0:T(8,128)(2,1)} %hist.1, ...), custom_call_target="tpu_custom_call" | custom-call | tf_op jit(solution)/shard_map/collect/pallas_call | solution.py:421
  116.6 65.3 %project.1 = (bf16[512,512]{1,0:T(8,128)(2,1)}, bf16[512,512]{1,0:T(8,128)(2,1)}, bf16[512,512]{1,0:T(8,128)(2,1)}, bf16[512,512]{1,0:T(8,128)(2,1)}, bf16[512,5...) custom-call(f32[4,128,2048]{2,1,0:T(8,128)} %get-tuple-element.69.streams_in.stream_in.streams, ...), custom_call_target="tpu_custom_call" | custom-call | tf_op jit(solution)/shard_map/project/pallas_call | solution.py:1264
  182.0 161.7 %middle.1 = (bf16[128,2048]{1,0:T(8,128)(2,1)}, f32[100,128]{1,0:T(8,128)}, f32[128,2048]{1,0:T(8,128)}, f32[2,2048]{1,0:T(2,128)}, bf16[2,8,128,2048]{3,2,1,0:T...) custom-call(bf16[512,512]{1,0:T(8,128)(2,1)} %get-tuple-element.71.q, ...), custom_call_target="tpu_custom_call" | custom-call | tf_op jit(solution)/shard_map/middle/pallas_call | solution.py:1067
  343.7 76.3 %inward.1 = (bf16[4,128,2048]{2,1,0:T(8,128)(2,1)}, f32[8,2048]{1,0:T(8,128)}, bf16[8,4,128,512]{3,2,1,0:T(8,128)(2,1)}, f32[128,1024]{1,0:T(8,128)}) custom-call(f32[512,512]{1,0:T(8,128)} %get-tuple-element.79.dq_in, f32[512,512]{1,0:T(8,128)} %get-tuple-element.80.dk_in, f32[512,512]{1,0:T(8,128)} %get-tuple-element.81.dv_in, ...), custom_call_target="tpu_custom_call" | custom-call | tf_op jit(solution)/shard_map/inward/pallas_call | solution.py:1547
  420.0 129.0 %hand_out.1 = (bf16[3,1024,2048]{2,1,0:T(8,128)(2,1)}, f32[3,4,1024]{2,1,0:T(4,128)}, f32[5,2048]{1,0:T(8,128)}, f32[3,128,256]{2,1,0:T(8,128)}, f32[128,256]{1,0:T(8,128)}, /*index=5*/f32[128,1024]{1,0:T(8,128)}) custom-call(bf16[2,4,3,64,2048]{4,3,2,1,0:T(8,128)(2,1)} %get-tuple-element.65.top_hist, ...), custom_call_target="tpu_custom_call" | custom-call | tf_op jit(solution)/shard_map/hand_out/pallas_call | solution.py:1849
  548.9 11.7 %place_outputs.1 = (bf16[3072,2048]{1,0:T(8,128)(2,1)}, bf16[128,2048]{1,0:T(8,128)(2,1)}, f32[100,128]{1,0:T(8,128)}, f32[3,4,1024]{2,1,0:T(4,128)}, f32[5,2048...) custom-call(bf16[3072,2048]{1,0:T(8,128)(2,1)} %bitcast.17, ...), custom_call_target="tpu_custom_call" | custom-call | tf_op jit(solution)/shard_map/place_outputs/pallas_call | solution.py:1941
